TPU v7x, 128 devices: a whole 4x4x4 slice. The times are simulated.
128 devices in a mesh: slab: 4 (over x_hi, core), sub: 32 (over y, x_lo, z).
Axes of the slice: x: 4 (x_hi: 2, x_lo: 2; x = x_hi * 2 + x_lo), y: 4, z: 4, core: 2. Of those that a mesh axis runs over, the one named last changes fastest.
Arguments:
- positions: float32 [3, 131072], P(None, ('slab', 'sub')), may hold values from 0 to 10
- fraction: float32 [3, 131072], P(None, ('slab', 'sub')), may hold values from 0 to 1
- grid_base: int32 [3, 131072], P(None, ('slab', 'sub')), may hold values from 0 to 255, as said below
- polarizability: float32 [131072], P(('slab', 'sub')), may hold values from 0.1 to 0.5
- perm_field: float32 [3, 131072], P(None, ('slab', 'sub')), may hold values from -6 to 6
- influence: float32 [256, 256, 256], P('slab', 'sub'), may hold values from 0.5 to 1094
- neighbour_cells: int32 [2048, 16], P(('slab', 'sub')), may hold values from 0 to 47, as said below
- neighbour_count: int32 [2048], P(('slab', 'sub')), may hold values from 1 to 16, as said below
- send_cells: int32 [128, 4, 8], P(('slab', 'sub')), may hold values from 0 to 15, as said below
Outputs:
- dipoles: float32 [3, 131072], P(None, ('slab', 'sub'))
Inputs may be any that keep to these rules, and one draw needn't show every extreme that they name: `grid_base`: rows 0, 1, 2 are the first grid point along x, y, z: along x counted within the device's 256/4 points, along y within its 256/32 points, along z over all 256 points. `neighbour_cells`: entry 0 of a cell's row is the cell's own index among its device's 16 cells; the entries of a row are distinct and index the device's extended table of 48 cells. Only the first neighbour_count entries of a cell's row are live; some cell has all 16 live. send_cells[d, q] lists 8 distinct cells of device d: q = 0 go to the next device along sub, q = 1 to the previous along sub, q = 2 to the next along slab, q = 3 to the previous along slab, cyclically.
All inputs are finite; a program needn't handle non-finite values.
Results may differ from a plain program's by a relative error of at most 0.0003.
Values sent between devices are 32-bit elements; how exact they have to be, the bound alone decides.
A program may use at most 128 MiB of HBM per device.

v0:
```python
import math

import jax
import jax.numpy as jnp
from jax import lax
from jax.sharding import PartitionSpec as P

G = 256
ITERS = 2


damping = 1.0
recip_scale = 16.0
highest = lax.Precision.HIGHEST


def shifted(value, axis, steps):
    count = lax.axis_size(axis)
    pairs = [(source, (source + steps) % count) for source in range(count)]
    return lax.ppermute(value, axis, pairs)


def in_blocks(x, dim, length):
    dims = x.shape
    pieces = x.reshape(*dims[:dim], length, dims[dim] // length, *dims[dim + 1 :])
    return jnp.moveaxis(pieces, dim, 0)


def laid_out(pieces, dim):
    pieces = jnp.moveaxis(pieces, 0, dim)
    dims = pieces.shape
    return pieces.reshape(*dims[:dim], dims[dim] * dims[dim + 1], *dims[dim + 2 :])


def one_exchange(x, axis, axes, splits, concats):
    sizes = [lax.axis_size(a) for a in axes]
    pieces = in_blocks(x, splits[0], sizes[0])
    pieces = jnp.moveaxis(in_blocks(pieces, splits[1] + 1, sizes[1]), 0, 1)
    inside = pieces.shape[2:]
    pieces = pieces.reshape(-1, *inside)
    pieces = lax.all_to_all(pieces, axis, split_axis=0, concat_axis=0, tiled=True)
    pieces = laid_out(pieces.reshape(*sizes, *inside), concats[0] + 1)
    return laid_out(pieces, concats[1])


def spline_weights(fraction):
    square = fraction * fraction
    cube = square * fraction
    rest = 1.0 - fraction
    return jnp.stack(
        [
            rest * rest * rest / 6.0,
            (3.0 * cube - 6.0 * square + 4.0) / 6.0,
            (-3.0 * cube + 3.0 * square + 3.0 * fraction + 1.0) / 6.0,
            cube / 6.0,
        ]
    )


def signed_index(position):
    return jnp.where(position < G // 2, position, position - G).astype(jnp.float32)


def pair_field(pos_near, pos_far, mom_far, live_pairs):
    delta_x = pos_near[0][..., :, None] - pos_far[0][..., None, :]
    delta_y = pos_near[1][..., :, None] - pos_far[1][..., None, :]
    delta_z = pos_near[2][..., :, None] - pos_far[2][..., None, :]
    softened = delta_x * delta_x + delta_y * delta_y + delta_z * delta_z + damping
    inverse = 1.0 / jnp.sqrt(softened)
    inverse_cube = inverse * inverse * inverse
    inverse_fifth = inverse_cube * inverse * inverse
    projection = (
        delta_x * mom_far[0][..., None, :]
        + delta_y * mom_far[1][..., None, :]
        + delta_z * mom_far[2][..., None, :]
    )
    radial = jnp.where(live_pairs, 3.0 * projection * inverse_fifth, 0.0)
    plain = jnp.where(live_pairs, inverse_cube, 0.0)
    return jnp.stack(
        [
            jnp.sum(radial * delta_x - plain * mom_far[0][..., None, :], axis=-1),
            jnp.sum(radial * delta_y - plain * mom_far[1][..., None, :], axis=-1),
            jnp.sum(radial * delta_z - plain * mom_far[2][..., None, :], axis=-1),
        ]
    )


def axis_table(start, weights, length, wrapped):
    offset = jnp.arange(length, dtype=jnp.int32)[:, None] - start[None, :]
    if wrapped:
        offset = offset % length
    table = jnp.zeros((length, start.shape[0]), jnp.float32)
    for stencil in range(4):
        table = table + jnp.where(offset == stencil, weights[stencil][None, :], 0.0)
    return table


def ghost_cells(blocks, send_cells):
    picked = [jnp.take(blocks, send_cells[0, direction], axis=1) for direction in range(4)]
    sub_lower = shifted(picked[0], "sub", 1)
    sub_upper = shifted(picked[1], "sub", -1)
    slab_lower = shifted(picked[2], "slab", 1)
    slab_upper = shifted(picked[3], "slab", -1)
    return jnp.concatenate([blocks, sub_lower, sub_upper, slab_lower, slab_upper], axis=1)


def apply_kernel(spectra, moduli, index_y, index_z):
    index_x = jnp.arange(G, dtype=jnp.int32)
    freq_x = signed_index(index_x)[:, None, None]
    freq_y = signed_index(index_y)[None, :, None]
    freq_z = signed_index(index_z)[None, None, :]
    freq_sq = freq_x * freq_x + freq_y * freq_y + freq_z * freq_z
    anchor = (
        (index_x[:, None, None] == 0)
        & (index_y[None, :, None] == 0)
        & (index_z[None, None, :] == 0)
    )
    width_sq = G / 4.0 * (G / 4.0)
    kernel = jnp.where(
        anchor,
        0.0,
        -recip_scale
        * moduli
        * jnp.exp(-freq_sq / (2.0 * width_sq))
        / jnp.where(anchor, 1.0, freq_sq),
    )
    kernel = kernel / (float(G) * float(G) * float(G))
    dotted = freq_x * spectra[0] + freq_y * spectra[1] + freq_z * spectra[2]
    return (freq_x * kernel * dotted, freq_y * kernel * dotted, freq_z * kernel * dotted)


def shards(
    positions,
    fraction,
    grid_base,
    polarizability,
    perm_field,
    influence,
    neighbour_cells,
    neighbour_count,
    send_cells,
):
    atom_count = positions.shape[1]
    cell_count = neighbour_cells.shape[0]
    cell_width = atom_count // cell_count
    slab_count = lax.axis_size("slab")
    sub_count = lax.axis_size("sub")
    grid_x = G // slab_count
    grid_y = G // sub_count
    wide_x = grid_x + 3
    wide_y = grid_y + 3
    block_rows = min(512, atom_count)
    block_count = atom_count // block_rows
    weights = spline_weights(fraction)
    along_x = axis_table(grid_base[0], weights[:, 0], wide_x, False)
    along_y = axis_table(grid_base[1], weights[:, 1], wide_y, False)
    along_depth = axis_table(grid_base[2], weights[:, 2], G, True)
    plane_table = (along_x[:, None, :] * along_y[None, :, :]).reshape(wide_x * wide_y, atom_count)
    frequency = jnp.arange(G, dtype=jnp.int32)
    phases = (frequency[:, None] * frequency[None, :] % G).astype(jnp.float32) * (2.0 * math.pi / G)
    cosine = jnp.cos(phases)
    sine = jnp.sin(phases)
    real_table = jnp.stack([cosine, -sine])
    forward_table = jnp.stack([jnp.stack([cosine, sine]), jnp.stack([-sine, cosine])])
    inverse_table = jnp.stack([jnp.stack([cosine, -sine]), jnp.stack([sine, cosine])])
    slab_index = lax.axis_index("slab")
    sub_index = lax.axis_index("sub")
    moved = lax.all_to_all(influence, "slab", split_axis=1, concat_axis=0, tiled=True)
    moduli = jnp.transpose(moved, (2, 0, 1))
    depth_count = G // (sub_count * slab_count)
    index_y = jnp.arange(G, dtype=jnp.int32)
    index_z = (
        sub_index * grid_y + slab_index * depth_count + jnp.arange(depth_count, dtype=jnp.int32)
    )

    def spread(moments):

        def spread_accumulate(block, running):
            start = block * block_rows
            plane_rows = lax.dynamic_slice_in_dim(plane_table, start, block_rows, 1)
            depth_rows = lax.dynamic_slice_in_dim(along_depth, start, block_rows, 1)
            moment_rows = lax.dynamic_slice_in_dim(moments, start, block_rows, 1)
            values = (moment_rows[:, None, :] * depth_rows[None, :, :]).reshape(3 * G, block_rows)
            return running + lax.dot_general(
                plane_rows, values, (((1,), (1,)), ((), ())), precision=highest
            )

        running = lax.fori_loop(
            0, block_count, spread_accumulate, jnp.zeros((wide_x * wide_y, 3 * G), jnp.float32)
        )
        widened = running.reshape(wide_x, wide_y, 3 * G)
        spilled_x = shifted(widened[grid_x:], "slab", 1)
        folded = widened[:grid_x].at[:3].add(spilled_x)
        spilled_y = shifted(folded[:, grid_y:], "sub", 1)
        return folded[:, :grid_y].at[:, :3].add(spilled_y)

    own_cells = jnp.arange(cell_count, dtype=jnp.int32)
    atom_slot = jnp.arange(cell_width, dtype=jnp.int32)
    partner_slot = jnp.arange(2 * cell_width, dtype=jnp.int32) % cell_width
    same_atom = atom_slot[:, None] == partner_slot[None, :]
    pos_cells = positions.reshape(3, cell_count, cell_width)
    moments = polarizability[None, :] * perm_field
    pos_ext = pos_cells
    for advance in range(ITERS):
        mom_cells = moments.reshape(3, cell_count, cell_width)
        if advance == 0:
            extended = ghost_cells(jnp.concatenate([pos_cells, mom_cells], axis=0), send_cells)
            pos_ext = extended[:3]
            mom_ext = extended[3:]
        else:
            mom_ext = ghost_cells(mom_cells, send_cells)

        def real_accumulate(pair_index, running):
            chosen = lax.dynamic_slice_in_dim(neighbour_cells, 2 * pair_index, 2, 1)
            flat_cells = chosen.reshape(-1)
            pos_far = jnp.take(pos_ext, flat_cells, axis=1).reshape(3, cell_count, 2 * cell_width)
            mom_far = jnp.take(mom_ext, flat_cells, axis=1).reshape(3, cell_count, 2 * cell_width)
            live_cell = (2 * pair_index + jnp.arange(2, dtype=jnp.int32))[
                None, :
            ] < neighbour_count[:, None]
            itself = chosen == own_cells[:, None]
            live_far = jnp.repeat(live_cell, cell_width, axis=1)
            self_far = jnp.repeat(itself, cell_width, axis=1)
            live_pairs = live_far[:, None, :] & jnp.logical_not(
                self_far[:, None, :] & same_atom[None]
            )
            return running + pair_field(pos_cells, pos_far, mom_far, live_pairs)

        real_part = lax.fori_loop(
            0,
            neighbour_cells.shape[1] // 2,
            real_accumulate,
            jnp.zeros((3, cell_count, cell_width), jnp.float32),
        ).reshape(3, atom_count)
        density = spread(moments).reshape(grid_x, grid_y, 3, G)
        z_spectra = tuple(
            (
                jnp.einsum(
                    "rkn,xyn->yrxk", real_table, density[:, :, component, :], precision=highest
                )
                for component in range(3)
            )
        )
        gathered = jax.tree.map(
            lambda part: one_exchange(part, ("sub", "slab"), ("sub", "slab"), (3, 3), (0, 2)),
            z_spectra,
        )
        spectra = tuple(
            (
                jnp.einsum(
                    "oikn,niyz->okyz",
                    forward_table,
                    jnp.einsum("oikn,nixz->xokz", forward_table, spectrum, precision=highest),
                    precision=highest,
                )
                for spectrum in gathered
            )
        )
        field_spec = apply_kernel(spectra, moduli, index_y, index_z)
        back_x = tuple(
            (
                jnp.einsum("oikn,inyz->yokz", inverse_table, spectrum, precision=highest)
                for spectrum in field_spec
            )
        )
        back_y = tuple(
            (
                jnp.einsum("oikn,nixz->zoxk", inverse_table, spectrum, precision=highest)
                for spectrum in back_x
            )
        )
        returned = jax.tree.map(
            lambda part: one_exchange(part, ("slab", "sub"), ("slab", "sub"), (2, 3), (0, 0)),
            back_y,
        )
        spatial = jnp.stack(
            [
                jnp.einsum("rkn,krxy->xyn", real_table, spectrum, precision=highest)
                for spectrum in returned
            ],
            axis=2,
        )
        field_grid = spatial.reshape(grid_x, grid_y, 3 * G)
        rim_y = shifted(field_grid[:, :3], "sub", -1)
        wider = jnp.concatenate([field_grid, rim_y], axis=1)
        rim_x = shifted(wider[:3], "slab", -1)
        interpolate_widened = jnp.concatenate([wider, rim_x], axis=0).reshape(
            wide_x * wide_y, 3 * G
        )

        def sample(block, sampled):
            start = block * block_rows
            plane_rows = lax.dynamic_slice_in_dim(plane_table, start, block_rows, 1)
            depth_rows = lax.dynamic_slice_in_dim(along_depth, start, block_rows, 1)
            mixed = lax.dot_general(
                interpolate_widened, plane_rows, (((0,), (0,)), ((), ())), precision=highest
            )
            values = jnp.sum(mixed.reshape(3, G, block_rows) * depth_rows[None, :, :], axis=1)
            return lax.dynamic_update_slice_in_dim(sampled, values, start, 1)

        moments = polarizability[None, :] * (
            perm_field
            + real_part
            + lax.fori_loop(0, block_count, sample, jnp.zeros((3, atom_count), jnp.float32))
        )
    return moments


def solution(mesh):
    in_specs = (
        P(None, ("slab", "sub")),
        P(None, ("slab", "sub")),
        P(None, ("slab", "sub")),
        P(("slab", "sub")),
        P(None, ("slab", "sub")),
        P("slab", "sub", None),
        P(("slab", "sub"), None),
        P(("slab", "sub")),
        P(("slab", "sub"), None, None),
    )
    out_specs = P(None, ("slab", "sub"))
    return jax.shard_map(shards, mesh=mesh, in_specs=in_specs, out_specs=out_specs, check_vma=False)
```

profile of v0, /device:TPU:1, one launch (start us, length us, event | category | flops | bytes accessed | tf_op | source)
XLA Modules:
  0.0 1002.8 jit_solution(8312500967528878539)
XLA Ops:
  9.4 18.6 %while.89 = (s32[]{:T(128)}, f32[737,768]{1,0:T(8,128)}, f32[737,1024]{1,0:T(8,128)S(1)}, f32[3,1024]{1,0:T(4,128)S(1)}, f32[256,1024]{1,0:T(8,128)}, /*index=5*/s32[]{:T(128)}, s32[]{:T(128)}, s32[]{:T(128)}, s32[]{:T(128)}) while((s32[]{:T(128)}, f32[737,768]{1,0:T(8,128)}, f32[737,1024]{1,0:T(8,128)S(1)}, ...), condition=%wide.region_6.9_spmd.clone, body=%wide.region_5.8_spmd.clone.sunk | while | flops 3479127552 | bytes 10789025 | solution.py:188
  11.9 6.6 select_add_fusion.7
  21.0 7.0 select_add_fusion.7
  61.3 14.8 %collective-permute-done.5 = f32[64,3,768]{2,0,1:T(8,128)S(1)} collective-permute-done((f32[64,3,768]{2,0,1:T(8,128)S(1)}, f32[64,3,768]{2,0,1:T(8,128)S(1)}, u32[]{:S(2)}, u32[]{:S(2)}) %collective-permute-start.5) | collective-permute-done | bytes 589856 | tf_op jit(solution)/shard_map/ppermute | solution.py:20
  77.4 8.3 scatter-add.15
  89.4 5.5 fusion.154
  113.0 6.5 all-to-all-start.3
  138.6 10.7 %all-to-all-start.2 = ((f32[128,1,2048]{2,1,0:T(1,128)}), f32[128,1,2048]{2,1,0:T(1,128)}, u32[]{:S(2)}, u32[]{:S(2)}) async-start(f32[128,1,2048]{2,1,0:T(1,128)} %reshape.1260), calls=%async_computation.2 | async-start | bytes 2097152 | tf_op jit(solution)/shard_map/all_to_all | solution.py:41
  169.4 10.9 %all-to-all-start.1 = ((f32[128,1,2048]{2,1,0:T(1,128)}), f32[128,1,2048]{2,1,0:T(1,128)}, u32[]{:S(2)}, u32[]{:S(2)}) async-start(f32[128,1,2048]{2,1,0:T(1,128)} %reshape.1258), calls=%async_computation.1 | async-start | bytes 2097152 | tf_op jit(solution)/shard_map/all_to_all | solution.py:41
  190.3 5.3 reduce.58
  205.1 5.3 reduce.57
  227.4 5.3 reduce.56
  271.6 10.2 %all-to-all-start.4 = ((f32[128,1,2048]{2,1,0:T(1,128)}), f32[128,1,2048]{2,1,0:T(1,128)}, u32[]{:S(2)}, u32[]{:S(2)}) async-start(f32[128,1,2048]{2,1,0:T(1,128)} %reshape.1268), calls=%async_computation.4 | async-start | bytes 2097152 | tf_op jit(solution)/shard_map/all_to_all | solution.py:41
  286.1 5.1 convolution_bitcast_fusion.13
  305.6 10.2 %all-to-all-start.5 = ((f32[128,1,2048]{2,1,0:T(1,128)}), f32[128,1,2048]{2,1,0:T(1,128)}, u32[]{:S(2)}, u32[]{:S(2)}) async-start(f32[128,1,2048]{2,1,0:T(1,128)} %reshape.1266), calls=%async_computation.5 | async-start | bytes 2097152 | tf_op jit(solution)/shard_map/all_to_all | solution.py:41
  316.5 6.5 collective-permute-start.1
  328.5 5.1 convolution_bitcast_fusion.12
  356.3 5.3 reduce.61
  372.1 5.3 reduce.60
  392.4 5.3 reduce.59
  417.9 8.3 collective-permute-done.6
  431.9 70.2 %while.88 = (s32[]{:T(128)}, f32[3,16,64]{2,1,0:T(8,128)S(1)}, s32[16]{0:T(128)}, s32[16,16]{1,0:T(8,128)}, f32[3,16,64]{2,1,0:T(8,128)S(1)}, /*index=5*/f32[3,4...) while((s32[]{:T(128)}, f32[3,16,64]{2,1,0:T(8,128)S(1)}, ...), condition=%wide.region_4.7_spmd.clone, body=%wide.region_0.6_spmd.clone.sunk | while | flops 4880745 | bytes 567493 | solution.py:229
  509.5 25.5 %while.86 = (s32[]{:T(128)}, f32[3,1024]{1,0:T(4,128)S(1)}, f32[737,1024]{1,0:T(8,128)S(1)}, f32[737,768]{1,0:T(8,128)}, f32[256,1024]{1,0:T(8,128)}, /*index=5*/s32[]{:T(128)}, s32[]{:T(128)}, s32[]{:T(128)}, s32[]{:T(128)}) while((s32[]{:T(128)}, f32[3,1024]{1,0:T(4,128)S(1)}, f32[737,1024]{1,0:T(8,128)S(1)}, f32[737,768]{1,0:T(8,128)}, ...), condition=%wide.region_9.12_spmd, body=%wide.region_7.11_spmd.sunk | while | flops 3478387200 | bytes 11674775 | solution.py:304
  509.5 6.9 fusion.209
  522.2 6.9 fusion.209
  535.0 18.7 %while.91 = (s32[]{:T(128)}, f32[737,768]{1,0:T(8,128)}, f32[737,1024]{1,0:T(8,128)S(1)}, f32[3,1024]{1,0:T(4,128)S(1)}, f32[256,1024]{1,0:T(8,128)}, /*index=5*/s32[]{:T(128)}, s32[]{:T(128)}, s32[]{:T(128)}, s32[]{:T(128)}) while((s32[]{:T(128)}, f32[737,768]{1,0:T(8,128)}, f32[737,1024]{1,0:T(8,128)S(1)}, ...), condition=%wide.region_16.20_spmd.clone, body=%wide.region_15.19_spmd.clone.sunk | while | flops 3479127552 | bytes 10789025 | solution.py:188
  537.5 6.7 select_add_fusion.8
  546.7 7.1 select_add_fusion.8
  571.4 15.7 %collective-permute-done.13 = f32[64,3,768]{2,0,1:T(8,128)S(1)} collective-permute-done((f32[64,3,768]{2,0,1:T(8,128)S(1)}, f32[64,3,768]{2,0,1:T(8,128)S(1)}, u32[]{:S(2)}, u32[]{:S(2)}) %collective-permute-start.13) | collective-permute-done | bytes 589856 | tf_op jit(solution)/shard_map/ppermute | solution.py:20
  589.8 8.5 scatter-add.19
  602.0 5.6 fusion.150
  625.6 5.7 all-to-all-start.9
  650.4 10.6 %all-to-all-start.8 = ((f32[128,1,2048]{2,1,0:T(1,128)}), f32[128,1,2048]{2,1,0:T(1,128)}, u32[]{:S(2)}, u32[]{:S(2)}) async-start(f32[128,1,2048]{2,1,0:T(1,128)} %reshape.1272), calls=%async_computation.8 | async-start | bytes 2097152 | tf_op jit(solution)/shard_map/all_to_all | solution.py:41
  680.2 10.6 %all-to-all-start.7 = ((f32[128,1,2048]{2,1,0:T(1,128)}), f32[128,1,2048]{2,1,0:T(1,128)}, u32[]{:S(2)}, u32[]{:S(2)}) async-start(f32[128,1,2048]{2,1,0:T(1,128)} %reshape.1270), calls=%async_computation.7 | async-start | bytes 2097152 | tf_op jit(solution)/shard_map/all_to_all | solution.py:41
  690.8 5.3 reduce.64
  705.6 5.3 reduce.63
  728.0 5.3 reduce.62
  772.1 10.2 %all-to-all-start.10 = ((f32[128,1,2048]{2,1,0:T(1,128)}), f32[128,1,2048]{2,1,0:T(1,128)}, u32[]{:S(2)}, u32[]{:S(2)}) async-start(f32[128,1,2048]{2,1,0:T(1,128)} %reshape.1280), calls=%async_computation.10 | async-start | bytes 2097152 | tf_op jit(solution)/shard_map/all_to_all | solution.py:41
  806.3 10.2 %all-to-all-start.11 = ((f32[128,1,2048]{2,1,0:T(1,128)}), f32[128,1,2048]{2,1,0:T(1,128)}, u32[]{:S(2)}, u32[]{:S(2)}) async-start(f32[128,1,2048]{2,1,0:T(1,128)} %reshape.1278), calls=%async_computation.11 | async-start | bytes 2097152 | tf_op jit(solution)/shard_map/all_to_all | solution.py:41
  816.6 6.5 collective-permute-start.9
  852.6 5.3 reduce.67
  868.2 5.3 reduce.66
  888.5 5.4 reduce.65
  914.0 8.4 collective-permute-done.14
  928.1 41.0 %while.90 = (s32[]{:T(128)}, f32[3,16,64]{2,1,0:T(8,128)S(1)}, s32[16]{0:T(128)}, s32[16,16]{1,0:T(8,128)}, f32[3,16,64]{2,1,0:T(8,128)S(1)}, /*index=5*/f32[3,4...) while((s32[]{:T(128)}, f32[3,16,64]{2,1,0:T(8,128)S(1)}, ...), condition=%wide.region_14.18_spmd.clone, body=%wide.region_10.17_spmd.clone.sunk | while | flops 4880745 | bytes 567493 | solution.py:229
  976.5 25.5 %while.87 = (s32[]{:T(128)}, f32[3,1024]{1,0:T(4,128)S(1)}, f32[737,1024]{1,0:T(8,128)S(1)}, f32[737,768]{1,0:T(8,128)}, f32[256,1024]{1,0:T(8,128)}, /*index=5*/s32[]{:T(128)}, s32[]{:T(128)}, s32[]{:T(128)}, s32[]{:T(128)}) while((s32[]{:T(128)}, f32[3,1024]{1,0:T(4,128)S(1)}, f32[737,1024]{1,0:T(8,128)S(1)}, f32[737,768]{1,0:T(8,128)}, ...), condition=%wide.region_19.23_spmd, body=%wide.region_17.22_spmd.sunk | while | flops 3478387200 | bytes 11674775 | solution.py:304
  976.5 7.0 fusion.212
  989.2 6.9 fusion.212
  (859 shorter events, 686.2 us)
Async XLA Ops:
  30.3 23.6 %collective-permute-start.4 = (f32[3,11,768]{2,1,0:T(8,128)}, f32[3,11,768]{2,1,0:T(8,128)}, u32[]{:S(2)}, u32[]{:S(2)}) collective-permute-start(f32[3,11,768]{2,1,0:T(8,128)} %slice.518), channel_id=1, source_target_pairs={{0,32},{32,64},{64,96},{96,0},{1,33},{33,65},{65,97},{97,1},{2,34}... | collective-permute-start | bytes 304136 | tf_op jit(solution)/shard_map/ppermute | solution.py:20
  36.4 76.6 %all-to-all-start = ((f32[64,8,256]{2,0,1:T(8,128)}), f32[64,8,256]{2,0,1:T(8,128)}, u32[]{:S(2)}, u32[]{:S(2)}) async-start(f32[64,8,256]{2,0,1:T(8,128)} %copy.278), calls=%async_computation | async-start | bytes 1048576 | tf_op jit(solution)/shard_map/all_to_all | solution.py:168
  47.1 200.6 %copy-start.51 = (f32[256]{0:T(256)}, f32[256]{0:T(256)S(1)}, u32[]{:S(2)}) copy-start(f32[256]{0:T(256)S(1)} %fusion.135) | copy-start | bytes 3076
  51.1 232.1 %copy-start.69 = (pred[8]{0:T(512)(128)(4,1)}, pred[8]{0:T(512)(128)(4,1)S(1)}, u32[]{:S(2)}) copy-start(pred[8]{0:T(512)(128)(4,1)S(1)} %get-tuple-element.1085) | copy-start | bytes 28
  51.1 264.6 %copy-start.67 = (pred[8]{0:T(512)(128)(4,1)}, pred[8]{0:T(512)(128)(4,1)S(1)}, u32[]{:S(2)}) copy-start(pred[8]{0:T(512)(128)(4,1)S(1)} %get-tuple-element.1083) | copy-start | bytes 28
  51.2 272.4 %copy-start.65 = (pred[8]{0:T(512)(128)(4,1)}, pred[8]{0:T(512)(128)(4,1)S(1)}, u32[]{:S(2)}) copy-start(pred[8]{0:T(512)(128)(4,1)S(1)} %get-tuple-element.1087) | copy-start | bytes 28
  51.2 301.5 %copy-start.63 = (pred[8]{0:T(512)(128)(4,1)}, pred[8]{0:T(512)(128)(4,1)S(1)}, u32[]{:S(2)}) copy-start(pred[8]{0:T(512)(128)(4,1)S(1)} %get-tuple-element.990) | copy-start | bytes 28
  57.2 18.9 %collective-permute-start.5 = (f32[64,3,768]{2,0,1:T(8,128)S(1)}, f32[64,3,768]{2,0,1:T(8,128)S(1)}, u32[]{:S(2)}, u32[]{:S(2)}) collective-permute-start(f32[64,3,768]{2,0,1:T(8,128)S(1)} %copy.281), channel_id=1, source_target_pairs={{0,1},{1,2},{2,3},{3,4},{4,5},{5,6},{6,7},{7,8},{8,9},{9,10},{10,1... | collective-permute-start | bytes 1769480 | tf_op jit(solution)/shard_map/ppermute | solution.py:20
  113.0 25.6 %all-to-all-start.3 = ((f32[128,1,2048]{2,1,0:T(1,128)}), f32[128,1,2048]{2,1,0:T(1,128)}, u32[]{:S(2)}, u32[]{:S(2)}) async-start(f32[128,1,2048]{2,1,0:T(1,128)} %reshape.1262), calls=%async_computation.3 | async-start | bytes 2097152 | tf_op jit(solution)/shard_map/all_to_all | solution.py:41
  119.5 130.2 %copy-start.57 = (f32[2]{0:T(128)}, f32[2]{0:T(128)S(1)}, u32[]{:S(2)}) copy-start(f32[2]{0:T(128)S(1)} %fusion.136) | copy-start | bytes 28
  138.6 30.8 %all-to-all-start.2 = ((f32[128,1,2048]{2,1,0:T(1,128)}), f32[128,1,2048]{2,1,0:T(1,128)}, u32[]{:S(2)}, u32[]{:S(2)}) async-start(f32[128,1,2048]{2,1,0:T(1,128)} %reshape.1260), calls=%async_computation.2 | async-start | bytes 2097152 | tf_op jit(solution)/shard_map/all_to_all | solution.py:41
  169.4 58.0 %all-to-all-start.1 = ((f32[128,1,2048]{2,1,0:T(1,128)}), f32[128,1,2048]{2,1,0:T(1,128)}, u32[]{:S(2)}, u32[]{:S(2)}) async-start(f32[128,1,2048]{2,1,0:T(1,128)} %reshape.1258), calls=%async_computation.1 | async-start | bytes 2097152 | tf_op jit(solution)/shard_map/all_to_all | solution.py:41
  268.1 13.8 %copy-start.56 = (f32[3,1024]{1,0:T(4,128)S(1)}, f32[3,1024]{1,0:T(4,128)}, u32[]{:S(2)}) copy-start(f32[3,1024]{1,0:T(4,128)} %param.35) | copy-start | bytes 36868
  271.6 34.0 %all-to-all-start.4 = ((f32[128,1,2048]{2,1,0:T(1,128)}), f32[128,1,2048]{2,1,0:T(1,128)}, u32[]{:S(2)}, u32[]{:S(2)}) async-start(f32[128,1,2048]{2,1,0:T(1,128)} %reshape.1268), calls=%async_computation.4 | async-start | bytes 2097152 | tf_op jit(solution)/shard_map/all_to_all | solution.py:41
  281.8 13.9 %copy-start.59 = (s32[1024]{0:T(1024)}, s32[1024]{0:T(1024)S(1)}, u32[]{:S(2)}) copy-start(s32[1024]{0:T(1024)S(1)} %pad_clamp_fusion.5) | copy-start | bytes 12292
  284.0 70.8 %collective-permute-start = (f32[6,8,64]{2,0,1:T(8,128)}, f32[6,8,64]{2,0,1:T(8,128)}, u32[]{:S(2)}, u32[]{:S(2)}) collective-permute-start(f32[6,8,64]{2,0,1:T(8,128)} %select_bitcast_fusion.7), channel_id=1, source_target_pairs={{0,1},{1,2},{2,3},{3,4},{4,5},{5,6},{6,7},{7,8},{8,9},{9,10},{10,1... | collective-permute-start | bytes 36872 | tf_op jit(solution)/shard_map/ppermute | solution.py:20
  305.6 42.4 %all-to-all-start.5 = ((f32[128,1,2048]{2,1,0:T(1,128)}), f32[128,1,2048]{2,1,0:T(1,128)}, u32[]{:S(2)}, u32[]{:S(2)}) async-start(f32[128,1,2048]{2,1,0:T(1,128)} %reshape.1266), calls=%async_computation.5 | async-start | bytes 2097152 | tf_op jit(solution)/shard_map/all_to_all | solution.py:41
  316.5 39.0 %collective-permute-start.1 = (f32[6,8,64]{2,0,1:T(8,128)}, f32[6,8,64]{2,0,1:T(8,128)}, u32[]{:S(2)}, u32[]{:S(2)}) collective-permute-start(f32[6,8,64]{2,0,1:T(8,128)} %select_bitcast_fusion.6), channel_id=1, source_target_pairs={{0,31},{1,0},{2,1},{3,2},{4,3},{5,4},{6,5},{7,6},{8,7},{9,8},{10,9... | collective-permute-start | bytes 36872 | tf_op jit(solution)/shard_map/ppermute | solution.py:20
  323.0 15.1 %copy-start.61 = (s32[1024]{0:T(1024)}, s32[1024]{0:T(1024)S(1)}, u32[]{:S(2)}) copy-start(s32[1024]{0:T(1024)S(1)} %pad_clamp_fusion.3) | copy-start | bytes 12292
  324.2 91.2 %collective-permute-start.2 = (f32[6,8,64]{2,0,1:T(8,128)}, f32[6,8,64]{2,0,1:T(8,128)}, u32[]{:S(2)}, u32[]{:S(2)}) collective-permute-start(f32[6,8,64]{2,0,1:T(8,128)} %select_bitcast_fusion.5), channel_id=1, source_target_pairs={{0,32},{32,64},{64,96},{96,0},{1,33},{33,65},{65,97},{97,1},{2,34}... | collective-permute-start | bytes 36872 | tf_op jit(solution)/shard_map/ppermute | solution.py:20
  327.3 10.7 %copy-start.62 = (s32[1024]{0:T(1024)}, s32[1024]{0:T(1024)S(1)}, u32[]{:S(2)}) copy-start(s32[1024]{0:T(1024)S(1)} %pad_clamp_fusion.2) | copy-start | bytes 12292
  348.0 44.4 %all-to-all-start.6 = ((f32[128,1,2048]{2,1,0:T(1,128)}), f32[128,1,2048]{2,1,0:T(1,128)}, u32[]{:S(2)}, u32[]{:S(2)}) async-start(f32[128,1,2048]{2,1,0:T(1,128)} %reshape.1264), calls=%async_computation.6 | async-start | bytes 2097152 | tf_op jit(solution)/shard_map/all_to_all | solution.py:41
  354.2 62.1 %collective-permute-start.3 = (f32[6,8,64]{2,0,1:T(8,128)}, f32[6,8,64]{2,0,1:T(8,128)}, u32[]{:S(2)}, u32[]{:S(2)}) collective-permute-start(f32[6,8,64]{2,0,1:T(8,128)} %select_bitcast_fusion.4), channel_id=1, source_target_pairs={{0,96},{32,0},{64,32},{96,64},{1,97},{33,1},{65,33},{97,65},{2,98}... | collective-permute-start | bytes 36872 | tf_op jit(solution)/shard_map/ppermute | solution.py:20
  410.8 15.5 %collective-permute-start.6 = (f32[64,3,768]{2,0,1:T(8,128)S(1)}, f32[64,3,768]{2,0,1:T(8,128)S(1)}, u32[]{:S(2)}, u32[]{:S(2)}) collective-permute-start(f32[64,3,768]{2,0,1:T(8,128)S(1)} %copy.325), channel_id=1, source_target_pairs={{0,31},{1,0},{2,1},{3,2},{4,3},{5,4},{6,5},{7,6},{8,7},{9,8},{10,9... | collective-permute-start | bytes 1769480 | tf_op jit(solution)/shard_map/ppermute | solution.py:20
  429.1 73.1 %collective-permute-start.7 = (f32[3,11,768]{2,1,0:T(8,128)}, f32[3,11,768]{2,1,0:T(8,128)}, u32[]{:S(2)}, u32[]{:S(2)}) collective-permute-start(f32[3,11,768]{2,1,0:T(8,128)} %slice.651), channel_id=1, source_target_pairs={{0,96},{32,0},{64,32},{96,64},{1,97},{33,1},{65,33},{97,65},{2,98}... | collective-permute-start | bytes 304136 | tf_op jit(solution)/shard_map/ppermute | solution.py:20
  509.5 25.5 %copy-start.50 = (f32[3,1024]{1,0:T(4,128)S(1)}, f32[3,1024]{1,0:T(4,128)}, u32[]{:S(2)}) copy-start(f32[3,1024]{1,0:T(4,128)} %param.39) | copy-start | bytes 36868
  509.5 25.5 %copy-start.54 = (f32[1024]{0:T(1024)S(1)}, f32[1024]{0:T(1024)}, u32[]{:S(2)}) copy-start(f32[1024]{0:T(1024)} %param.38) | copy-start | bytes 12292
  556.0 9.3 collective-permute-start.12
  568.6 18.5 %collective-permute-start.13 = (f32[64,3,768]{2,0,1:T(8,128)S(1)}, f32[64,3,768]{2,0,1:T(8,128)S(1)}, u32[]{:S(2)}, u32[]{:S(2)}) collective-permute-start(f32[64,3,768]{2,0,1:T(8,128)S(1)} %copy.336), channel_id=1, source_target_pairs={{0,1},{1,2},{2,3},{3,4},{4,5},{5,6},{6,7},{7,8},{8,9},{9,10},{10,1... | collective-permute-start | bytes 1769480 | tf_op jit(solution)/shard_map/ppermute | solution.py:20
  625.6 24.8 %all-to-all-start.9 = ((f32[128,1,2048]{2,1,0:T(1,128)}), f32[128,1,2048]{2,1,0:T(1,128)}, u32[]{:S(2)}, u32[]{:S(2)}) async-start(f32[128,1,2048]{2,1,0:T(1,128)} %reshape.1274), calls=%async_computation.9 | async-start | bytes 2097152 | tf_op jit(solution)/shard_map/all_to_all | solution.py:41
  650.4 29.8 %all-to-all-start.8 = ((f32[128,1,2048]{2,1,0:T(1,128)}), f32[128,1,2048]{2,1,0:T(1,128)}, u32[]{:S(2)}, u32[]{:S(2)}) async-start(f32[128,1,2048]{2,1,0:T(1,128)} %reshape.1272), calls=%async_computation.8 | async-start | bytes 2097152 | tf_op jit(solution)/shard_map/all_to_all | solution.py:41
  680.2 47.8 %all-to-all-start.7 = ((f32[128,1,2048]{2,1,0:T(1,128)}), f32[128,1,2048]{2,1,0:T(1,128)}, u32[]{:S(2)}, u32[]{:S(2)}) async-start(f32[128,1,2048]{2,1,0:T(1,128)} %reshape.1270), calls=%async_computation.7 | async-start | bytes 2097152 | tf_op jit(solution)/shard_map/all_to_all | solution.py:41
  768.6 16.6 %copy-start.70 = (pred[8]{0:T(512)(128)(4,1)S(1)}, pred[8]{0:T(512)(128)(4,1)}, u32[]{:S(2)}) copy-start(pred[8]{0:T(512)(128)(4,1)} %copy-done.69) | copy-start | bytes 28
  772.1 34.2 %all-to-all-start.10 = ((f32[128,1,2048]{2,1,0:T(1,128)}), f32[128,1,2048]{2,1,0:T(1,128)}, u32[]{:S(2)}, u32[]{:S(2)}) async-start(f32[128,1,2048]{2,1,0:T(1,128)} %reshape.1280), calls=%async_computation.10 | async-start | bytes 2097152 | tf_op jit(solution)/shard_map/all_to_all | solution.py:41
  785.3 66.1 %collective-permute-start.8 = (f32[3,8,64]{2,0,1:T(4,128)S(1)}, f32[3,8,64]{2,0,1:T(4,128)S(1)}, u32[]{:S(2)}, u32[]{:S(2)}) collective-permute-start(f32[3,8,64]{2,0,1:T(4,128)S(1)} %select_bitcast_fusion.11), channel_id=1, source_target_pairs={{0,1},{1,2},{2,3},{3,4},{4,5},{5,6},{6,7},{7,8},{8,9},{9,10},{10,1... | collective-permute-start | bytes 18440 | tf_op jit(solution)/shard_map/ppermute | solution.py:20
  802.8 13.6 %copy-start.68 = (pred[8]{0:T(512)(128)(4,1)S(1)}, pred[8]{0:T(512)(128)(4,1)}, u32[]{:S(2)}) copy-start(pred[8]{0:T(512)(128)(4,1)} %copy-done.67) | copy-start | bytes 28
  802.8 20.2 %copy-start.66 = (pred[8]{0:T(512)(128)(4,1)S(1)}, pred[8]{0:T(512)(128)(4,1)}, u32[]{:S(2)}) copy-start(pred[8]{0:T(512)(128)(4,1)} %copy-done.65) | copy-start | bytes 28
  806.3 40.3 %all-to-all-start.11 = ((f32[128,1,2048]{2,1,0:T(1,128)}), f32[128,1,2048]{2,1,0:T(1,128)}, u32[]{:S(2)}, u32[]{:S(2)}) async-start(f32[128,1,2048]{2,1,0:T(1,128)} %reshape.1278), calls=%async_computation.11 | async-start | bytes 2097152 | tf_op jit(solution)/shard_map/all_to_all | solution.py:41
  816.5 15.7 %copy-start.5 = (f32[1,2,256,256]{3,2,1,0:T(8,128)S(1)}, f32[1,2,256,256]{3,2,1,0:T(8,128)}, u32[]{:S(2)}) copy-start(f32[1,2,256,256]{3,2,1,0:T(8,128)} %get-tuple-element.1054) | copy-start | bytes 1572868
  816.5 15.7 %copy-start.11 = (f32[1,2,256,256]{3,2,1,0:T(8,128)S(1)}, f32[1,2,256,256]{3,2,1,0:T(8,128)}, u32[]{:S(2)}) copy-start(f32[1,2,256,256]{3,2,1,0:T(8,128)} %get-tuple-element.1059) | copy-start | bytes 1572868
  816.6 35.4 %collective-permute-start.9 = (f32[3,8,64]{2,0,1:T(4,128)S(1)}, f32[3,8,64]{2,0,1:T(4,128)S(1)}, u32[]{:S(2)}, u32[]{:S(2)}) collective-permute-start(f32[3,8,64]{2,0,1:T(4,128)S(1)} %select_bitcast_fusion.10), channel_id=1, source_target_pairs={{0,31},{1,0},{2,1},{3,2},{4,3},{5,4},{6,5},{7,6},{8,7},{9,8},{10,9... | collective-permute-start | bytes 18440 | tf_op jit(solution)/shard_map/ppermute | solution.py:20
  823.2 88.5 %collective-permute-start.10 = (f32[3,8,64]{2,0,1:T(4,128)S(1)}, f32[3,8,64]{2,0,1:T(4,128)S(1)}, u32[]{:S(2)}, u32[]{:S(2)}) collective-permute-start(f32[3,8,64]{2,0,1:T(4,128)S(1)} %select_bitcast_fusion.9), channel_id=1, source_target_pairs={{0,32},{32,64},{64,96},{96,0},{1,33},{33,65},{65,97},{97,1},{2,34}... | collective-permute-start | bytes 18440 | tf_op jit(solution)/shard_map/ppermute | solution.py:20
  846.6 41.9 %all-to-all-start.12 = ((f32[128,1,2048]{2,1,0:T(1,128)}), f32[128,1,2048]{2,1,0:T(1,128)}, u32[]{:S(2)}, u32[]{:S(2)}) async-start(f32[128,1,2048]{2,1,0:T(1,128)} %reshape.1276), calls=%async_computation.12 | async-start | bytes 2097152 | tf_op jit(solution)/shard_map/all_to_all | solution.py:41
  851.3 61.0 %collective-permute-start.11 = (f32[3,8,64]{2,0,1:T(4,128)S(1)}, f32[3,8,64]{2,0,1:T(4,128)S(1)}, u32[]{:S(2)}, u32[]{:S(2)}) collective-permute-start(f32[3,8,64]{2,0,1:T(4,128)S(1)} %select_bitcast_fusion.8), channel_id=1, source_target_pairs={{0,96},{32,0},{64,32},{96,64},{1,97},{33,1},{65,33},{97,65},{2,98}... | collective-permute-start | bytes 18440 | tf_op jit(solution)/shard_map/ppermute | solution.py:20
  907.0 15.5 %collective-permute-start.14 = (f32[64,3,768]{2,0,1:T(8,128)S(1)}, f32[64,3,768]{2,0,1:T(8,128)S(1)}, u32[]{:S(2)}, u32[]{:S(2)}) collective-permute-start(f32[64,3,768]{2,0,1:T(8,128)S(1)} %copy.378), channel_id=1, source_target_pairs={{0,31},{1,0},{2,1},{3,2},{4,3},{5,4},{6,5},{7,6},{8,7},{9,8},{10,9... | collective-permute-start | bytes 1769480 | tf_op jit(solution)/shard_map/ppermute | solution.py:20
  913.8 14.3 %copy-start.42 = (f32[3,48,64]{2,0,1:T(4,128)S(1)}, f32[3,48,64]{2,0,1:T(4,128)}, u32[]{:S(2)}) copy-start(f32[3,48,64]{2,0,1:T(4,128)} %get-tuple-element.1600) | copy-start | bytes 110596
  925.4 43.9 %collective-permute-start.15 = (f32[3,11,768]{2,1,0:T(8,128)}, f32[3,11,768]{2,1,0:T(8,128)}, u32[]{:S(2)}, u32[]{:S(2)}) collective-permute-start(f32[3,11,768]{2,1,0:T(8,128)} %slice.671), channel_id=1, source_target_pairs={{0,96},{32,0},{64,32},{96,64},{1,97},{33,1},{65,33},{97,65},{2,98}... | collective-permute-start | bytes 304136 | tf_op jit(solution)/shard_map/ppermute | solution.py:20
  976.5 25.5 %copy-start.55 = (f32[1024]{0:T(1024)S(1)}, f32[1024]{0:T(1024)}, u32[]{:S(2)}) copy-start(f32[1024]{0:T(1024)} %param.38) | copy-start | bytes 12292
  (53 other events, 195.8 us)
where the time goes:
time: 1020 us; the launch traced here: 1000 us
  local copies, waits for them, and re-layouts  449 us (44%)
  matrix products  176 us (17%)
  other arithmetic  172 us (17%)
  starting transfers between devices  155 us (15%)
  waiting for transfers between devices  47.3 us (5%)
    all_to_all x12, starting transfers between devices, one_exchange(): lax.all_to_all(pieces, axis, split_axis=0, concat_axis=0, tiled=True)  105 us
    unnamed x179, local copies, waits for them, and re-layouts  91.6 us
    all_to_all x12, other arithmetic, one_exchange(): lax.all_to_all(pieces, axis, split_axis=0, concat_axis=0, tiled=True)  64 us
    ppermute x16, waiting for transfers between devices, shifted(): return lax.ppermute(value, axis, pairs)  47.2 us
    ppermute x16, starting transfers between devices, shifted(): return lax.ppermute(value, axis, pairs)  46 us
    another operation x16, local copies, waits for them, and re-layouts  37.5 us
    dot_general x4, matrix products, sample(): lax.dot_general(interpolate_widened, plane_rows, (((0,), (0,)), ((), ()))...  27.8 us
    dot_general x6, matrix products, shards(): jnp.einsum('oikn,nixz->zoxk', inverse_table, spectrum, precision=highest)  27.7 us
  transfers between devices with their start and end apart: 29, of which 4 were waited for; matrix products, arithmetic and copies ran while one was open for 54% of the time, Pallas kernels for 0%

commit v1 on v0

v1 whole, which is shorter than its diff:
```python
import functools
import math

import jax
import jax.numpy as jnp
import numpy as np
from jax import lax
from jax.experimental import pallas as pl
from jax.experimental.pallas import tpu as pltpu
from jax.sharding import PartitionSpec as P

G = 256
ITERS = 2

damping = 1.0
recip_scale = 16.0
high = lax.Precision.HIGH
highest = lax.Precision.HIGHEST
LANES = 128
MESH = pl.DeviceIdType.MESH


def shifted(value, axis, steps):
    count = lax.axis_size(axis)
    pairs = [(source, (source + steps) % count) for source in range(count)]
    return lax.ppermute(value, axis, pairs)


def spline_weights(fraction):
    square = fraction * fraction
    cube = square * fraction
    rest = 1.0 - fraction
    return [
        rest * rest * rest / 6.0,
        (3.0 * cube - 6.0 * square + 4.0) / 6.0,
        (-3.0 * cube + 3.0 * square + 3.0 * fraction + 1.0) / 6.0,
        cube / 6.0,
    ]


def axis_table(start, fraction, length, wrapped):
    offset = jnp.arange(length, dtype=jnp.int32)[:, None] - start[..., None, :]
    if wrapped:
        offset = offset % length
    table = 0.0
    for stencil, weight in enumerate(spline_weights(fraction)):
        table = table + jnp.where(offset == stencil, weight[..., None, :], 0.0)
    return table


def pair_kernel(cell_count, width, list_ref, count_ref, table_ref, near_ref, out_ref):
    lane = lax.broadcasted_iota(jnp.int32, (8, 2 * width), 1)
    row = lax.broadcasted_iota(jnp.int32, (8, 2 * width), 0)
    first_half = lane < width
    is_moment = row >= 3
    itself = lax.broadcasted_iota(jnp.int32, (width, 2 * width), 0) == lax.broadcasted_iota(
        jnp.int32, (width, 2 * width), 1
    )

    def one_cell(cell, _):
        base = pl.multiple_of(cell * width, width)
        near = near_ref[pl.ds(base, width), :]
        near_x = jnp.broadcast_to(near[:, 0:1], (width, 2 * width))
        near_y = jnp.broadcast_to(near[:, 1:2], (width, 2 * width))
        near_z = jnp.broadcast_to(near[:, 2:3], (width, 2 * width))
        count = count_ref[cell]

        def terms(pair, masked):
            one = table_ref[list_ref[cell, 2 * pair]]
            two = table_ref[list_ref[cell, 2 * pair + 1]]
            live = 2 * pair + 1 < count
            two = jnp.where(jnp.logical_and(is_moment, jnp.logical_not(live)), 0.0, two)
            far = jnp.where(first_half, one, two)
            dx = near_x - far[0:1]
            dy = near_y - far[1:2]
            dz = near_z - far[2:3]
            mx, my, mz = far[3:4], far[4:5], far[5:6]
            softened = dx * dx + dy * dy + dz * dz + damping
            inverse = lax.rsqrt(softened)
            square = inverse * inverse
            cube = square * inverse
            if masked:
                cube = jnp.where(itself, 0.0, cube)
            radial = (3.0 * (dx * mx + dy * my + dz * mz)) * (cube * square)
            return radial * dx - cube * mx, radial * dy - cube * my, radial * dz - cube * mz

        def step(pair, totals):
            return tuple(t + a for t, a in zip(totals, terms(pair, False)))

        totals = lax.fori_loop(1, (count + 1) // 2, step, terms(0, True))
        sums = [jnp.sum(t, axis=1, keepdims=True) for t in totals]
        column = lax.broadcasted_iota(jnp.int32, (width, 8), 1)
        out = jnp.where(column == 0, sums[0], jnp.where(column == 1, sums[1], sums[2]))
        out_ref[pl.ds(base, width), :] = out
        return 0

    lax.fori_loop(0, cell_count, one_cell, 0)


def pair_field(lists, counts, table, near):
    cell_count = counts.shape[0]
    width = near.shape[0] // cell_count
    vmem = pl.BlockSpec(memory_space=pltpu.VMEM)
    smem = pl.BlockSpec(memory_space=pltpu.SMEM)
    pairs = cell_count * lists.shape[1] * width * width // 2
    return pl.pallas_call(
        functools.partial(pair_kernel, cell_count, width),
        out_shape=jax.ShapeDtypeStruct((near.shape[0], 8), jnp.float32),
        in_specs=[smem, smem, vmem, vmem],
        out_specs=vmem,
        cost_estimate=pl.CostEstimate(flops=40 * pairs, bytes_accessed=1 << 20, transcendentals=pairs),
        name="pair_field",
    )(lists, counts, table, near)


def influence_kernel(slabs, subs, moved_ref, planes_ref, send_sem, recv_sem):
    slab, sub = lax.axis_index("slab"), lax.axis_index("sub")
    depth, rows = moved_ref.shape[0], moved_ref.shape[1]
    half = slabs * subs

    def parts(i):
        kz = depth * sub + i
        upper = kz >= half
        folded = jnp.where(upper, lax.rem(2 * half - kz, half), kz)
        slot = upper.astype(jnp.int32)
        return lax.rem(folded, slabs), folded // slabs, slot

    def both(i):
        to_slab, to_sub, slot = parts(i)
        target = planes_ref.at[slot, pl.ds(slab * rows, rows)]
        far = pltpu.make_async_remote_copy(
            src_ref=moved_ref.at[i],
            dst_ref=target,
            send_sem=send_sem.at[i],
            recv_sem=recv_sem.at[slot, slab],
            device_id=(to_slab, to_sub),
            device_id_type=MESH,
        )
        here = pltpu.make_async_copy(moved_ref.at[i], target, recv_sem.at[slot, slab])
        return far, here, jnp.logical_and(to_slab == slab, to_sub == sub)

    for i in range(depth):
        far, here, mine = both(i)

        @pl.when(mine)
        def _():
            here.start()

        @pl.when(jnp.logical_not(mine))
        def _():
            far.start()

    for slot in range(2):
        for source in range(slabs):
            pltpu.make_async_copy(
                planes_ref.at[slot, pl.ds(source * rows, rows)],
                planes_ref.at[slot, pl.ds(source * rows, rows)],
                recv_sem.at[slot, source],
            ).wait()
    for i in range(depth):
        far, here, mine = both(i)

        @pl.when(jnp.logical_not(mine))
        def _():
            far.wait_send()


def influence_planes(influence, slabs, subs):
    moved = jnp.transpose(influence, (1, 0, 2))
    depth, rows, columns = moved.shape
    anywhere = pl.BlockSpec(memory_space=pl.ANY)
    return pl.pallas_call(
        functools.partial(influence_kernel, slabs, subs),
        out_shape=jax.ShapeDtypeStruct((2, slabs * rows, columns), jnp.float32),
        in_specs=[anywhere],
        out_specs=anywhere,
        scratch_shapes=[pltpu.SemaphoreType.DMA((depth,)), pltpu.SemaphoreType.DMA((2, slabs))],
        compiler_params=pltpu.CompilerParams(has_side_effects=True),
        name="influence_planes",
    )(moved)


def shards(
    positions,
    fraction,
    grid_base,
    polarizability,
    perm_field,
    influence,
    neighbour_cells,
    neighbour_count,
    send_cells,
):
    atoms = positions.shape[1]
    cells = neighbour_cells.shape[0]
    width = atoms // cells
    ghosts = send_cells.shape[2]
    slabs = lax.axis_size("slab")
    subs = lax.axis_size("sub")
    slab = lax.axis_index("slab")
    sub = lax.axis_index("sub")
    grid_x = G // slabs
    grid_y = G // subs
    pad_x = grid_x + 8
    half = G // 2
    nyquist = float(-half)

    index = np.arange(G)
    angle = (index[:, None] * index[None, :] % G) * (2.0 * np.pi / G)
    cosine = jnp.asarray(np.cos(angle), jnp.float32)
    sine = jnp.asarray(np.sin(angle), jnp.float32)
    signed = np.where(index < half, index, index - G).astype(np.float32)
    odd = np.where(index == half, 0.0, signed).astype(np.float32)
    even = np.where(index == half, nyquist, 0.0).astype(np.float32)

    kz_all = slabs * jnp.arange(subs, dtype=jnp.int32) + slab
    kz_here = slabs * sub + slab

    planes = influence_planes(influence, slabs, subs)
    flip = jnp.asarray((index[:, None] == (-index[None, :]) % G).astype(np.float32))
    mirrored = jnp.dot(jnp.dot(flip, planes[1], precision=highest), flip, precision=highest)
    first = planes[0]
    sq = jnp.asarray(signed[:, None] ** 2 + signed[None, :] ** 2)
    kzf = kz_here.astype(jnp.float32)
    freq_sq = sq + kzf * kzf
    width_sq = G / 4.0 * (G / 4.0)
    gauss = jnp.where(
        freq_sq == 0.0,
        0.0,
        jnp.exp(-freq_sq / (2.0 * width_sq)) / jnp.where(freq_sq == 0.0, 1.0, freq_sq),
    ) * (-recip_scale / (float(G) ** 3))
    flat = kz_here == 0
    kernel_even = gauss * jnp.where(flat, first, first + mirrored)
    kernel_odd = gauss * jnp.where(flat, first, first - mirrored)
    rows_mid = jnp.transpose(influence[:, 0, :])
    rows_mid = lax.all_to_all(rows_mid, "slab", split_axis=0, concat_axis=1, tiled=True)
    rows_mid = lax.all_to_all(
        rows_mid.reshape(subs, 2, G), "sub", split_axis=0, concat_axis=0, tiled=True
    )
    mid = rows_mid[subs // 2]
    kx_mid = (2 * (subs * slab + sub) + jnp.arange(2, dtype=jnp.int32)).astype(jnp.float32)
    kx_mid = jnp.where(kx_mid < half, kx_mid, kx_mid - G)
    mid_sq = (kx_mid * kx_mid)[None, :] + jnp.asarray(signed[:, None] ** 2) + float(half * half)
    kernel_mid = (
        jnp.transpose(mid) * jnp.exp(-mid_sq / (2.0 * width_sq)) / mid_sq * (-recip_scale / (float(G) ** 3))
    )

    moments = polarizability[None, :] * perm_field
    sent_lists = jnp.pad(
        send_cells.reshape(1, 4 * ghosts).astype(jnp.float32), ((0, 0), (0, atoms - 4 * ghosts))
    )
    packet = jnp.concatenate(
        [moments, positions, fraction, grid_base.astype(jnp.float32), sent_lists], axis=0
    )

    def blocks(packet):
        own = lax.all_gather(packet, "slab", axis=0)
        before = shifted(own, "sub", 1)
        after = shifted(packet, "sub", -1)
        near = jnp.stack(
            [
                packet,
                lax.dynamic_index_in_dim(before, slab, 0, keepdims=False),
                after,
                lax.dynamic_index_in_dim(own, lax.rem(slab + slabs - 1, slabs), 0, keepdims=False),
                lax.dynamic_index_in_dim(own, lax.rem(slab + 1, slabs), 0, keepdims=False),
            ]
        )
        return jnp.stack([own, before]), near

    both, near = blocks(packet)
    frac = both[:, :, 6:9]
    base = both[:, :, 9:12].astype(jnp.int32)
    table_x = axis_table(base[:, :, 0], frac[:, :, 0], pad_x, False)
    table_y = axis_table(base[:, :, 1], frac[:, :, 1], grid_y + 3, False)
    depth = axis_table(base[:, :, 2], frac[:, :, 2], G, True)
    plane_own = (table_y[0, :, :grid_y, None, :] * table_x[0, :, None, :, :]).reshape(
        slabs, grid_y * pad_x, atoms
    )
    plane_before = (table_y[1, :, grid_y:, None, :] * table_x[1, :, None, :, :]).reshape(
        slabs, 3 * pad_x, atoms
    )
    pick = (kz_all[:, None] == jnp.arange(G)[None, :]).astype(jnp.float32)
    cos_z = jnp.dot(pick, cosine, precision=highest)
    sin_z = jnp.dot(pick, sine, precision=highest)
    alternate = jnp.asarray(np.where(index % 2 == 0, 1.0, -1.0).astype(np.float32))[None]
    phase = jnp.concatenate([cos_z, -sin_z, alternate], axis=0)
    zhat = jnp.einsum("rz,pbza->pbra", phase, depth, precision=high)
    ranks = 2 * subs + 1

    lists = jnp.where(neighbour_cells < cells, neighbour_cells, 0)
    for q in range(4):
        for slot in range(ghosts):
            entry = cells + q * ghosts + slot
            cell = near[1 + q, 12, q * ghosts + slot].astype(jnp.int32) + cells * (1 + q)
            lists = lists + jnp.where(neighbour_cells == entry, cell, 0)
    near_atoms = jnp.pad(jnp.transpose(positions), ((0, 0), (0, 5)))

    def far_table(near_moments):
        rows = jnp.concatenate([near[:, 3:6], near_moments], axis=1)
        rows = jnp.transpose(rows.reshape(5, 6, cells, width), (0, 2, 1, 3)).reshape(5 * cells, 6, width)
        rows = jnp.pad(rows, ((0, 0), (0, 2), (0, 0)))
        return jnp.concatenate([rows, rows], axis=2)

    forward = jnp.concatenate([cosine, sine], axis=1)
    upright = jnp.concatenate([cosine, sine], axis=0)
    odd_j, even_j, signed_j = jnp.asarray(odd), jnp.asarray(even), jnp.asarray(signed)
    at_half = jnp.asarray((index == half).astype(np.float32))
    kz_f = kz_all.astype(jnp.float32)[:, None, None]
    group = 2 * subs
    cos_group = lax.dynamic_slice_in_dim(cosine, slab * group, group, 0)
    sin_group = lax.dynamic_slice_in_dim(sine, slab * group, group, 0)
    signed_group = lax.dynamic_slice_in_dim(signed_j, slab * group, group, 0)

    def reciprocal(block_moments):
        values = (block_moments[:, :, :, None, :] * zhat[:, :, None, :, :]).reshape(
            2, slabs, 3 * ranks, atoms
        )
        spread = jnp.einsum("bga,bra->bgr", plane_own, values[0], precision=high)
        extra = jnp.einsum("bga,bra->bgr", plane_before, values[1], precision=high)
        spread = spread.reshape(slabs, grid_y, pad_x, 3 * ranks)
        extra = extra.reshape(slabs, 3, pad_x, 3 * ranks)
        spread = jnp.concatenate([spread[:, :3] + extra, spread[:, 3:]], axis=1)
        spill = jnp.roll(spread[:, :, grid_x:], 1, axis=0)
        spread = jnp.concatenate(
            [spread[:, :, :8] + spill, spread[:, :, 8:grid_x]], axis=2
        )
        turned = jnp.einsum(
            "byxr,bxk->ryk", spread, forward.reshape(slabs, grid_x, 2 * G), precision=high
        ).reshape(3, ranks, grid_y, 2, G)
        real_c, real_s = turned[:, :subs, :, 0], turned[:, :subs, :, 1]
        imag_c, imag_s = turned[:, subs : 2 * subs, :, 0], turned[:, subs : 2 * subs, :, 1]
        spec_re = real_c + imag_s
        spec_im = imag_c - real_s
        a_re = odd_j * spec_re[0] + kz_f * spec_re[2]
        a_im = odd_j * spec_im[0] + kz_f * spec_im[2]
        ae = nyquist * jnp.stack([spec_re[0, :, :, half], spec_im[0, :, :, half]], axis=-1)
        mid_re = lax.dynamic_slice_in_dim(turned[:, -1, :, 0], slab * group, group, 2)
        mid_im = -lax.dynamic_slice_in_dim(turned[:, -1, :, 1], slab * group, group, 2)
        mid_ab = jnp.stack(
            [
                signed_group * mid_re[0] + nyquist * mid_re[2],
                signed_group * mid_im[0] + nyquist * mid_im[2],
                mid_re[1],
                mid_im[1],
            ]
        )
        mid_ab = jnp.transpose(mid_ab.reshape(4, grid_y, subs, 2), (2, 1, 0, 3)).reshape(
            subs, grid_y, 8
        )
        payload = jnp.concatenate(
            [
                a_re,
                a_im,
                spec_re[1],
                spec_im[1],
                ae,
                mid_ab,
                jnp.zeros((subs, grid_y, LANES - 10), jnp.float32),
            ],
            axis=2,
        )
        got = lax.all_to_all(payload, "sub", split_axis=0, concat_axis=0, tiled=True)
        got = got.reshape(G, 4 * G + LANES)

        y = jnp.dot(upright, got, precision=high)
        yc, ys = y[:G], y[G:]

        def pick2(part, start, count):
            return part[:, start : start + count]

        def forward_y(re_start, im_start, count):
            return (
                pick2(yc, re_start, count) + pick2(ys, im_start, count),
                pick2(yc, im_start, count) - pick2(ys, re_start, count),
            )

        ar, ai = forward_y(0, G, G)
        br, bi = forward_y(2 * G, 3 * G, G)
        er, ei = forward_y(4 * G, 4 * G + 1, 1)
        mar, mai = forward_y(4 * G + 2, 4 * G + 4, 2)
        mbr, mbi = forward_y(4 * G + 6, 4 * G + 8, 2)
        odd_y, even_y, full_y = odd_j[:, None], even_j[:, None], signed_j[:, None]

        def applied(a, b, e):
            level = a + odd_y * b
            edge = even_y * b + at_half[None, :] * e
            phi = kernel_even * level + kernel_odd * edge
            phi_edge = kernel_odd * level + kernel_even * edge
            return phi, odd_y * phi + even_y * phi_edge, phi_edge[:, half : half + 1]

        phr, oyr, per = applied(ar, br, er)
        phi_, oyi, pei = applied(ai, bi, ei)
        mpr = kernel_mid * (mar + full_y * mbr)
        mpi = kernel_mid * (mai + full_y * mbi)
        spec = jnp.concatenate(
            [
                phr,
                phi_,
                oyr,
                oyi,
                per,
                pei,
                mpr,
                mpi,
                full_y * mpr,
                full_y * mpi,
                jnp.zeros((G, LANES - 10), jnp.float32),
            ],
            axis=1,
        )
        y = jnp.dot(upright, spec, precision=high)
        yc, ys = y[:G], y[G:]

        def backward_y(re_start, im_start, count):
            return [
                pick2(yc, re_start, count) - pick2(ys, im_start, count),
                pick2(yc, im_start, count) + pick2(ys, re_start, count),
            ]

        payload = jnp.concatenate(
            backward_y(0, G, G)
            + backward_y(2 * G, 3 * G, G)
            + backward_y(4 * G, 4 * G + 1, 1)
            + backward_y(4 * G + 2, 4 * G + 4, 2)
            + backward_y(4 * G + 6, 4 * G + 8, 2)
            + [jnp.zeros((G, LANES - 10), jnp.float32)],
            axis=1,
        ).reshape(subs, grid_y, 4 * G + LANES)
        got = lax.all_to_all(payload, "sub", split_axis=0, concat_axis=0, tiled=True)

        ph_r, ph_i = got[:, :, :G], got[:, :, G : 2 * G]
        pe_r, pe_i = got[:, :, 4 * G : 4 * G + 1], got[:, :, 4 * G + 1 : 4 * G + 2]
        ex_r = odd_j * ph_r + even_j * pe_r
        ex_i = odd_j * ph_i + even_j * pe_i
        stacked_r = jnp.stack([ex_r, got[:, :, 2 * G : 3 * G], kz_f * ph_r])
        stacked_i = jnp.stack([ex_i, got[:, :, 3 * G : 4 * G], kz_f * ph_i])
        parts = jnp.einsum(
            "icjyk,kn->cyijn", jnp.stack([stacked_r, stacked_i]), forward, precision=high
        )
        field_r = parts[:, :, 0, :, :G] - parts[:, :, 1, :, G:]
        field_i = parts[:, :, 0, :, G:] + parts[:, :, 1, :, :G]
        mids = jnp.transpose(
            got[:, :, 4 * G + 2 : 4 * G + 10].reshape(subs, grid_y, 4, 2), (2, 1, 0, 3)
        ).reshape(4, grid_y, group)
        mid_r = jnp.stack([signed_group * mids[0], mids[2], nyquist * mids[0]])
        mid_i = jnp.stack([signed_group * mids[1], mids[3], nyquist * mids[1]])
        field_m = jnp.dot(mid_r, cos_group, precision=high) - jnp.dot(mid_i, sin_group, precision=high)
        field = jnp.concatenate([field_r, field_i, field_m[:, :, None, :]], axis=2)
        field = jnp.transpose(field, (1, 3, 0, 2)).reshape(grid_y, slabs, grid_x, 3 * ranks)
        wide = jnp.concatenate([field, jnp.roll(field[:, :, :8], -1, axis=1)], axis=2)
        wide = jnp.transpose(wide, (1, 0, 2, 3))
        mixed_own = jnp.einsum(
            "bga,bgr->bra",
            plane_own,
            wide.reshape(slabs, grid_y * pad_x, 3 * ranks),
            precision=high,
        )
        mixed_before = jnp.einsum(
            "bga,bgr->bra",
            plane_before,
            wide[:, :3].reshape(slabs, 3 * pad_x, 3 * ranks),
            precision=high,
        )
        mixed = jnp.stack([mixed_own, mixed_before]).reshape(2, slabs, 3, ranks, atoms)
        return jnp.sum(mixed * zhat[:, :, None], axis=3)

    block_moments = both[:, :, :3]
    near_moments = near[:, :3]
    for advance in range(ITERS):
        pair = pair_field(lists, neighbour_count, far_table(near_moments), near_atoms)
        share = reciprocal(block_moments)
        share = jnp.transpose(share, (1, 0, 2, 3)).reshape(slabs, 6, atoms)
        share = lax.psum_scatter(share, "slab", scatter_dimension=0)
        field = share[:3] + shifted(share[3:], "sub", -1)
        moments = polarizability[None, :] * (perm_field + jnp.transpose(pair[:, :3]) + field)
        if advance + 1 < ITERS:
            block_moments, near_moments = blocks(moments)
    return moments


def solution(mesh):
    in_specs = (
        P(None, ("slab", "sub")),
        P(None, ("slab", "sub")),
        P(None, ("slab", "sub")),
        P(("slab", "sub")),
        P(None, ("slab", "sub")),
        P("slab", "sub", None),
        P(("slab", "sub"), None),
        P(("slab", "sub")),
        P(("slab", "sub"), None, None),
    )
    out_specs = P(None, ("slab", "sub"))
    return jax.shard_map(shards, mesh=mesh, in_specs=in_specs, out_specs=out_specs, check_vma=False)
```

time: 1020 us -> 664 us (0.65)
  local copies, waits for them, and re-layouts: 449 us -> 238 us
  other arithmetic: 172 us -> 61.7 us
  starting transfers between devices: 155 us -> 53.8 us
  matrix products: 176 us -> 75.4 us
  waiting for transfers between devices: 47.3 us -> 114 us
  Pallas kernels: 0 us -> 38.5 us
  blocking collectives: 0 us -> 38.2 us
  between operations: 1.68 us -> 35.3 us
    dot_general x44 -> x25, matrix products: 176 us -> 75.4 us  [the longest x2 15.7 us: reciprocal(): jnp.einsum('bga,bgr->bra', plane_own, wide.reshape(slabs, grid_y * pad_x,...]
    all_to_all x13 -> x5, starting transfers between devices: 109 us -> 30.3 us  [the longest x3 17.2 us: reciprocal(): lax.all_to_all(payload, 'sub', split_axis=0, concat_axis=0, tiled=True)]
    reduce_scatter x0 -> x2, waiting for transfers between devices: none -> 73.6 us  [shards(): share = lax.psum_scatter(share, 'slab', scatter_dimension=0)]
    another operation x28 -> x14, local copies, waits for them, and re-layouts: 80 us -> 14.1 us  [the longest x6 7.92 us: reciprocal(): jnp.stack([signed_group * mid_re[0] + nyquist * mid_re[2], signed_group *...]
    all_to_all x12 -> x1, other arithmetic: 64 us -> 0.8 us  [shards(): lax.all_to_all(rows_mid, 'slab', split_axis=0, concat_axis=1, tiled=True)]
    unnamed x179 -> x184, local copies, waits for them, and re-layouts: 91.6 us -> 32.9 us
    reshape x54 -> x13, local copies, waits for them, and re-layouts: 83.4 us -> 29.3 us  [the longest x2 10.1 us: reciprocal(): turned = jnp.einsum('byxr,bxk->ryk', spread, forward.reshape(slabs, grid_...]
    slice x58 -> x60, local copies, waits for them, and re-layouts: 43.1 us -> 91.7 us  [the longest x2 11.3 us: reciprocal(): turned[:, subs:2 * subs, :, 0]]
  transfers between devices with their start and end apart: 29 -> 13, of which waited for: 4 -> 8; matrix products, arithmetic and copies ran while one was open for 54% -> 18% of each run, Pallas kernels for 0% -> 6%
where the time goes in v1:
time: 664 us; the launch traced here: 655 us
  local copies, waits for them, and re-layouts  238 us (36%)
  waiting for transfers between devices  114 us (17%)
  matrix products  75.4 us (11%)
  other arithmetic  61.7 us (9%)
  starting transfers between devices  53.8 us (8%)
  Pallas kernels  38.5 us (6%)
  blocking collectives  38.2 us (6%)
  between operations  35.3 us (5%)
    reduce_scatter x2, waiting for transfers between devices, shards(): share = lax.psum_scatter(share, 'slab', scatter_dimension=0)  73.6 us
    unnamed x184, local copies, waits for them, and re-layouts  32.9 us
    ppermute x6, waiting for transfers between devices, shifted(): return lax.ppermute(value, axis, pairs)  31.6 us
    pallas_call x1, Pallas kernels, influence_planes(): pl.pallas_call(functools.partial(influence_kernel, slabs, subs), out_shap...  24.7 us
    ppermute x6, starting transfers between devices, shifted(): return lax.ppermute(value, axis, pairs)  23.3 us
    all_to_all x1, blocking collectives, reciprocal(): lax.all_to_all(payload, 'sub', split_axis=0, concat_axis=0, tiled=True)  21.4 us
    all_to_all x3, starting transfers between devices, reciprocal(): lax.all_to_all(payload, 'sub', split_axis=0, concat_axis=0, tiled=True)  17.2 us
    all_gather x2, blocking collectives, blocks(): own = lax.all_gather(packet, 'slab', axis=0)  16.8 us
  transfers between devices with their start and end apart: 13, of which 8 were waited for; matrix products, arithmetic and copies ran while one was open for 18% of the time, Pallas kernels for 6%

profile of v1, /device:TPU:1, one launch (start us, length us, event | category | flops | bytes accessed | tf_op | source)
XLA Modules:
  0.0 654.5 jit_solution(10526384504273298144)
XLA Ops:
  10.4 8.6 %all-gather.2 = f32[4,13,1024]{2,1,0:T(8,128)S(1)} all-gather(f32[1,13,1024]{2,1,0:T(8,128)S(1)} %bitcast.486), channel_id=2, replica_groups=mesh['slab'=4,'sub'=32] {'slab'}, dimensions={0}, use_global_device_ids=true | all-gather | bytes 266240 | tf_op jit(solution)/shard_map/all_gather | solution.py:257
  23.0 4.7 all-to-all-start.1
  34.8 8.3 %all-to-all-start.2 = ((f32[32,2,256]{2,1,0:T(2,128)}), f32[32,2,256]{2,1,0:T(2,128)}, u32[]{:S(2)}, u32[]{:S(2)}) async-start(f32[32,2,256]{2,1,0:T(2,128)} %reshape.607), calls=%async_computation.2 | async-start | bytes 131072 | tf_op jit(solution)/shard_map/all_to_all | solution.py:237
  43.8 9.1 %fusion.62 = f32[2,4,65,1024]{3,2,1,0:T(8,128)S(1)} fusion(f32[2,4,1024]{2,1,0:T(4,128)S(1)} %get-tuple-element.159, f32[2,4,1024]{2,1,0:T(4,128)S(1)} %get-tuple-element.160, f32[2,4,1024]{2,1,0:T(4,128)S(1)} %get-tuple-element.158, f32[2,4,1024]{2,1,0:T(4,128)S(1)} %get-tuple-element.31, s32[2,4,1024]{2,1,0:T(4,128)S(1)} %get-tuple-element.139, ...), kind=kOutput, calls=%fused_computation.76 | convolution fusion | flops 866157056 | bytes 2360320 | tf_op jit(solution)/shard_map/rz,pbza->pbra/dot_general | solution.py:288
  59.4 3.5 fusion.34
  64.2 5.9 fusion.36
  71.1 3.6 fusion.56
  74.8 5.0 reshape.646
  80.7 5.8 fusion.285
  114.4 3.0 copy.707
  117.4 7.9 %all-to-all-start = ((f32[32,8,1152]{2,1,0:T(8,128)}), f32[32,8,1152]{2,1,0:T(8,128)}, u32[]{:S(2)}, u32[]{:S(2)}) async-start(f32[32,8,1152]{2,1,0:T(8,128)} %copy.707), calls=%async_computation | async-start | bytes 2359296 | tf_op jit(solution)/shard_map/all_to_all | solution.py:363
  125.3 5.5 collective-permute-start.1
  130.8 24.7 %influence_planes.1 = f32[2,256,256]{2,1,0:T(8,128)} custom-call(f32[8,64,256]{2,1,0:T(8,128)} %bitcast.474), custom_call_target="tpu_custom_call" | custom-call | tf_op jit(solution)/shard_map/influence_planes/pallas_call | solution.py:172
  211.7 4.7 all-to-all-start.3
  228.5 6.1 all-to-all-done.3
  265.9 3.8 reshape.610
  272.3 2.9 slice.1217
  275.2 3.5 maximum_bitcast_fusion
  281.8 4.7 copy.732
  288.9 8.6 %fusion.297 = f32[4,195,1024]{2,1,0:T(8,128)S(1)} fusion(f32[4,576,195]{2,1,0:T(8,128)} %bitcast.462, f32[4,576,1024]{2,1,0:T(8,128)} %bitcast.438), kind=kOutput, calls=%fused_computation.512 | convolution fusion | flops 2760376320 | bytes 14429184 | tf_op jit(solution)/shard_map/bga,bgr->bra/dot_general | solution.py:453
  303.4 3.0 fusion.16
  306.4 2.9 copy.738
  310.0 34.4 %reduce-scatter.3.cloned.1.call-done = f32[1,6,1024]{1,2,0:T(8,128)} async-done(((f32[4,6,1024]{1,2,0:T(8,128)}), f32[1,6,1024]{1,2,0:T(8,128)}) %reduce-scatter.3.cloned.1.call-update) | async-done | bytes 24592 | tf_op jit(solution)/shard_map/reduce_scatter | solution.py:474
  346.4 4.9 collective-permute-start.2
  353.2 6.9 %pair_field.2 = f32[1024,8]{1,0:T(8,128)} custom-call(s32[16,16]{1,0:T(8,128)} %select_add_fusion.2.list_ref, s32[16]{0:T(128)} %count_ref.3, f32[80,8,128]{2,1,0:T(8,128)} %pad_maximum_fusion.table_ref, f32[1024,8]{1,0:T(8,128)} %pad.17.near_ref), custom_call_target="tpu_custom_call" | custom-call | flops 20971520 | bytes 1048576 | tf_op jit(solution)/shard_map/pair_field/pallas_call | solution.py:106
  365.9 8.1 %all-gather.3 = f32[4,3,1024]{2,1,0:T(4,128)S(1)} all-gather(f32[1,3,1024]{2,1,0:T(4,128)S(1)} %copy.742), channel_id=3, replica_groups=mesh['slab'=4,'sub'=32] {'slab'}, dimensions={0}, use_global_device_ids=true | all-gather | bytes 61440 | tf_op jit(solution)/shard_map/all_gather | solution.py:257
  374.6 8.4 %collective-permute-done.3 = f32[4,3,1024]{2,0,1:T(4,128)S(1)} collective-permute-done((f32[4,3,1024]{2,0,1:T(4,128)S(1)}, f32[4,3,1024]{2,0,1:T(4,128)S(1)}, u32[]{:S(2)}, u32[]{:S(2)}) %collective-permute-start.3) | collective-permute-done | bytes 49184 | tf_op jit(solution)/shard_map/ppermute | solution.py:26
  383.6 3.2 broadcast_multiply_fusion.1
  386.9 3.3 fusion.280
  390.2 3.5 fusion.30
  393.7 5.5 fusion.32
  400.3 3.8 fusion.59
  404.1 5.1 reshape.647
  410.1 5.5 fusion.283
  444.1 21.4 %all_to_all.41 = f32[32,8,1152]{2,1,0:T(8,128)S(1)} all-to-all(f32[32,8,1152]{2,1,0:T(8,128)S(1)} %copy.773), channel_id=1, replica_groups=mesh['slab'=4,'sub'=32] {'sub'}, dimensions={0} | all-to-all | bytes 2359296 | tf_op jit(solution)/shard_map/all_to_all | solution.py:363
  481.6 4.7 all-to-all-start.5
  486.4 5.8 collective-permute-start.4
  492.7 18.3 %collective-permute-done.4 = f32[3,1024]{0,1:T(8,128)} collective-permute-done((f32[3,1024]{0,1:T(8,128)}, f32[3,1024]{0,1:T(8,128)}, u32[]{:S(2)}, u32[]{:S(2)}) %collective-permute-start.4) | collective-permute-done | bytes 12320 | tf_op jit(solution)/shard_map/ppermute | solution.py:26
  546.8 3.8 reshape.623
  553.2 2.9 slice.1301
  556.2 3.5 maximum_bitcast_fusion.1
  562.7 4.7 copy.792
  569.8 2.9 fusion.301
  574.7 7.1 %fusion.300 = f32[4,195,1024]{2,1,0:T(8,128)S(1)} fusion(f32[4,576,195]{2,1,0:T(8,128)S(1)} %bitcast.461, f32[4,576,1024]{2,1,0:T(8,128)} %bitcast.439), kind=kOutput, calls=%fused_computation.515 | convolution fusion | flops 2760376320 | bytes 14429184 | tf_op jit(solution)/shard_map/bga,bgr->bra/dot_general | solution.py:453
  589.3 39.2 %reduce-scatter.5.cloned.1.call-done = f32[1,6,1024]{1,2,0:T(8,128)} async-done(((f32[4,6,1024]{1,2,0:T(8,128)}), f32[1,6,1024]{1,2,0:T(8,128)}) %reduce-scatter.5.cloned.1.call-update) | async-done | bytes 24592 | tf_op jit(solution)/shard_map/reduce_scatter | solution.py:474
  629.8 4.9 collective-permute-start.5
  635.6 6.9 %pair_field.3 = f32[1024,8]{1,0:T(8,128)} custom-call(s32[16,16]{1,0:T(8,128)} %select_add_fusion.2.list_ref, s32[16]{0:T(128)} %count_ref.3, f32[80,8,128]{2,1,0:T(8,128)} %pad_maximum_fusion.1.table_ref, f32[1024,8]{1,0:T(8,128)} %pad.17.near_ref), custom_call_target="tpu_custom_call" | custom-call | flops 20971520 | bytes 1048576 | tf_op jit(solution)/shard_map/pair_field/pallas_call | solution.py:106
  642.5 2.9 collective-permute-done.5
  (416 shorter events, 261.8 us)
Async XLA Ops:
  6.5 21.2 %copy-start.32 = (f32[256,256]{1,0:T(8,128)S(1)}, f32[256,256]{1,0:T(8,128)}, u32[]{:S(2)}) copy-start(f32[256,256]{1,0:T(8,128)} %constant.245.clone) | copy-start | bytes 786436
  6.5 21.5 %copy-start.33 = (f32[256,256]{1,0:T(8,128)S(1)}, f32[256,256]{1,0:T(8,128)}, u32[]{:S(2)}) copy-start(f32[256,256]{1,0:T(8,128)} %constant.244.clone) | copy-start | bytes 786436
  6.5 22.3 %copy-start.62 = (f32[256]{0:T(256)S(1)}, f32[256]{0:T(256)}, u32[]{:S(2)}) copy-start(f32[256]{0:T(256)} %constant.252.clone) | copy-start | bytes 3076
  10.4 8.8 %copy-start.34 = (f32[13,1024]{1,0:T(8,128)}, f32[13,1024]{1,0:T(8,128)S(1)}, u32[]{:S(2)}) copy-start(f32[13,1024]{1,0:T(8,128)S(1)} %concatenate.84) | copy-start | bytes 159748
  19.1 24.1 %copy-start.16 = (f32[4,13,1024]{2,1,0:T(8,128)}, f32[4,13,1024]{2,1,0:T(8,128)S(1)}, u32[]{:S(2)}) copy-start(f32[4,13,1024]{2,1,0:T(8,128)S(1)} %all-gather.2) | copy-start | bytes 638980
  19.2 23.9 %collective-permute-start = (f32[4,13,1024]{2,0,1:T(4,128)S(1)}, f32[4,13,1024]{2,0,1:T(4,128)S(1)}, u32[]{:S(2)}, u32[]{:S(2)}) collective-permute-start(f32[4,13,1024]{2,0,1:T(4,128)S(1)} %copy.673), channel_id=1, source_target_pairs={{0,1},{1,2},{2,3},{3,4},{4,5},{5,6},{6,7},{7,8},{8,9},{9,10},{10,1... | collective-permute-start | bytes 638984 | tf_op jit(solution)/shard_map/ppermute | solution.py:26
  22.1 21.4 %copy-start.17 = (f32[64,8,256]{2,0,1:T(8,128)}, f32[64,8,256]{2,0,1:T(8,128)S(1)}, u32[]{:S(2)}) copy-start(f32[64,8,256]{2,0,1:T(8,128)S(1)} %copy.922) | copy-start | bytes 1572868
  23.0 9.5 %all-to-all-start.1 = ((f32[4,1,4096]{2,1,0:T(1,128)}), f32[4,1,4096]{2,1,0:T(1,128)S(1)}, u32[]{:S(2)}, u32[]{:S(2)}) async-start(f32[4,1,4096]{2,1,0:T(1,128)} %reshape.656), calls=%async_computation.1 | async-start | bytes 131072 | tf_op jit(solution)/shard_map/all_to_all | solution.py:236
  28.0 15.8 %copy-start.76 = (f32[1,256]{1,0:T(1,128)S(1)}, f32[1,256]{1,0:T(1,128)}, u32[]{:S(2)}) copy-start(f32[1,256]{1,0:T(1,128)} %constant.269) | copy-start | bytes 3076
  34.8 82.6 %all-to-all-start.2 = ((f32[32,2,256]{2,1,0:T(2,128)}), f32[32,2,256]{2,1,0:T(2,128)}, u32[]{:S(2)}, u32[]{:S(2)}) async-start(f32[32,2,256]{2,1,0:T(2,128)} %reshape.607), calls=%async_computation.2 | async-start | bytes 131072 | tf_op jit(solution)/shard_map/all_to_all | solution.py:237
  64.2 5.9 copy-start
  80.7 5.9 copy-start.57
  86.5 12.7 %copy-start.37 = (f32[32,2]{1,0:T(8,128)S(1)}, f32[32,2]{1,0:T(8,128)}, u32[]{:S(2)}) copy-start(f32[32,2]{1,0:T(8,128)} %mul.946) | copy-start | bytes 772
  100.7 9.0 %copy-start.48 = (f32[256]{0:T(256)S(1)}, f32[256]{0:T(256)}, u32[]{:S(2)}) copy-start(f32[256]{0:T(256)} %constant.250.clone) | copy-start | bytes 3076
  100.7 9.0 %copy-start.59 = (f32[32]{0:T(128)S(1)}, f32[32]{0:T(128)}, u32[]{:S(2)}) copy-start(f32[32]{0:T(128)} %fusion.271) | copy-start | bytes 388
  105.7 4.9 copy-start.53
  117.4 44.1 %copy-start.45 = (f32[3,1024]{1,0:T(4,128)S(1)}, f32[3,1024]{1,0:T(4,128)}, u32[]{:S(2)}) copy-start(f32[3,1024]{1,0:T(4,128)} %param.19) | copy-start | bytes 36868
  117.4 74.8 %all-to-all-start = ((f32[32,8,1152]{2,1,0:T(8,128)}), f32[32,8,1152]{2,1,0:T(8,128)}, u32[]{:S(2)}, u32[]{:S(2)}) async-start(f32[32,8,1152]{2,1,0:T(8,128)} %copy.707), calls=%async_computation | async-start | bytes 2359296 | tf_op jit(solution)/shard_map/all_to_all | solution.py:363
  125.3 52.2 %collective-permute-start.1 = (f32[13,1024]{1,0:T(8,128)}, f32[13,1024]{1,0:T(8,128)}, u32[]{:S(2)}, u32[]{:S(2)}) collective-permute-start(f32[13,1024]{1,0:T(8,128)} %copy-done.34), channel_id=1, source_target_pairs={{0,31},{1,0},{2,1},{3,2},{4,3},{5,4},{6,5},{7,6},{8,7},{9,8},{10,9... | collective-permute-start | bytes 159752 | tf_op jit(solution)/shard_map/ppermute | solution.py:26
  184.7 10.5 %copy-start.49 = (f32[256]{0:T(256)S(1)}, f32[256]{0:T(256)}, u32[]{:S(2)}) copy-start(f32[256]{0:T(256)} %constant.250.clone) | copy-start | bytes 3076
  184.7 10.5 %copy-start.54 = (f32[256]{0:T(256)S(1)}, f32[256]{0:T(256)}, u32[]{:S(2)}) copy-start(f32[256]{0:T(256)} %constant.251.clone) | copy-start | bytes 3076
  184.7 10.5 %copy-start.67 = (f32[256]{0:T(256)S(1)}, f32[256]{0:T(256)}, u32[]{:S(2)}) copy-start(f32[256]{0:T(256)} %constant.253.clone) | copy-start | bytes 3076
  195.3 3.8 copy-start.19
  195.3 3.8 copy-start.63
  195.3 3.8 copy-start.65
  195.4 3.8 copy-start.69
  196.7 3.6 copy-start.27
  211.7 22.9 %all-to-all-start.3 = ((f32[32,8,1152]{2,1,0:T(8,128)}), f32[32,8,1152]{2,1,0:T(8,128)}, u32[]{:S(2)}, u32[]{:S(2)}) async-start(f32[32,8,1152]{2,1,0:T(8,128)} %bitcast.463), calls=%async_computation.3 | async-start | bytes 2359296 | tf_op jit(solution)/shard_map/all_to_all | solution.py:430
  216.4 128.0 %reduce-scatter.3.cloned.1.call-start = ((), (), s32[]{:S(2)}) async-start(), calls=%async_computation.8 | async-start | bytes 2621440 | tf_op jit(solution)/shard_map/reduce_scatter | solution.py:474
  309.3 52.9 %copy-start.46 = (f32[1024]{0:T(1024)S(1)}, f32[1024]{0:T(1024)}, u32[]{:S(2)}) copy-start(f32[1024]{0:T(1024)} %param.22) | copy-start | bytes 12292
  346.4 15.7 %collective-permute-start.2 = (f32[3,1024]{0,1:T(8,128)}, f32[3,1024]{0,1:T(8,128)}, u32[]{:S(2)}, u32[]{:S(2)}) collective-permute-start(f32[3,1024]{0,1:T(8,128)} %slice_bitcast_fusion.5), channel_id=1, source_target_pairs={{0,31},{1,0},{2,1},{3,2},{4,3},{5,4},{6,5},{7,6},{8,7},{9,8},{10,9... | collective-permute-start | bytes 36872 | tf_op jit(solution)/shard_map/ppermute | solution.py:26
  365.9 21.0 %copy-start.39 = (f32[1,3,1024]{2,1,0:T(4,128)}, f32[1,3,1024]{2,1,0:T(4,128)S(1)}, u32[]{:S(2)}) copy-start(f32[1,3,1024]{2,1,0:T(4,128)S(1)} %copy.742) | copy-start | bytes 36868
  374.1 9.0 %copy-start.29 = (f32[4,3,1024]{2,1,0:T(4,128)}, f32[4,3,1024]{2,1,0:T(4,128)S(1)}, u32[]{:S(2)}) copy-start(f32[4,3,1024]{2,1,0:T(4,128)S(1)} %all-gather.3) | copy-start | bytes 147460
  374.1 8.9 %collective-permute-start.3 = (f32[4,3,1024]{2,0,1:T(4,128)S(1)}, f32[4,3,1024]{2,0,1:T(4,128)S(1)}, u32[]{:S(2)}, u32[]{:S(2)}) collective-permute-start(f32[4,3,1024]{2,0,1:T(4,128)S(1)} %copy.741), channel_id=1, source_target_pairs={{0,1},{1,2},{2,3},{3,4},{4,5},{5,6},{6,7},{7,8},{8,9},{9,10},{10,1... | collective-permute-start | bytes 147464 | tf_op jit(solution)/shard_map/ppermute | solution.py:26
  386.9 6.8 %slice-start = ((s8[9437184]{0:T(1024)(128)(4,1)}), s8[4194304]{0:T(1024)(128)(4,1)S(1)}, s32[]{:S(2)}) async-start(s8[9437184]{0:T(1024)(128)(4,1)} %bitcast.440), calls=%async_computation.10 | async-start | bytes 8388608
  386.9 6.8 %slice-start.1 = ((s8[9437184]{0:T(1024)(128)(4,1)}), s8[4194304]{0:T(1024)(128)(4,1)S(1)}, s32[]{:S(2)}) async-start(s8[9437184]{0:T(1024)(128)(4,1)} %bitcast.440), calls=%async_computation.11 | async-start | bytes 8388608
  410.1 5.7 copy-start.58
  417.8 12.2 %copy-start.38 = (f32[32,2]{1,0:T(8,128)S(1)}, f32[32,2]{1,0:T(8,128)}, u32[]{:S(2)}) copy-start(f32[32,2]{1,0:T(8,128)} %mul.946) | copy-start | bytes 772
  442.1 23.5 %copy-start.10 = (f32[512,256]{1,0:T(8,128)S(1)}, f32[512,256]{1,0:T(8,128)}, u32[]{:S(2)}) copy-start(f32[512,256]{1,0:T(8,128)} %constant.267) | copy-start | bytes 1572868
  479.1 13.0 %copy-start.40 = (f32[1,3,1024]{2,1,0:T(4,128)S(1)}, f32[1,3,1024]{2,1,0:T(4,128)}, u32[]{:S(2)}) copy-start(f32[1,3,1024]{2,1,0:T(4,128)} %copy-done.39) | copy-start | bytes 36868
  481.6 34.0 %all-to-all-start.5 = ((f32[32,8,1152]{2,1,0:T(8,128)}), f32[32,8,1152]{2,1,0:T(8,128)}, u32[]{:S(2)}, u32[]{:S(2)}) async-start(f32[32,8,1152]{2,1,0:T(8,128)} %bitcast.464), calls=%async_computation.6 | async-start | bytes 2359296 | tf_op jit(solution)/shard_map/all_to_all | solution.py:430
  486.3 142.2 %reduce-scatter.5.cloned.1.call-start = ((), (), s32[]{:S(2)}) async-start(), calls=%async_computation.9 | async-start | bytes 2621440 | tf_op jit(solution)/shard_map/reduce_scatter | solution.py:474
  486.4 24.7 %collective-permute-start.4 = (f32[3,1024]{0,1:T(8,128)}, f32[3,1024]{0,1:T(8,128)}, u32[]{:S(2)}, u32[]{:S(2)}) collective-permute-start(f32[3,1024]{0,1:T(8,128)} %fusion.89), channel_id=1, source_target_pairs={{0,31},{1,0},{2,1},{3,2},{4,3},{5,4},{6,5},{7,6},{8,7},{9,8},{10,9... | collective-permute-start | bytes 36872 | tf_op jit(solution)/shard_map/ppermute | solution.py:26
  518.9 22.4 %copy-start.52 = (f32[256]{0:T(256)S(1)}, f32[256]{0:T(256)}, u32[]{:S(2)}) copy-start(f32[256]{0:T(256)} %constant.250.clone) | copy-start | bytes 3076
  589.0 56.3 %copy-start.11 = (f32[3,1024]{0,1:T(8,128)S(1)}, f32[3,1024]{0,1:T(8,128)}, u32[]{:S(2)}) copy-start(f32[3,1024]{0,1:T(8,128)} %copy.746) | copy-start | bytes 36868
  589.1 56.3 %copy-start.47 = (f32[1024]{0:T(1024)S(1)}, f32[1024]{0:T(1024)}, u32[]{:S(2)}) copy-start(f32[1024]{0:T(1024)} %param.22) | copy-start | bytes 12292
  628.5 16.8 %copy-start.18 = (f32[1,6,1024]{1,2,0:T(8,128)S(1)}, f32[1,6,1024]{1,2,0:T(8,128)}, u32[]{:S(2)}) copy-start(f32[1,6,1024]{1,2,0:T(8,128)} %reduce-scatter.5.cloned.1.call-done) | copy-start | bytes 73732
  629.8 15.5 %collective-permute-start.5 = (f32[3,1024]{0,1:T(8,128)S(1)}, f32[3,1024]{0,1:T(8,128)S(1)}, u32[]{:S(2)}, u32[]{:S(2)}) collective-permute-start(f32[3,1024]{0,1:T(8,128)S(1)} %slice_bitcast_fusion.2), channel_id=1, source_target_pairs={{0,31},{1,0},{2,1},{3,2},{4,3},{5,4},{6,5},{7,6},{8,7},{9,8},{10,9... | collective-permute-start | bytes 36872 | tf_op jit(solution)/shard_map/ppermute | solution.py:26
  (45 other events, 90.4 us)
Sparse Core Ops, SparseCore 0:
  309.4 34.9 reduce-scatter.2
  588.4 40.1 reduce-scatter.4

commit v2 on v1

v2 whole, which is shorter than its diff:
```python
import functools
import math

import jax
import jax.numpy as jnp
import numpy as np
from jax import lax
from jax.experimental import pallas as pl
from jax.experimental.pallas import tpu as pltpu
from jax.sharding import PartitionSpec as P

G = 256
ITERS = 2

damping = 1.0
recip_scale = 16.0
highest = lax.Precision.HIGHEST
LANES = 128
TILES = 4 * G // LANES + 1
MESH = pl.DeviceIdType.MESH


def spline_weights(fraction):
    square = fraction * fraction
    cube = square * fraction
    rest = 1.0 - fraction
    return [
        rest * rest * rest / 6.0,
        (3.0 * cube - 6.0 * square + 4.0) / 6.0,
        (-3.0 * cube + 3.0 * square + 3.0 * fraction + 1.0) / 6.0,
        cube / 6.0,
    ]


def pair_kernel(cell_count, width, list_ref, count_ref, ghost_ref, table_ref, near_ref, out_ref):
    lane = lax.broadcasted_iota(jnp.int32, (8, 2 * width), 1)
    row = lax.broadcasted_iota(jnp.int32, (8, 2 * width), 0)
    first_half = lane < width
    is_moment = row >= 3
    itself = lax.broadcasted_iota(jnp.int32, (width, 2 * width), 0) == lax.broadcasted_iota(
        jnp.int32, (width, 2 * width), 1
    )

    ghosts = ghost_ref.shape[1]

    def place(entry):
        ghost = jnp.maximum(entry - cell_count, 0)
        source = lax.div(ghost, ghosts)
        there = cell_count * (1 + source) + ghost_ref[source, lax.rem(ghost, ghosts)]
        return jnp.where(entry < cell_count, entry, there)

    def one_cell(cell, _):
        base = pl.multiple_of(cell * width, width)
        near = near_ref[pl.ds(base, width), :]
        near_x = jnp.broadcast_to(near[:, 0:1], (width, 2 * width))
        near_y = jnp.broadcast_to(near[:, 1:2], (width, 2 * width))
        near_z = jnp.broadcast_to(near[:, 2:3], (width, 2 * width))
        count = count_ref[cell]

        def terms(pair, masked):
            one = table_ref[place(list_ref[cell, 2 * pair])]
            two = table_ref[place(list_ref[cell, 2 * pair + 1])]
            live = 2 * pair + 1 < count
            two = jnp.where(jnp.logical_and(is_moment, jnp.logical_not(live)), 0.0, two)
            far = jnp.where(first_half, one, two)
            dx = near_x - far[0:1]
            dy = near_y - far[1:2]
            dz = near_z - far[2:3]
            mx, my, mz = far[3:4], far[4:5], far[5:6]
            softened = dx * dx + dy * dy + dz * dz + damping
            inverse = lax.rsqrt(softened)
            square = inverse * inverse
            cube = square * inverse
            if masked:
                cube = jnp.where(itself, 0.0, cube)
            radial = (3.0 * (dx * mx + dy * my + dz * mz)) * (cube * square)
            return radial * dx - cube * mx, radial * dy - cube * my, radial * dz - cube * mz

        def step(pair, totals):
            return tuple(t + a for t, a in zip(totals, terms(pair, False)))

        totals = lax.fori_loop(1, (count + 1) // 2, step, terms(0, True))
        sums = [jnp.sum(t, axis=1, keepdims=True) for t in totals]
        column = lax.broadcasted_iota(jnp.int32, (width, 8), 1)
        out = jnp.where(column == 0, sums[0], jnp.where(column == 1, sums[1], sums[2]))
        out_ref[pl.ds(base, width), :] = out
        return 0

    lax.fori_loop(0, cell_count, one_cell, 0)


def pair_field(lists, counts, ghosts, table, near):
    cell_count = counts.shape[0]
    width = near.shape[0] // cell_count
    vmem = pl.BlockSpec(memory_space=pltpu.VMEM)
    smem = pl.BlockSpec(memory_space=pltpu.SMEM)
    pairs = cell_count * lists.shape[1] * width * width // 2
    return pl.pallas_call(
        functools.partial(pair_kernel, cell_count, width),
        out_shape=jax.ShapeDtypeStruct((near.shape[0], 8), jnp.float32),
        in_specs=[smem, smem, smem, vmem, vmem],
        out_specs=vmem,
        cost_estimate=pl.CostEstimate(flops=40 * pairs, bytes_accessed=1 << 20, transcendentals=pairs),
        name="pair_field",
    )(lists, counts, ghosts, table, near)


def split(x):
    top = x.astype(jnp.bfloat16)
    return top, (x - top.astype(jnp.float32)).astype(jnp.bfloat16)


def dot3(a, b, turned=False):
    dims = (((1,), (1 if turned else 0,)), ((), ()))

    def one(x, y):
        return lax.dot_general(x, y, dims, preferred_element_type=jnp.float32)

    return one(a[0], b[0]) + (one(a[1], b[0]) + one(a[0], b[1]))


def parts_of(table):
    table = np.asarray(table, np.float32)
    top = table.astype(jnp.bfloat16)
    low = (table - top.astype(np.float32)).astype(jnp.bfloat16)
    return jnp.asarray(top), jnp.asarray(low)


def lanes_of(shape):
    return lax.broadcasted_iota(jnp.int32, shape, len(shape) - 1)


def rows_of(shape):
    return lax.broadcasted_iota(jnp.int32, shape, len(shape) - 2)


def tables_of(packet_ref, block, phase, tx_ref, ty_ref, zh_ref):
    packet = packet_ref[block]

    def table(axis, length, wrapped):
        start = packet[9 + axis : 10 + axis].astype(jnp.int32)
        offset = rows_of((length, packet.shape[1])) - start
        if wrapped:
            offset = jnp.where(offset < 0, offset + length, offset)
        total = jnp.zeros(offset.shape, jnp.float32)
        for stencil, weight in enumerate(spline_weights(packet[6 + axis : 7 + axis])):
            total = jnp.where(offset == stencil, weight, total)
        return total

    tx_ref[block] = table(0, tx_ref.shape[1], False)
    ty_ref[block] = table(1, ty_ref.shape[1], False)
    zh_ref[block] = dot3(phase, split(table(2, G, True)))


def frequency_rows(kind):
    k = lanes_of((1, G))
    signed = jnp.where(k < G // 2, k, k - G).astype(jnp.float32)
    if kind == "odd":
        return jnp.where(k == G // 2, 0.0, signed)
    if kind == "even":
        return jnp.where(k == G // 2, signed, 0.0)
    return signed


def frequency_columns(kind):
    k = lax.broadcasted_iota(jnp.int32, (G, 1), 0)
    signed = jnp.where(k < G // 2, k, k - G).astype(jnp.float32)
    if kind == "odd":
        return jnp.where(k == G // 2, 0.0, signed)
    if kind == "even":
        return jnp.where(k == G // 2, signed, 0.0)
    return signed


def spread_kernel(
    slabs, subs, slab_ref, mom_ref, tx_ref, ty_ref, zh_ref, wt_ref, wl_ref, sel_ref, out_ref, grid_ref, mid_ref
):
    slab = slab_ref[0]
    grid_y = G // subs
    grid_x = G // slabs
    pad_x = grid_x + 8
    half = G // 2
    grid_ref[...] = jnp.zeros_like(grid_ref)

    def one(block, _):
        for part in range(2):
            mu = mom_ref[part * slabs + block]
            zh = zh_ref[part * slabs + block]
            tx = tx_ref[part * slabs + block][:pad_x]
            ty = ty_ref[part * slabs + block]
            values = jnp.concatenate(
                [zh[: 2 * subs] * mu[c : c + 1] for c in range(3)] + [mu[:8] * zh[2 * subs : 2 * subs + 1]],
                axis=0,
            )
            first, count = (0, grid_y) if part == 0 else (grid_y, 3)
            plane = jnp.concatenate([tx * ty[first + y : first + y + 1] for y in range(count)], axis=0)
            got = dot3(split(plane), split(values), True)
            columns = values.shape[0]
            for y in range(count):
                where = pl.ds(pl.multiple_of(block * grid_x, grid_x), pad_x)
                grid_ref[y, where, :columns] += got[y * pad_x : (y + 1) * pad_x]
        return 0

    lax.fori_loop(0, slabs, one, 0)
    rows = []
    for y in range(grid_y):
        grid_ref[y, :8] += grid_ref[y, G : G + 8]
        turned = grid_ref[y, :G].T
        for c in range(3):
            base = 2 * subs * c
            rows.append(
                jnp.concatenate([turned[base : base + subs], turned[base + subs : base + 2 * subs]], axis=1)
            )
        mids = turned[6 * subs : 6 * subs + 8]
        rows.append(jnp.concatenate([mids, jnp.zeros_like(mids)], axis=1))
    spec = dot3(split(jnp.concatenate(rows, axis=0)), (wt_ref[...], wl_ref[...]))
    odd, signed = frequency_rows("odd"), frequency_rows("signed")
    kz = (slabs * lax.broadcasted_iota(jnp.int32, (subs, 1), 0) + slab).astype(jnp.float32)
    lane = lanes_of((subs, LANES))
    per_y = 3 * subs + 8
    for y in range(grid_y):
        at = spec[y * per_y : (y + 1) * per_y]
        re = [at[c * subs : (c + 1) * subs, :G] for c in range(3)]
        im = [at[c * subs : (c + 1) * subs, G:] for c in range(3)]
        edge = jnp.where(
            lane == 0,
            -float(half) * re[0][:, half : half + 1],
            jnp.where(lane == 1, -float(half) * im[0][:, half : half + 1], 0.0),
        )
        full = [odd * re[0] + kz * re[2], odd * im[0] + kz * im[2], re[1], im[1]]
        tiles = [v[:, t * LANES : (t + 1) * LANES] for v in full for t in range(G // LANES)]
        for t, value in enumerate([*tiles, edge]):
            out_ref[pl.ds(t * grid_y + y, subs, stride=TILES * grid_y), :] = value
        mid = at[3 * subs :]
        for part, shift in ((0, 0), (1, G)):
            mx, my, mz = (mid[c : c + 1, shift : shift + G] for c in range(3))
            mid_ref[part, y : y + 1] = signed * mx - float(half) * mz
            mid_ref[2 + part, y : y + 1] = my
    window = pl.ds(pl.multiple_of(slab // 2 * LANES, LANES), LANES)
    pair = (lanes_of((grid_y, LANES)) - lax.rem(slab, 2) * (2 * subs)) >> 1
    columns = []
    for q in range(4):
        value = mid_ref[q, :, window]
        columns.append(jnp.concatenate([jnp.where(pair == j, value, 0.0) for j in range(subs)], axis=0))
    top, low = split(jnp.concatenate(columns, axis=1))
    sel = sel_ref[...]
    more = jnp.dot(top, sel, preferred_element_type=jnp.float32) + jnp.dot(
        low, sel, preferred_element_type=jnp.float32
    )
    for j in range(subs):
        where = pl.ds((j * TILES + TILES - 1) * grid_y, grid_y)
        out_ref[where, :] += more[j * grid_y : (j + 1) * grid_y]


def from_tiles(ref):
    blocks, rows, lanes = ref.shape
    high = rows // TILES
    return jnp.concatenate(
        [ref[:, t * high : (t + 1) * high, :].reshape(blocks * high, lanes) for t in range(TILES)], axis=1
    )


def swapped(x):
    last = x[:, 4 * G :]
    lane = lanes_of(last.shape)
    back = pltpu.roll(last, LANES - 1, 1)
    on = pltpu.roll(last, 1, 1)
    back2 = pltpu.roll(last, LANES - 2, 1)
    on2 = pltpu.roll(last, 2, 1)
    upper = ((lane - 2) & 2) == 0
    last = jnp.where(lane == 0, back, jnp.where(lane == 1, -on, jnp.where(upper, back2, -on2)))
    return jnp.concatenate(
        [x[:, G : 2 * G], -x[:, :G], x[:, 3 * G : 4 * G], -x[:, 2 * G : 3 * G], last], axis=1
    )


def middle_kernel(got_ref, even_ref, odd_ref, mid_ref, ft_ref, fl_ref, bt_ref, bl_ref, out_ref):
    half = G // 2

    def both(x):
        return split(jnp.concatenate([x, swapped(x)], axis=0))

    y = dot3((ft_ref[...], fl_ref[...]), both(from_tiles(got_ref)))
    last = y[:, 4 * G :]
    lane = lanes_of(last.shape)
    at_half = (lanes_of((1, G)) == half).astype(jnp.float32)
    odd_y, even_y, full_y = (frequency_columns(k) for k in ("odd", "even", "signed"))
    kernel_even, kernel_odd = even_ref[...], odd_ref[...]
    blocks, columns = [None] * 4, []
    for part in range(2):
        a = y[:, part * G : (part + 1) * G]
        b = y[:, (2 + part) * G : (3 + part) * G]
        level = a + odd_y * b
        edge = even_y * b + at_half * last[:, part : part + 1]
        phi = kernel_even * level + kernel_odd * edge
        phi_edge = kernel_odd * level + kernel_even * edge
        blocks[part] = phi
        blocks[2 + part] = odd_y * phi + even_y * phi_edge
        columns.append(phi_edge[:, half : half + 1])
    mid = mid_ref[...] * (last + full_y * pltpu.roll(last, LANES - 4, 1))
    mid = mid + full_y * pltpu.roll(mid, 4, 1)
    last = jnp.where(lane == 0, columns[0], jnp.where(lane == 1, columns[1], mid))
    back = dot3((bt_ref[...], bl_ref[...]), both(jnp.concatenate(blocks + [last], axis=1)))
    count, rows, lanes = out_ref.shape
    high = rows // TILES
    for t in range(TILES):
        out_ref[:, t * high : (t + 1) * high, :] = back[:, t * lanes : (t + 1) * lanes].reshape(
            count, high, lanes
        )


def sample_kernel(
    slabs,
    subs,
    slab_ref,
    got_ref,
    tx_ref,
    ty_ref,
    zh_ref,
    wt_ref,
    wl_ref,
    mt_ref,
    ml_ref,
    sel_ref,
    out_ref,
    field_ref,
    top_ref,
    low_ref,
):
    slab = slab_ref[0]
    grid_y = G // subs
    half = G // 2
    got = from_tiles(got_ref)
    last = got[:, 4 * G :]
    odd, even = frequency_rows("odd"), frequency_rows("even")
    kz = (slabs * (lax.broadcasted_iota(jnp.int32, (G, 1), 0) // grid_y) + slab).astype(jnp.float32)
    phi = [got[:, :G], got[:, G : 2 * G]]
    along_x = [odd * phi[part] + even * last[:, part : part + 1] for part in range(2)]
    lhs = jnp.concatenate(
        [
            jnp.concatenate(along_x, axis=1),
            got[:, 2 * G : 4 * G],
            jnp.concatenate([kz * phi[0], kz * phi[1]], axis=1),
        ],
        axis=0,
    )
    field = dot3(split(lhs), (wt_ref[...], wl_ref[...]))
    for t in range(2 * G // LANES):
        field_ref[pl.ds(t * 3 * G, 3 * G), :] = field[:, t * LANES : (t + 1) * LANES]
    sel = sel_ref[...]
    top, low = split(last)
    expanded = jnp.dot(top, sel, preferred_element_type=jnp.float32) + jnp.dot(
        low, sel, preferred_element_type=jnp.float32
    )
    pair = ((lanes_of((grid_y, 4 * LANES)) & (LANES - 1)) - lax.rem(slab, 2) * (2 * subs)) >> 1
    mids = jnp.zeros((grid_y, 4 * LANES), jnp.float32)
    for j in range(subs):
        mids = mids + jnp.where(pair == j, expanded[j * grid_y : (j + 1) * grid_y], 0.0)
    k = slab // 2 * LANES + (lanes_of((1, 2 * LANES)) & (LANES - 1))
    signed = jnp.where(k < half, k, k - G).astype(jnp.float32)
    mid_phi = mids[:, : 2 * LANES]
    mid_lhs = jnp.concatenate([signed * mid_phi, mids[:, 2 * LANES :], -float(half) * mid_phi], axis=0)
    mid_field = dot3(split(mid_lhs), (mt_ref[...], ml_ref[...]))
    row = rows_of((8, G))
    for y in range(grid_y):
        rows = []
        for c in range(3):
            for part in range(2):
                tiles = [
                    field_ref[pl.ds((part * G // LANES + t) * 3 * G + c * G + y, subs, stride=grid_y), :]
                    for t in range(G // LANES)
                ]
                rows.append(jnp.concatenate(tiles, axis=1))
        mid = jnp.zeros((8, G), jnp.float32)
        for c in range(3):
            mid = jnp.where(row == c, mid_field[c * grid_y + y : c * grid_y + y + 1], mid)
        here = jnp.concatenate(rows + [mid, jnp.zeros((8, G), jnp.float32)], axis=0)
        for turn in range(2):
            value = here if turn == 0 else pltpu.roll(here, G - G // slabs, 1)
            top_ref[turn, y], low_ref[turn, y] = split(value)

    def one(block, _):
        turn = lax.rem(block, 2)
        window = pl.ds(pl.multiple_of(block // 2 * LANES, LANES), LANES)
        for part in range(2):
            zh = zh_ref[part * slabs + block]
            tx = tx_ref[part * slabs + block]
            ty = ty_ref[part * slabs + block]
            first, count = (0, grid_y) if part == 0 else (grid_y, 3)
            a = tuple(
                jnp.concatenate([ref[turn, y, :, window] for y in range(count)], axis=1)
                for ref in (top_ref, low_ref)
            )
            tops, lows = [], []
            blank = jnp.zeros((LANES - tx.shape[0], tx.shape[1]), jnp.bfloat16)
            for y in range(count):
                top, low = split(tx * ty[first + y : first + y + 1])
                tops += [top, blank]
                lows += [low, blank]
            b = (jnp.concatenate(tops, axis=0), jnp.concatenate(lows, axis=0))
            mixed = dot3(a, b)
            fields = []
            for c in range(3):
                base = 2 * subs * c
                field = jnp.sum(mixed[base : base + 2 * subs] * zh[: 2 * subs], axis=0, keepdims=True)
                at = 6 * subs + c
                fields.append(field + mixed[at : at + 1] * zh[2 * subs : 2 * subs + 1])
            r = rows_of((8, tx.shape[1]))
            out_ref[part * slabs + block] = jnp.where(
                r == 0, fields[0], jnp.where(r == 1, fields[1], jnp.where(r == 2, fields[2], 0.0))
            )
        return 0

    lax.fori_loop(0, slabs, one, 0)


def around(slabs, subs):
    slab, sub = lax.axis_index("slab"), lax.axis_index("sub")
    up, down = lax.rem(sub + 1, subs), lax.rem(sub + subs - 1, subs)
    turns = [lax.rem(slab + k, slabs) for k in range(slabs)]
    return slab, sub, up, down, turns


def send_packet(slabs, subs, source_ref, all_ref, send_sem, recv_sem, first):
    slab, sub, up, down, turns = around(slabs, subs)
    goals = [(t, sub, slab) for t in turns[1:]]
    goals += [(t, up, slabs + slab) for t in turns]
    goals += [(slab, down, 2 * slabs)]
    copies = []
    for number, (to_slab, to_sub, slot) in enumerate(goals):
        copies.append(
            pltpu.make_async_remote_copy(
                src_ref=source_ref,
                dst_ref=all_ref.at[slot],
                send_sem=send_sem.at[first + number],
                recv_sem=recv_sem.at[slot],
                device_id=(to_slab, to_sub),
                device_id_type=MESH,
            )
        )
    return copies


def wait_packets(slabs, subs, all_ref, recv_sem):
    slab, sub, up, down, turns = around(slabs, subs)
    for slot in [*turns[1:], *(slabs + k for k in range(slabs)), 2 * slabs]:
        pltpu.make_async_copy(all_ref.at[slot], all_ref.at[slot], recv_sem.at[slot]).wait()


def greet(peers):
    barrier = pltpu.get_barrier_semaphore()
    for peer in peers:
        pl.semaphore_signal(barrier, inc=1, device_id=peer, device_id_type=MESH)
    pl.semaphore_wait(barrier, len(peers))


def all_peers(slabs, subs):
    slab, sub, up, down, turns = around(slabs, subs)
    return [(t, sub) for t in turns[1:]] + [(t, up) for t in turns] + [(t, down) for t in turns]


def start_kernel(
    slabs,
    subs,
    pol_ref,
    perm_ref,
    pos_ref,
    frac_ref,
    base_ref,
    lists_ref,
    top_ref,
    low_ref,
    influence_ref,
    all_ref,
    tx_ref,
    ty_ref,
    zh_ref,
    planes_ref,
    mids_ref,
    packet_ref,
    moved_ref,
    turned_ref,
    hop_ref,
    send_sem,
    recv_sem,
    move_sem,
    plane_send,
    plane_recv,
    hop_send,
    hop_recv,
    mid_send,
    mid_recv,
):
    slab, sub, up, down, turns = around(slabs, subs)
    depth, rows = moved_ref.shape[0], moved_ref.shape[1]
    half = slabs * subs
    middle = subs // 2
    group = 2 * subs

    moves = [pltpu.make_async_copy(influence_ref.at[:, i, :], moved_ref.at[i], move_sem.at[i]) for i in range(depth)]
    for move in moves:
        move.start()
    packet_ref[0:3] = pol_ref[...] * perm_ref[...]
    packet_ref[3:6] = pos_ref[...]
    packet_ref[6:9] = frac_ref[...]
    packet_ref[9:12] = base_ref[...].astype(jnp.float32)
    packet_ref[12:16] = jnp.zeros((4, packet_ref.shape[1]), jnp.float32)
    packet_ref[12:13, : lists_ref.shape[1]] = lists_ref[...].astype(jnp.float32)
    copies = send_packet(slabs, subs, packet_ref, all_ref, send_sem, recv_sem, 0)
    for copy in copies:
        copy.start()
    all_ref[slab] = packet_ref[...]

    def plane(i):
        kz = depth * sub + i
        upper = kz >= half
        folded = jnp.where(upper, lax.rem(2 * half - kz, half), kz)
        slot = jnp.where(upper, 1, 0)
        to_slab, to_sub = lax.rem(folded, slabs), lax.div(folded, slabs)
        target = planes_ref.at[slot, pl.ds(slab * rows, rows)]
        far = pltpu.make_async_remote_copy(
            src_ref=moved_ref.at[i],
            dst_ref=target,
            send_sem=plane_send.at[i],
            recv_sem=plane_recv.at[slot, slab],
            device_id=(to_slab, to_sub),
            device_id_type=MESH,
        )
        return far, slot, jnp.logical_and(to_slab == slab, to_sub == sub)

    def here(i, slot):
        return pltpu.make_async_copy(
            moved_ref.at[i], planes_ref.at[slot, pl.ds(slab * rows, rows)], plane_recv.at[slot, slab]
        )

    for i in range(depth):
        moves[i].wait()
        far, slot, mine = plane(i)

        @pl.when(mine)
        def _():
            here(i, slot).start()

        @pl.when(jnp.logical_not(mine))
        def _():
            far.start()

    first = moved_ref[0]
    turned_ref[...] = jnp.concatenate([first] + [first] * (LANES // rows - 1), axis=0).T

    def hop(number):
        return pltpu.make_async_remote_copy(
            src_ref=turned_ref.at[pl.ds(turns[number] * group, group)],
            dst_ref=hop_ref.at[slab],
            send_sem=hop_send.at[number - 1],
            recv_sem=hop_recv.at[slab],
            device_id=(turns[number], sub),
            device_id_type=MESH,
        )

    def mid(number):
        to_sub = lax.rem(middle + number, subs)
        return pltpu.make_async_remote_copy(
            src_ref=hop_ref.at[:, pl.ds(lax.div(to_sub, 4) * 8, 8)],
            dst_ref=mids_ref,
            send_sem=mid_send.at[number - 1],
            recv_sem=mid_recv,
            device_id=(slab, to_sub),
            device_id_type=MESH,
        )

    @pl.when(sub == middle)
    def _():
        for number in range(1, slabs):
            hop(number).start()
        hop_ref[slab] = turned_ref[pl.ds(pl.multiple_of(slab * group, group), group)]

    wait_packets(slabs, subs, all_ref, recv_sem)
    phase = (top_ref[...], low_ref[...])

    def one(block, _):
        tables_of(all_ref, block, phase, tx_ref, ty_ref, zh_ref)
        return 0

    lax.fori_loop(0, slabs, one, 0)

    @pl.when(sub == middle)
    def _():
        for t in turns[1:]:
            pltpu.make_async_copy(hop_ref.at[t], hop_ref.at[t], hop_recv.at[t]).wait()
        for number in range(1, subs):
            mid(number).start()
        mids_ref[...] = hop_ref[:, (middle // 4) * 8 : (middle // 4) * 8 + 8]

    lax.fori_loop(slabs, 2 * slabs, one, 0)

    @pl.when(sub == middle)
    def _():
        for number in range(1, slabs):
            hop(number).wait_send()
        for number in range(1, subs):
            mid(number).wait_send()

    @pl.when(sub != middle)
    def _():
        pltpu.make_async_copy(mids_ref, mids_ref, mid_recv).wait()

    for slot in range(2):
        for source in range(slabs):
            target = planes_ref.at[slot, pl.ds(source * rows, rows)]
            pltpu.make_async_copy(target, target, plane_recv.at[slot, source]).wait()
    for i in range(depth):
        far, slot, mine = plane(i)

        @pl.when(jnp.logical_not(mine))
        def _():
            far.wait_send()

    for copy in copies:
        copy.wait_send()


def update_kernel(slabs, subs, last, share_ref, rest_ref, pol_ref, *refs):
    if last:
        out_ref, land_ref, send_sem, land_sem = refs
    else:
        out_ref, all_ref, land_ref, send_sem, land_sem, recv_sem = refs
    slab, sub, up, down, turns = around(slabs, subs)
    greet(all_peers(slabs, subs))
    goals = [(t, sub, t, slab) for t in turns[1:]] + [(t, down, slabs + t, slabs + slab) for t in turns]
    copies = []
    for number, (to_slab, to_sub, source, slot) in enumerate(goals):
        copies.append(
            pltpu.make_async_remote_copy(
                src_ref=share_ref.at[source],
                dst_ref=land_ref.at[slot],
                send_sem=send_sem.at[number],
                recv_sem=land_sem.at[slot],
                device_id=(to_slab, to_sub),
                device_id_type=MESH,
            )
        )
    for copy in copies:
        copy.start()
    total = rest_ref[...] + share_ref[slab]
    for slot in [*turns[1:], *(slabs + k for k in range(slabs))]:
        pltpu.make_async_copy(land_ref.at[slot], land_ref.at[slot], land_sem.at[slot]).wait()
        total = total + land_ref[slot]
    moments = pol_ref[...] * total
    out_ref[...] = moments[: out_ref.shape[0]]
    if not last:
        more = send_packet(slabs, subs, out_ref, all_ref, send_sem, recv_sem, len(goals))
        for copy in more:
            copy.start()
        all_ref[slab] = moments
        wait_packets(slabs, subs, all_ref, recv_sem)
        copies += more
    for copy in copies:
        copy.wait_send()


def in_vmem(
    body, name, shapes, operands, scratch=(), smem_first=False, collective=None, anywhere=None, flops=0
):
    vmem = pl.BlockSpec(memory_space=pltpu.VMEM)
    smem = pl.BlockSpec(memory_space=pltpu.SMEM)
    params = dict(vmem_limit_bytes=56 << 20)
    if collective is not None:
        params.update(collective_id=collective, has_side_effects=True)
    if anywhere is not None:
        params.update(has_side_effects=True)
    specs = [smem if smem_first and n == 0 else vmem for n in range(len(operands))]
    if anywhere is not None:
        specs[anywhere] = pl.BlockSpec(memory_space=pl.ANY)
    out_shape = [jax.ShapeDtypeStruct(shape, jnp.float32) for shape in shapes]
    single = len(shapes) == 1
    return pl.pallas_call(
        body,
        out_shape=out_shape[0] if single else out_shape,
        in_specs=specs,
        out_specs=vmem if single else [vmem] * len(shapes),
        scratch_shapes=list(scratch),
        compiler_params=pltpu.CompilerParams(**params),
        cost_estimate=pl.CostEstimate(flops=flops, bytes_accessed=1 << 22, transcendentals=0),
        name=name,
    )(*operands)


def shards(
    positions,
    fraction,
    grid_base,
    polarizability,
    perm_field,
    influence,
    neighbour_cells,
    neighbour_count,
    send_cells,
):
    atoms = positions.shape[1]
    cells = neighbour_cells.shape[0]
    width = atoms // cells
    ghosts = send_cells.shape[2]
    slabs = lax.axis_size("slab")
    subs = lax.axis_size("sub")
    slab = lax.axis_index("slab")
    sub = lax.axis_index("sub")
    grid_x = G // slabs
    grid_y = G // subs
    half = G // 2

    index = np.arange(G)
    angle = (index[:, None] * index[None, :] % G) * (2.0 * np.pi / G)
    signed = np.where(index < half, index, index - G).astype(np.float32)

    kz_here = slabs * sub + slab

    slab_word = slab.astype(jnp.int32).reshape(1)
    kz_rows = np.arange(slabs)[:, None] + slabs * np.arange(subs)[None, :]
    turn = kz_rows[:, :, None] * index[None, None, :] % G * (2.0 * np.pi / G)
    phase = np.zeros((slabs, 2 * subs + 8, G), np.float32)
    phase[:, :subs] = np.cos(turn)
    phase[:, subs : 2 * subs] = -np.sin(turn)
    phase[:, 2 * subs] = np.where(index % 2 == 0, 1.0, -1.0)
    cos_np, sin_np = np.cos(angle), np.sin(angle)
    turn_x = parts_of(np.block([[cos_np, -sin_np], [sin_np, cos_np]]))
    back_x = parts_of(np.block([[cos_np, sin_np], [-sin_np, cos_np]]))
    turn_y = parts_of(np.concatenate([cos_np, sin_np], axis=1))
    back_y = parts_of(np.concatenate([cos_np, -sin_np], axis=1))
    wide = np.stack(
        [
            np.concatenate([cos_np[w : w + LANES], -sin_np[w : w + LANES]], axis=0)
            for w in (np.arange(slabs) // 2 * LANES)
        ]
    )

    def mine(pair):
        return tuple(lax.dynamic_index_in_dim(p, slab, 0, keepdims=False) for p in pair)

    phase, back_mid = mine(parts_of(phase)), mine(parts_of(wide))
    select = np.zeros((4, LANES, LANES), np.float32)
    for q in range(4):
        for lane in range(LANES):
            select[q, lane, 2 + 2 * q + lane % 2] = 1.0
    gather = jnp.asarray(select.reshape(4 * LANES, LANES), jnp.bfloat16)
    expand = jnp.asarray(np.concatenate(list(select.transpose(0, 2, 1)), axis=1), jnp.bfloat16)
    slots = 2 * slabs + 1
    ranks = 2 * subs + 8
    depth = G // subs
    dma = pltpu.SemaphoreType.DMA
    packets, tx, ty, zh, planes, mids = in_vmem(
        functools.partial(start_kernel, slabs, subs),
        "start",
        [
            (slots, 16, atoms),
            (2 * slabs, grid_x + 16, atoms),
            (2 * slabs, 16, atoms),
            (2 * slabs, ranks, atoms),
            (2, G, G),
            (slabs, 8, LANES),
        ],
        [
            polarizability[None, :],
            perm_field,
            positions,
            fraction,
            grid_base,
            send_cells.reshape(1, 4 * ghosts),
            *phase,
            influence,
        ],
        [
            pltpu.VMEM((16, atoms), jnp.float32),
            pltpu.VMEM((depth, grid_x, G), jnp.float32),
            pltpu.VMEM((G, LANES), jnp.float32),
            pltpu.VMEM((slabs, grid_x, LANES), jnp.float32),
            dma((2 * slabs,)),
            dma((slots,)),
            dma((depth,)),
            dma((depth,)),
            dma((2, slabs)),
            dma((slabs - 1,)),
            dma((slabs,)),
            dma((subs - 1,)),
            dma,
        ],
        anywhere=8,
        flops=1 << 31,
    )

    flip = jnp.asarray((index[:, None] == (-index[None, :]) % G).astype(np.float32))
    mirrored = jnp.dot(jnp.dot(flip, planes[1], precision=highest), flip, precision=highest)
    first = planes[0]
    sq = jnp.asarray(signed[:, None] ** 2 + signed[None, :] ** 2)
    kzf = kz_here.astype(jnp.float32)
    freq_sq = sq + kzf * kzf
    width_sq = G / 4.0 * (G / 4.0)
    gauss = jnp.where(
        freq_sq == 0.0,
        0.0,
        jnp.exp(-freq_sq / (2.0 * width_sq)) / jnp.where(freq_sq == 0.0, 1.0, freq_sq),
    ) * (-recip_scale / (float(G) ** 3))
    flat = kz_here == 0
    kernel_even = gauss * jnp.where(flat, first, first + mirrored)
    kernel_odd = gauss * jnp.where(flat, first, first - mirrored)
    mid = lax.dynamic_slice_in_dim(mids[:, :, :grid_x], lax.rem(2 * sub, 8), 2, 1)
    mid = jnp.transpose(mid, (1, 0, 2)).reshape(2, G)
    kx_mid = (2 * (subs * slab + sub) + jnp.arange(2, dtype=jnp.int32)).astype(jnp.float32)
    kx_mid = jnp.where(kx_mid < half, kx_mid, kx_mid - G)
    mid_sq = (kx_mid * kx_mid)[None, :] + jnp.asarray(signed[:, None] ** 2) + float(half * half)
    kernel_mid = (
        jnp.transpose(mid) * jnp.exp(-mid_sq / (2.0 * width_sq)) / mid_sq * (-recip_scale / (float(G) ** 3))
    )

    mid_tile = jnp.concatenate(
        [jnp.zeros((G, 2), jnp.float32), kernel_mid, kernel_mid, jnp.zeros((G, LANES - 6), jnp.float32)], axis=1
    )

    def near_of(blocks):
        own = [lax.dynamic_index_in_dim(blocks, k, 0, keepdims=False) for k in (
            slab,
            slabs + slab,
            2 * slabs,
            lax.rem(slab + slabs - 1, slabs),
            lax.rem(slab + 1, slabs),
        )]
        return jnp.stack(own)

    near = near_of(packets)

    ghost_lists = jnp.stack(
        [near[1 + q, 12, q * ghosts : (q + 1) * ghosts] for q in range(4)]
    ).astype(jnp.int32)
    near_atoms = jnp.pad(jnp.transpose(positions), ((0, 0), (0, 5)))

    def far_table(near_moments):
        rows = jnp.concatenate([near[:, 3:6], near_moments], axis=1)
        rows = jnp.transpose(rows.reshape(5, 6, cells, width), (0, 2, 1, 3)).reshape(5 * cells, 6, width)
        rows = jnp.pad(rows, ((0, 0), (0, 2), (0, 0)))
        return jnp.concatenate([rows, rows], axis=2)

    def reciprocal(block_moments):
        payload = in_vmem(
            functools.partial(spread_kernel, slabs, subs),
            "spread",
            [(subs * TILES * grid_y, LANES)],
            [slab_word, block_moments, tx, ty, zh, *turn_x, gather],
            [pltpu.VMEM((grid_y, G + 8, 256), jnp.float32), pltpu.VMEM((4, grid_y, G), jnp.float32)],
            smem_first=True,
            flops=1 << 33,
        ).reshape(subs, TILES * grid_y, LANES)
        got = lax.all_to_all(payload, "sub", split_axis=0, concat_axis=0, tiled=True)
        payload = in_vmem(
            middle_kernel,
            "second_frequency",
            [(subs, TILES * grid_y, LANES)],
            [got, kernel_even, kernel_odd, mid_tile, *turn_y, *back_y],
            flops=1 << 32,
        ).reshape(subs, TILES * grid_y, LANES)
        got = lax.all_to_all(payload, "sub", split_axis=0, concat_axis=0, tiled=True)
        columns = 6 * subs + 16
        return in_vmem(
            functools.partial(sample_kernel, slabs, subs),
            "sample",
            [(2 * slabs, 8, atoms)],
            [slab_word, got, tx, ty, zh, *back_x, *back_mid, expand],
            [
                pltpu.VMEM((6 * G * G // LANES, LANES), jnp.float32),
                pltpu.VMEM((2, grid_y, columns, G), jnp.bfloat16),
                pltpu.VMEM((2, grid_y, columns, G), jnp.bfloat16),
            ],
            smem_first=True,
            flops=1 << 33,
        )

    block_moments = packets
    near_moments = near[:, :3]
    pol = polarizability[None, :]
    for advance in range(ITERS):
        last = advance + 1 == ITERS
        pair = pair_field(neighbour_cells, neighbour_count, ghost_lists, far_table(near_moments), near_atoms)
        share = reciprocal(block_moments)
        rest = jnp.pad(perm_field + jnp.transpose(pair[:, :3]), ((0, 5), (0, 0)))
        scratch = [
            pltpu.VMEM((2 * slabs, 8, atoms), jnp.float32),
            pltpu.SemaphoreType.DMA((4 * slabs,)),
            pltpu.SemaphoreType.DMA((2 * slabs,)),
        ]
        if last:
            moments = in_vmem(
                functools.partial(update_kernel, slabs, subs, True),
                "last_update",
                [(3, atoms)],
                [share, rest, pol],
                scratch,
                collective=2,
            )
        else:
            moments, blocks = in_vmem(
                functools.partial(update_kernel, slabs, subs, False),
                "update",
                [(8, atoms), (slots, 8, atoms)],
                [share, rest, pol],
                scratch + [pltpu.SemaphoreType.DMA((slots,))],
                collective=3,
            )
            block_moments, near_moments = blocks, near_of(blocks)[:, :3]
    return moments


def solution(mesh):
    in_specs = (
        P(None, ("slab", "sub")),
        P(None, ("slab", "sub")),
        P(None, ("slab", "sub")),
        P(("slab", "sub")),
        P(None, ("slab", "sub")),
        P("slab", "sub", None),
        P(("slab", "sub"), None),
        P(("slab", "sub")),
        P(("slab", "sub"), None, None),
    )
    out_specs = P(None, ("slab", "sub"))
    return jax.shard_map(shards, mesh=mesh, in_specs=in_specs, out_specs=out_specs, check_vma=False)
```

time: 664 us -> 238 us (0.36); the launches traced: 655 us -> 237 us
  local copies, waits for them, and re-layouts: 238 us -> 15.2 us
  Pallas kernels: 38.5 us -> 153 us
  waiting for transfers between devices: 114 us -> 20.8 us
  matrix products: 75.4 us -> 3.98 us
  other arithmetic: 61.7 us -> 3.41 us
  starting transfers between devices: 53.8 us -> 16.1 us
  between operations: 35.3 us -> 0.37 us
  blocking collectives: 38.2 us -> 23.5 us
    pallas_call x1 -> x9, Pallas kernels: 24.7 us -> 141 us  [in_vmem(): pl.pallas_call(body, out_shape=out_shape[0] if single else out_shape, in_...]
    slice x59 -> x1, local copies, waits for them, and re-layouts: 90.6 us -> 0.01 us  [shards(): block_moments, near_moments = (blocks, near_of(blocks)[:, :3])]
    reduce_scatter x2 -> x0, waiting for transfers between devices: 73.6 us -> none  [shards(): share = lax.psum_scatter(share, 'slab', scatter_dimension=0)]
    dot_general x23 -> x0, matrix products: 71.9 us -> none  [the longest x2 15.7 us: reciprocal(): jnp.einsum('bga,bgr->bra', plane_own, wide.reshape(slabs, grid_y * pad_x,...]
    ppermute x6 -> x0, waiting for transfers between devices: 31.6 us -> none  [shifted(): return lax.ppermute(value, axis, pairs)]
    unnamed x184 -> x32, local copies, waits for them, and re-layouts: 32.9 us -> 7.25 us
    reshape x9 -> x1, local copies, waits for them, and re-layouts: 26.4 us -> 1.27 us  [shards(): send_cells.reshape(1, 4 * ghosts)]
    ppermute x6 -> x0, starting transfers between devices: 23.3 us -> none  [shifted(): return lax.ppermute(value, axis, pairs)]
  transfers between devices with their start and end apart: 13 -> 3, of which waited for: 8 -> 3; matrix products, arithmetic and copies ran while one was open for 18% -> 7% of each run, Pallas kernels for 6% -> 5%
where the time goes in v2:
time: 238 us; the launch traced here: 237 us
  Pallas kernels  153 us (64%)
  blocking collectives  23.5 us (10%)
  waiting for transfers between devices  20.8 us (9%)
  starting transfers between devices  16.1 us (7%)
  local copies, waits for them, and re-layouts  15.2 us (6%)
  matrix products  3.98 us (2%)
  other arithmetic  3.41 us (1%)
    pallas_call x9, Pallas kernels, in_vmem(): pl.pallas_call(body, out_shape=out_shape[0] if single else out_shape, in_...  141 us
    all_to_all x1, blocking collectives, reciprocal(): lax.all_to_all(payload, 'sub', split_axis=0, concat_axis=0, tiled=True)  23.5 us
    all_to_all x3, waiting for transfers between devices, reciprocal(): lax.all_to_all(payload, 'sub', split_axis=0, concat_axis=0, tiled=True)  20.8 us
    all_to_all x3, starting transfers between devices, reciprocal(): lax.all_to_all(payload, 'sub', split_axis=0, concat_axis=0, tiled=True)  16.1 us
    pallas_call x2, Pallas kernels, pair_field(): pl.pallas_call(functools.partial(pair_kernel, cell_count, width), out_sha...  12 us
    unnamed x32, local copies, waits for them, and re-layouts  7.25 us
  transfers between devices with their start and end apart: 3, of which 3 were waited for; matrix products, arithmetic and copies ran while one was open for 7% of the time, Pallas kernels for 5%

profile of v2, /device:TPU:1, one launch (start us, length us, event | category | flops | bytes accessed | tf_op | source)
XLA Modules:
  0.0 236.9 jit_solution(3665735846067192273)
XLA Ops:
  0.0 1.3 reshape.37.lists_ref
  1.3 1.4 dynamic-slice_bitcast_fusion.2
  2.7 41.8 %start.1 = (f32[9,16,1024]{2,1,0:T(8,128)}, f32[8,80,1024]{2,1,0:T(8,128)}, f32[8,16,1024]{2,1,0:T(8,128)}, f32[8,72,1024]{2,1,0:T(8,128)}, f32[2,256,256]{2,1,0:T(8,128)}, /*index=5*/f32[4,8,128]{2,1,0:T(8,128)}) custom-call(f32[1,1024]{1,0:T(1,128)} %bitcast.60, f32[3,1024]{1,0:T(4,128)} %perm_ref.1, f32[3,1024]{1,0:T(4,128)} %pos_ref.1, ...), custom_call_target="tpu_custom_call" | custom-call | flops 2147483648 | bytes 4194304 | tf_op jit(solution)/shard_map/start/pallas_call | solution.py:677
  44.5 12.6 %spread.2 = f32[2304,128]{1,0:T(8,128)} custom-call(s32[1]{0:T(128)} %bitcast.slab_ref, f32[9,16,1024]{2,1,0:T(8,128)} %get-tuple-element.12.mom_ref, f32[8,80,1024]{2,1,0:T(8,128)} %get-tuple-element.13.tx_ref, f32[8,16,1024]{2,1,0:T(8,128)} %get-tuple-element.14.ty_ref, f32[8,72,1024]{2,1,0:T(8,128)} %get-tuple-element.15.zh_ref, ...), custom_call_target="tpu_custom_call" | custom-call | flops 8589934592 | bytes 4194304 | tf_op jit(solution)/shard_map/spread/pallas_call | solution.py:677
  57.1 6.9 %all-to-all-start = ((f32[32,72,128]{2,1,0:T(8,128)}), f32[32,72,128]{2,1,0:T(8,128)S(1)}, u32[]{:S(2)}, u32[]{:S(2)}) async-start(f32[32,72,128]{2,1,0:T(8,128)} %bitcast.57), calls=%async_computation | async-start | bytes 2359296 | tf_op jit(solution)/shard_map/all_to_all | solution.py:852
  64.0 0.0 copy-start.8
  64.1 0.0 copy-start.3
  64.1 0.2 copy.36
  64.4 0.7 dynamic-slice_bitcast_fusion.4
  65.2 0.1 copy.33
  65.3 0.1 pad.38.clone
  65.4 0.1 fusion.11
  65.6 0.8 maximum_maximum_fusion.mid_ref
  66.4 1.5 fusion.7
  67.9 2.4 %fusion.3 = (f32[256,256]{1,0:T(8,128)}, f32[256,256]{1,0:T(8,128)}) fusion(f32[2,256,256]{2,1,0:T(8,128)} %get-tuple-element.16, pred[]{:T(512)S(6)} %eq.8, f32[256,256]{1,0:T(8,128)S(1)} %copy-done.9, f32[]{:T(128)S(6)} %mul.41, f32[256,256]{1,0:T(8,128)S(1)} %fusion.7, f32[256,256]{1,0:T(8,128)S(1)} %copy-done.3), kind=kOutput, calls=%fused_computation.10 | convolution fusion | flops 202244096 | bytes 1572869 | tf_op jit(solution)/shard_map/dot_general | solution.py:792
  70.4 9.9 %all-to-all-done.got_ref = f32[32,72,128]{2,1,0:T(8,128)S(1)} async-done(((f32[32,72,128]{2,1,0:T(8,128)}), f32[32,72,128]{2,1,0:T(8,128)S(1)}, u32[]{:S(2)}, u32[]{:S(2)}) %all-to-all-start) | async-done | bytes 1179680 | tf_op jit(solution)/shard_map/all_to_all | solution.py:852
  80.3 1.0 copy-done
  81.3 5.5 %second_frequency.2 = f32[32,72,128]{2,1,0:T(8,128)} custom-call(f32[32,72,128]{2,1,0:T(8,128)} %copy-done, f32[256,256]{1,0:T(8,128)} %get-tuple-element.20.even_ref, f32[256,256]{1,0:T(8,128)} %get-tuple-element.19.odd_ref, f32[256,128]{1,0:T(8,128)} %maximum_maximum_fusion.mid_ref, bf16[256,512]{1,0:T(8,128)(2,1)} %constant.136.clone.ft_ref, ...), custom_call_target="tpu_custom_call" | custom-call | flops 4294967296 | bytes 4194304 | tf_op jit(solution)/shard_map/second_frequency/pallas_call | solution.py:677
  86.8 4.7 %all-to-all-start.1 = ((f32[32,72,128]{2,1,0:T(8,128)}), f32[32,72,128]{2,1,0:T(8,128)S(1)}, u32[]{:S(2)}, u32[]{:S(2)}) async-start(f32[32,72,128]{2,1,0:T(8,128)} %second_frequency.2), calls=%async_computation.1 | async-start | bytes 2359296 | tf_op jit(solution)/shard_map/all_to_all | solution.py:860
  91.6 0.1 reshape.40
  91.7 0.1 copy.35
  91.8 0.9 pad.19.near_ref
  92.7 0.1 fusion.13
  92.8 0.6 maximum_convert_fusion.ghost_ref
  93.4 0.9 pad_maximum_fusion.table_ref
  94.3 6.0 %pair_field.2 = f32[1024,8]{1,0:T(8,128)} custom-call(s32[16,16]{1,0:T(8,128)} %list_ref.3, s32[16]{0:T(128)} %count_ref.3, s32[4,8]{1,0:T(4,128)} %maximum_convert_fusion.ghost_ref, f32[80,8,128]{2,1,0:T(8,128)} %pad_maximum_fusion.table_ref, f32[1024,8]{1,0:T(8,128)} %pad.19.near_ref), custom_call_target="tpu_custom_call" | custom-call | flops 20971520 | bytes 1048576 | tf_op jit(solution)/shard_map/pair_field/pallas_call | solution.py:98
  100.3 1.2 copy.40
  101.5 0.6 pad.20.rest_ref
  102.2 1.7 dynamic-slice_bitcast_fusion
  103.8 3.5 %all-to-all-done.1.got_ref = f32[32,72,128]{2,1,0:T(8,128)S(1)} async-done(((f32[32,72,128]{2,1,0:T(8,128)}), f32[32,72,128]{2,1,0:T(8,128)S(1)}, u32[]{:S(2)}, u32[]{:S(2)}) %all-to-all-start.1) | async-done | bytes 1179680 | tf_op jit(solution)/shard_map/all_to_all | solution.py:860
  107.4 1.1 copy-done.1
  108.4 14.7 %sample.2.share_ref = f32[8,8,1024]{2,1,0:T(8,128)} custom-call(s32[1]{0:T(128)} %bitcast.slab_ref, f32[32,72,128]{2,1,0:T(8,128)} %copy-done.1, f32[8,80,1024]{2,1,0:T(8,128)} %get-tuple-element.13.tx_ref, f32[8,16,1024]{2,1,0:T(8,128)} %get-tuple-element.14.ty_ref, f32[8,72,1024]{2,1,0:T(8,128)} %get-tuple-element.15.zh_ref, ...), custom_call_target="tpu_custom_call" | custom-call | flops 8589934592 | bytes 4194304 | tf_op jit(solution)/shard_map/sample/pallas_call | solution.py:677
  123.1 22.0 %update.1 = (f32[8,1024]{1,0:T(8,128)}, f32[9,8,1024]{2,1,0:T(8,128)}) custom-call(f32[8,8,1024]{2,1,0:T(8,128)} %sample.2.share_ref, f32[8,1024]{1,0:T(8,128)} %pad.20.rest_ref, f32[1,1024]{1,0:T(1,128)} %bitcast.61), custom_call_target="tpu_custom_call" | custom-call | bytes 4194304 | tf_op jit(solution)/shard_map/update/pallas_call | solution.py:677
  145.2 12.6 %spread.3 = f32[2304,128]{1,0:T(8,128)} custom-call(s32[1]{0:T(128)} %bitcast.slab_ref, f32[9,8,1024]{2,1,0:T(8,128)} %get-tuple-element.18.mom_ref, f32[8,80,1024]{2,1,0:T(8,128)} %get-tuple-element.13.tx_ref, f32[8,16,1024]{2,1,0:T(8,128)} %get-tuple-element.14.ty_ref, f32[8,72,1024]{2,1,0:T(8,128)} %get-tuple-element.15.zh_ref, ...), custom_call_target="tpu_custom_call" | custom-call | flops 8589934592 | bytes 4194304 | tf_op jit(solution)/shard_map/spread/pallas_call | solution.py:677
  157.7 23.5 %all_to_all.20.got_ref = f32[32,72,128]{2,1,0:T(8,128)} all-to-all(f32[32,72,128]{2,1,0:T(8,128)} %bitcast.58), channel_id=1, replica_groups=mesh['slab'=4,'sub'=32] {'sub'}, dimensions={0} | all-to-all | bytes 2359296 | tf_op jit(solution)/shard_map/all_to_all | solution.py:852
  181.3 5.5 %second_frequency.3 = f32[32,72,128]{2,1,0:T(8,128)} custom-call(f32[32,72,128]{2,1,0:T(8,128)} %all_to_all.20.got_ref, f32[256,256]{1,0:T(8,128)} %get-tuple-element.20.even_ref, f32[256,256]{1,0:T(8,128)} %get-tuple-element.19.odd_ref, f32[256,128]{1,0:T(8,128)} %maximum_maximum_fusion.mid_ref, bf16[256,512]{1,0:T(8,128)(2,1)} %constant.136.clone.ft_ref, ...), custom_call_target="tpu_custom_call" | custom-call | flops 4294967296 | bytes 4194304 | tf_op jit(solution)/shard_map/second_frequency/pallas_call | solution.py:677
  186.8 4.5 %all-to-all-start.3 = ((f32[32,72,128]{2,1,0:T(8,128)}), f32[32,72,128]{2,1,0:T(8,128)S(1)}, u32[]{:S(2)}, u32[]{:S(2)}) async-start(f32[32,72,128]{2,1,0:T(8,128)} %second_frequency.3), calls=%async_computation.3 | async-start | bytes 2359296 | tf_op jit(solution)/shard_map/all_to_all | solution.py:860
  191.5 0.1 reshape.43
  191.6 0.1 copy.38
  191.7 0.9 pad_maximum_fusion.1.table_ref
  192.6 6.0 %pair_field.3 = f32[1024,8]{1,0:T(8,128)} custom-call(s32[16,16]{1,0:T(8,128)} %list_ref.3, s32[16]{0:T(128)} %count_ref.3, s32[4,8]{1,0:T(4,128)} %maximum_convert_fusion.ghost_ref, f32[80,8,128]{2,1,0:T(8,128)} %pad_maximum_fusion.1.table_ref, f32[1024,8]{1,0:T(8,128)} %pad.19.near_ref), custom_call_target="tpu_custom_call" | custom-call | flops 20971520 | bytes 1048576 | tf_op jit(solution)/shard_map/pair_field/pallas_call | solution.py:98
  198.6 1.2 copy.41
  199.9 0.6 pad.22.rest_ref
  200.5 7.3 %all-to-all-done.3.got_ref = f32[32,72,128]{2,1,0:T(8,128)S(1)} async-done(((f32[32,72,128]{2,1,0:T(8,128)}), f32[32,72,128]{2,1,0:T(8,128)S(1)}, u32[]{:S(2)}, u32[]{:S(2)}) %all-to-all-start.3) | async-done | bytes 1179680 | tf_op jit(solution)/shard_map/all_to_all | solution.py:860
  207.8 1.1 copy-done.2
  208.9 14.7 %sample.3.share_ref = f32[8,8,1024]{2,1,0:T(8,128)} custom-call(s32[1]{0:T(128)} %bitcast.slab_ref, f32[32,72,128]{2,1,0:T(8,128)} %copy-done.2, f32[8,80,1024]{2,1,0:T(8,128)} %get-tuple-element.13.tx_ref, f32[8,16,1024]{2,1,0:T(8,128)} %get-tuple-element.14.ty_ref, f32[8,72,1024]{2,1,0:T(8,128)} %get-tuple-element.15.zh_ref, ...), custom_call_target="tpu_custom_call" | custom-call | flops 8589934592 | bytes 4194304 | tf_op jit(solution)/shard_map/sample/pallas_call | solution.py:677
  223.6 12.0 %last_update.1 = f32[3,1024]{1,0:T(4,128)} custom-call(f32[8,8,1024]{2,1,0:T(8,128)} %sample.3.share_ref, f32[8,1024]{1,0:T(8,128)} %pad.22.rest_ref, f32[1,1024]{1,0:T(1,128)} %bitcast.62), custom_call_target="tpu_custom_call" | custom-call | bytes 4194304 | tf_op jit(solution)/shard_map/last_update/pallas_call | solution.py:677
  235.6 1.3 copy.51
  (37 shorter events, 0.4 us)
Async XLA Ops:
  57.1 6.9 %copy-start.7 = (f32[3,1024]{1,0:T(4,128)S(1)}, f32[3,1024]{1,0:T(4,128)}, u32[]{:S(2)}) copy-start(f32[3,1024]{1,0:T(4,128)} %pos_ref.1) | copy-start | bytes 36868
  57.1 7.2 %copy-start.4 = (f32[9,16,1024]{2,1,0:T(8,128)S(1)}, f32[9,16,1024]{2,1,0:T(8,128)}, u32[]{:S(2)}) copy-start(f32[9,16,1024]{2,1,0:T(8,128)} %get-tuple-element.12.mom_ref) | copy-start | bytes 1769476
  57.1 23.2 %all-to-all-start = ((f32[32,72,128]{2,1,0:T(8,128)}), f32[32,72,128]{2,1,0:T(8,128)S(1)}, u32[]{:S(2)}, u32[]{:S(2)}) async-start(f32[32,72,128]{2,1,0:T(8,128)} %bitcast.57), calls=%async_computation | async-start | bytes 2359296 | tf_op jit(solution)/shard_map/all_to_all | solution.py:852
  64.0 1.4 copy-start.8
  64.1 2.3 copy-start.3
  64.3 3.6 %copy-start.9 = (f32[256,256]{1,0:T(8,128)S(1)}, f32[256,256]{1,0:T(8,128)}, u32[]{:S(2)}) copy-start(f32[256,256]{1,0:T(8,128)} %constant.147.clone) | copy-start | bytes 786436
  80.3 1.0 copy-start
  86.8 20.5 %all-to-all-start.1 = ((f32[32,72,128]{2,1,0:T(8,128)}), f32[32,72,128]{2,1,0:T(8,128)S(1)}, u32[]{:S(2)}, u32[]{:S(2)}) async-start(f32[32,72,128]{2,1,0:T(8,128)} %second_frequency.2), calls=%async_computation.1 | async-start | bytes 2359296 | tf_op jit(solution)/shard_map/all_to_all | solution.py:860
  93.4 8.1 %copy-start.6 = (f32[3,1024]{1,0:T(4,128)S(1)}, f32[3,1024]{1,0:T(4,128)}, u32[]{:S(2)}) copy-start(f32[3,1024]{1,0:T(4,128)} %perm_ref.1) | copy-start | bytes 36868
  107.4 1.1 copy-start.1
  186.8 4.6 %copy-start.5 = (f32[9,8,1024]{2,1,0:T(8,128)S(1)}, f32[9,8,1024]{2,1,0:T(8,128)}, u32[]{:S(2)}) copy-start(f32[9,8,1024]{2,1,0:T(8,128)} %get-tuple-element.18.mom_ref) | copy-start | bytes 884740
  186.8 21.0 %all-to-all-start.3 = ((f32[32,72,128]{2,1,0:T(8,128)}), f32[32,72,128]{2,1,0:T(8,128)S(1)}, u32[]{:S(2)}, u32[]{:S(2)}) async-start(f32[32,72,128]{2,1,0:T(8,128)} %second_frequency.3), calls=%async_computation.3 | async-start | bytes 2359296 | tf_op jit(solution)/shard_map/all_to_all | solution.py:860
  207.8 1.1 copy-start.2

commit v3 on v0

v3 whole, which is shorter than its diff:
```python
import functools
import math

import jax
import jax.numpy as jnp
import numpy as np
from jax import lax
from jax.experimental import pallas as pl
from jax.experimental.pallas import tpu as pltpu
from jax.sharding import PartitionSpec as P

G = 256
ITERS = 2

damping = 1.0
recip_scale = 16.0
highest = lax.Precision.HIGHEST
LANES = 128
TILES = 4 * G // LANES + 1
EXTRA = 2 * G // LANES
MESH = pl.DeviceIdType.MESH


def spline_weights(fraction):
    square = fraction * fraction
    cube = square * fraction
    rest = 1.0 - fraction
    return [
        rest * rest * rest / 6.0,
        (3.0 * cube - 6.0 * square + 4.0) / 6.0,
        (-3.0 * cube + 3.0 * square + 3.0 * fraction + 1.0) / 6.0,
        cube / 6.0,
    ]


def split(x):
    top = x.astype(jnp.bfloat16)
    return top, (x - top.astype(jnp.float32)).astype(jnp.bfloat16)


def dot3(a, b, turned=False):
    dims = (((1,), (1 if turned else 0,)), ((), ()))

    def one(x, y):
        return lax.dot_general(x, y, dims, preferred_element_type=jnp.float32)

    return one(a[0], b[0]) + (one(a[1], b[0]) + one(a[0], b[1]))


def parts_of(table):
    table = np.asarray(table, np.float32)
    top = table.astype(jnp.bfloat16)
    low = (table - top.astype(np.float32)).astype(jnp.bfloat16)
    return jnp.asarray(top), jnp.asarray(low)


def lanes_of(shape):
    return lax.broadcasted_iota(jnp.int32, shape, len(shape) - 1)


def rows_of(shape):
    return lax.broadcasted_iota(jnp.int32, shape, len(shape) - 2)


def window_of(slabs):
    return G // slabs + 8


def plane_rows(slabs, subs):
    window = window_of(slabs)
    return tuple(-(-count * window // LANES) * LANES for count in (G // subs, 3))


def tables_of(slabs, subs, still_ref, block, before, phase, top_ref, low_ref, zh_ref):
    at = block + slabs if before else block
    still = still_ref[at]
    atoms = still.shape[1]

    def table(axis, length, wrapped):
        start = still[3 + axis : 4 + axis].astype(jnp.int32)
        offset = rows_of((length, atoms)) - start
        if wrapped:
            offset = jnp.where(offset < 0, offset + length, offset)
        total = jnp.zeros(offset.shape, jnp.float32)
        for stencil, weight in enumerate(spline_weights(still[axis : 1 + axis])):
            total = jnp.where(offset == stencil, weight, total)
        return total

    along_x, along_y = table(0, window_of(slabs), False), table(1, 16, False)
    grid_y = G // subs
    first, count = (grid_y, 3) if before else (0, grid_y)
    own, spilt = plane_rows(slabs, subs)
    start, rows = (own, spilt) if before else (0, own)
    blank = jnp.zeros((rows - count * along_x.shape[0], atoms), jnp.float32)
    plane = [along_x * along_y[first + y : first + y + 1] for y in range(count)]
    top, low = split(jnp.concatenate([*plane, blank], axis=0))
    top_ref[block, start : start + rows] = top
    low_ref[block, start : start + rows] = low
    zh_ref[at] = dot3(phase, split(table(2, G, True)))


def frequency_rows(kind):
    k = lanes_of((1, G))
    signed = jnp.where(k < G // 2, k, k - G).astype(jnp.float32)
    if kind == "odd":
        return jnp.where(k == G // 2, 0.0, signed)
    if kind == "even":
        return jnp.where(k == G // 2, signed, 0.0)
    return signed


def frequency_columns(kind):
    k = lax.broadcasted_iota(jnp.int32, (G, 1), 0)
    signed = jnp.where(k < G // 2, k, k - G).astype(jnp.float32)
    if kind == "odd":
        return jnp.where(k == G // 2, 0.0, signed)
    if kind == "even":
        return jnp.where(k == G // 2, signed, 0.0)
    return signed


def density(slabs, subs, mom_ref, top_ref, low_ref, zh_ref, grid_ref):
    grid_y = G // subs
    grid_x = G // slabs
    window = window_of(slabs)
    own, _ = plane_rows(slabs, subs)
    grid_ref[...] = jnp.zeros_like(grid_ref)

    def one(block, _):
        for part in range(2):
            mu = mom_ref[part * slabs + block]
            zh = zh_ref[part * slabs + block]
            values = jnp.concatenate(
                [zh[: 2 * subs] * mu[c : c + 1] for c in range(3)] + [mu * zh[2 * subs : 2 * subs + 1]],
                axis=0,
            )
            start, count = (0, grid_y) if part == 0 else (own, 3)
            rows = -(-count * window // 16) * 16
            plane = tuple(ref[block, start : start + rows] for ref in (top_ref, low_ref))
            got = dot3(plane, split(values), True)
            columns = values.shape[0]
            for y in range(count):
                where = pl.ds(pl.multiple_of(block * grid_x, grid_x), window)
                grid_ref[y, where, :columns] += got[y * window : (y + 1) * window]
        return 0

    lax.fori_loop(0, slabs, one, 0)
    for y in range(grid_y):
        grid_ref[y, :8] += grid_ref[y, G : G + 8]


def first_frequency(slabs, subs, slab, grid_ref, wt_ref, wl_ref, sel_ref, out_ref, mid_ref, send_part):
    grid_y = G // subs
    half = G // 2
    flat_ref = out_ref.reshape(subs * TILES * grid_y, LANES)
    turned = [grid_ref[y, :G].T for y in range(grid_y)]
    weights = (wt_ref[...], wl_ref[...])

    def pair_rows(value, c):
        base = 2 * subs * c
        return jnp.concatenate([value[base : base + subs], value[base + subs : base + 2 * subs]], axis=1)

    def put(first, y, values):
        tiles = [v[:, t * LANES : (t + 1) * LANES] for v in values for t in range(v.shape[1] // LANES)]
        for t, value in enumerate(tiles):
            flat_ref[pl.ds((first + t) * grid_y + y, subs, stride=TILES * grid_y), :] = value

    spec = dot3(split(jnp.concatenate([pair_rows(v, 1) for v in turned], axis=0)), weights)
    for y in range(grid_y):
        put(EXTRA + 1, y, [spec[y * subs : (y + 1) * subs]])
    send_part(1)
    rows = []
    for v in turned:
        mids = v[6 * subs : 6 * subs + 8]
        rows += [pair_rows(v, 0), pair_rows(v, 2), jnp.concatenate([mids, jnp.zeros_like(mids)], axis=1)]
    spec = dot3(split(jnp.concatenate(rows, axis=0)), weights)
    odd, signed = frequency_rows("odd"), frequency_rows("signed")
    kz = (slabs * lax.broadcasted_iota(jnp.int32, (subs, 1), 0) + slab).astype(jnp.float32)
    lane = lanes_of((subs, LANES))
    per_y = 2 * subs + 8
    for y in range(grid_y):
        at = spec[y * per_y : (y + 1) * per_y]
        sx, sz, mid = at[:subs], at[subs : 2 * subs], at[2 * subs :]
        edge = jnp.where(
            lane == 0,
            -float(half) * sx[:, half : half + 1],
            jnp.where(lane == 1, -float(half) * sx[:, G + half : G + half + 1], 0.0),
        )
        put(0, y, [odd * sx[:, :G] + kz * sz[:, :G], odd * sx[:, G:] + kz * sz[:, G:], edge])
        for part, shift in ((0, 0), (1, G)):
            mx, my, mz = (mid[c : c + 1, shift : shift + G] for c in range(3))
            mid_ref[part, y : y + 1] = signed * mx - float(half) * mz
            mid_ref[2 + part, y : y + 1] = my
    window = pl.ds(pl.multiple_of(slab // 2 * LANES, LANES), LANES)
    pair = (lanes_of((grid_y, LANES)) - lax.rem(slab, 2) * (2 * subs)) >> 1
    columns = []
    for q in range(4):
        value = mid_ref[q, :, window]
        columns.append(jnp.concatenate([jnp.where(pair == j, value, 0.0) for j in range(subs)], axis=0))
    top, low = split(jnp.concatenate(columns, axis=1))
    sel = sel_ref[...]
    more = jnp.dot(top, sel, preferred_element_type=jnp.float32) + jnp.dot(
        low, sel, preferred_element_type=jnp.float32
    )
    out_ref[:, EXTRA * grid_y : (EXTRA + 1) * grid_y, :] += more.reshape(subs, grid_y, LANES)
    send_part(0)


def part_rows(part, high):
    return (0, (EXTRA + 1) * high) if part == 0 else ((EXTRA + 1) * high, EXTRA * high)


def from_tiles(ref, part):
    blocks, rows, lanes = ref.shape
    high = rows // TILES
    first, count = part_rows(part, high)
    return jnp.concatenate(
        [ref[:, r : r + high, :].reshape(blocks * high, lanes) for r in range(first, first + count, high)], axis=1
    )


def to_tiles(value, ref, part):
    blocks, rows, lanes = ref.shape
    high = rows // TILES
    first, count = part_rows(part, high)
    for t in range(count // high):
        ref[:, first + t * high : first + (t + 1) * high, :] = value[:, t * lanes : (t + 1) * lanes].reshape(
            blocks, high, lanes
        )


def with_swapped(x):
    top, low = split(x[:, : 2 * G])
    both = [
        jnp.concatenate([v, jnp.concatenate([v[:, G:], -v[:, :G]], axis=1)], axis=0) for v in (top, low)
    ]
    if x.shape[1] > 2 * G:
        last = x[:, 2 * G :]
        lane = lanes_of(last.shape)
        back, on = pltpu.roll(last, LANES - 1, 1), pltpu.roll(last, 1, 1)
        back2, on2 = pltpu.roll(last, LANES - 2, 1), pltpu.roll(last, 2, 1)
        upper = ((lane - 2) & 2) == 0
        turned = jnp.where(lane == 0, back, jnp.where(lane == 1, -on, jnp.where(upper, back2, -on2)))
        more = split(jnp.concatenate([last, turned], axis=0))
        both = [jnp.concatenate([a, b], axis=1) for a, b in zip(both, more)]
    return tuple(both)


def second(got_ref, even_ref, odd_ref, mid_ref, ft_ref, fl_ref, bt_ref, bl_ref, out_ref, wait_part, send_part):
    half = G // 2
    forward, backward = (ft_ref[...], fl_ref[...]), (bt_ref[...], bl_ref[...])
    wait_part(1)
    b_all = dot3(forward, with_swapped(from_tiles(got_ref, 1)))
    wait_part(0)
    a_all = dot3(forward, with_swapped(from_tiles(got_ref, 0)))
    last = a_all[:, 2 * G :]
    lane = lanes_of(last.shape)
    at_half = (lanes_of((1, G)) == half).astype(jnp.float32)
    odd_y, even_y, full_y = (frequency_columns(k) for k in ("odd", "even", "signed"))
    kernel_even, kernel_odd = even_ref[...], odd_ref[...]
    phis, along_y, columns = [], [], []
    for part in range(2):
        a = a_all[:, part * G : (part + 1) * G]
        b = b_all[:, part * G : (part + 1) * G]
        level = a + odd_y * b
        edge = even_y * b + at_half * last[:, part : part + 1]
        phi = kernel_even * level + kernel_odd * edge
        phi_edge = kernel_odd * level + kernel_even * edge
        phis.append(phi)
        along_y.append(odd_y * phi + even_y * phi_edge)
        columns.append(phi_edge[:, half : half + 1])
    mid = mid_ref[...] * (last + full_y * pltpu.roll(last, LANES - 4, 1))
    mid = mid + full_y * pltpu.roll(mid, 4, 1)
    last = jnp.where(lane == 0, columns[0], jnp.where(lane == 1, columns[1], mid))
    to_tiles(dot3(backward, with_swapped(jnp.concatenate([*phis, last], axis=1))), out_ref, 0)
    send_part(0)
    to_tiles(dot3(backward, with_swapped(jnp.concatenate(along_y, axis=1))), out_ref, 1)
    send_part(1)


def sample(
    slabs,
    subs,
    slab,
    got_ref,
    top_ref,
    low_ref,
    zh_ref,
    wt_ref,
    wl_ref,
    mt_ref,
    ml_ref,
    sel_ref,
    out_ref,
    field_ref,
    here_ref,
    lhs_t_ref,
    lhs_l_ref,
    wait_part,
):
    grid_y = G // subs
    grid_x = G // slabs
    half = G // 2
    window = window_of(slabs)
    own, spilt = plane_rows(slabs, subs)
    weights = (wt_ref[...], wl_ref[...])

    def put(component, value):
        for t in range(2 * G // LANES):
            field_ref[pl.ds((3 * t + component) * G, G), :] = value[:, t * LANES : (t + 1) * LANES]

    wait_part(0)
    got = from_tiles(got_ref, 0)
    last = got[:, 2 * G :]
    odd, even = frequency_rows("odd"), frequency_rows("even")
    kz = (slabs * (lax.broadcasted_iota(jnp.int32, (G, 1), 0) // grid_y) + slab).astype(jnp.float32)
    phi = [got[:, :G], got[:, G : 2 * G]]
    along_x = [odd * phi[part] + even * last[:, part : part + 1] for part in range(2)]
    lhs = jnp.concatenate(
        [jnp.concatenate(along_x, axis=1), jnp.concatenate([kz * phi[0], kz * phi[1]], axis=1)], axis=0
    )
    field = dot3(split(lhs), weights)
    put(0, field[:G])
    put(2, field[G:])
    sel = sel_ref[...]
    top, low = split(last)
    expanded = jnp.dot(top, sel, preferred_element_type=jnp.float32) + jnp.dot(
        low, sel, preferred_element_type=jnp.float32
    )
    pair = ((lanes_of((grid_y, 4 * LANES)) & (LANES - 1)) - lax.rem(slab, 2) * (2 * subs)) >> 1
    mids = jnp.zeros((grid_y, 4 * LANES), jnp.float32)
    for j in range(subs):
        mids = mids + jnp.where(pair == j, expanded[j * grid_y : (j + 1) * grid_y], 0.0)
    k = slab // 2 * LANES + (lanes_of((1, 2 * LANES)) & (LANES - 1))
    signed = jnp.where(k < half, k, k - G).astype(jnp.float32)
    mid_phi = mids[:, : 2 * LANES]
    mid_lhs = jnp.concatenate([signed * mid_phi, mids[:, 2 * LANES :], -float(half) * mid_phi], axis=0)
    mid_field = dot3(split(mid_lhs), (mt_ref[...], ml_ref[...]))
    wait_part(1)
    put(1, dot3(split(from_tiles(got_ref, 1)), weights))
    row = rows_of((8, G))
    for y in range(grid_y):
        rows = []
        for c in range(3):
            for part in range(2):
                tiles = [
                    field_ref[pl.ds((3 * (part * G // LANES + t) + c) * G + y, subs, stride=grid_y), :]
                    for t in range(G // LANES)
                ]
                rows.append(jnp.concatenate(tiles, axis=1))
        mid = jnp.zeros((8, G), jnp.float32)
        for c in range(3):
            mid = jnp.where(row == c, mid_field[c * grid_y + y : c * grid_y + y + 1], mid)
        here_ref[y] = jnp.concatenate(rows + [mid, jnp.zeros((8, G), jnp.float32)], axis=0)
    lane = lanes_of((here_ref.shape[1], LANES))
    for block in range(slabs):
        turned = [pltpu.roll(here_ref[y], (window * y - grid_x * block) % G, 1) for y in range(grid_y)]
        tiles = []
        for t in range(own // LANES):
            value = jnp.zeros(lane.shape, jnp.float32)
            for y in range(grid_y):
                low_lane = window * y - LANES * t
                if low_lane + window <= 0 or low_lane >= LANES:
                    continue
                side = t * LANES % G
                inside = jnp.logical_and(lane >= low_lane, lane < low_lane + window)
                value = jnp.where(inside, turned[y][:, side : side + LANES], value)
            tiles.append(value)
        lhs_t_ref[block], lhs_l_ref[block] = split(jnp.concatenate(tiles, axis=1))

    def one(block, _):
        for part in range(2):
            zh = zh_ref[part * slabs + block]
            start, rows = (0, own) if part == 0 else (own, spilt)
            a = tuple(ref[block, :, :rows] for ref in (lhs_t_ref, lhs_l_ref))
            b = tuple(ref[block, start : start + rows] for ref in (top_ref, low_ref))
            mixed = dot3(a, b)
            fields = []
            for c in range(3):
                base = 2 * subs * c
                value = jnp.sum(mixed[base : base + 2 * subs] * zh[: 2 * subs], axis=0, keepdims=True)
                at = 6 * subs + c
                fields.append(value + mixed[at : at + 1] * zh[2 * subs : 2 * subs + 1])
            r = rows_of((8, zh.shape[1]))
            out_ref[part * slabs + block] = jnp.where(
                r == 0, fields[0], jnp.where(r == 1, fields[1], jnp.where(r == 2, fields[2], 0.0))
            )
        return 0

    lax.fori_loop(0, slabs, one, 0)


def kernel_planes(slabs, subs, slab, sub, planes_ref, mids_ref, even_ref, odd_ref, mid_ref):
    half = G // 2
    width_sq = G / 4.0 * (G / 4.0)
    scale = -recip_scale / (float(G) ** 3)
    flip = ((rows_of((G, G)) + lanes_of((G, G))) & (G - 1)) == 0
    flip = flip.astype(jnp.float32).astype(jnp.bfloat16)

    def product(a, b):
        return jnp.dot(a, b, preferred_element_type=jnp.float32)

    top, low = split(planes_ref[1])
    top, low = split(product(flip, top) + product(flip, low))
    mirrored = product(top, flip) + product(low, flip)
    first = planes_ref[0]
    kx, ky = frequency_rows("signed"), frequency_columns("signed")
    kz_here = slabs * sub + slab
    kz = kz_here.astype(jnp.float32)
    freq_sq = kx * kx + ky * ky + kz * kz
    anchor = freq_sq == 0.0
    gauss = jnp.where(
        anchor, 0.0, scale * jnp.exp(freq_sq * (-0.5 / width_sq)) / jnp.where(anchor, 1.0, freq_sq)
    )
    flat = kz_here == 0
    even_ref[...] = gauss * jnp.where(flat, first, first + mirrored)
    odd_ref[...] = gauss * jnp.where(flat, first, first - mirrored)
    rows = G // slabs
    tall = [
        jnp.concatenate([mids_ref[s]] * (LANES // 8), axis=0).T[:rows] for s in range(slabs)
    ]
    tall = jnp.concatenate(tall, axis=0)
    lane = lanes_of(tall.shape)
    chosen = lax.rem(2 * sub, 8)
    columns = [jnp.sum(jnp.where(lane == chosen + t, tall, 0.0), axis=1, keepdims=True) for t in range(2)]
    kx = 2 * (subs * slab + sub) + (lane & 1)
    kx = jnp.where(kx < half, kx, kx - G).astype(jnp.float32)
    mid_sq = kx * kx + ky * ky + float(half * half)
    value = jnp.where((lane & 1) == 0, columns[0], columns[1])
    value = jnp.where(jnp.logical_and(lane >= 2, lane < 6), value, 0.0)
    mid_ref[...] = value * (scale * jnp.exp(mid_sq * (-0.5 / width_sq)) / mid_sq)


def near_columns(positions, near_ref):
    for t in range(positions.shape[1] // LANES):
        tile = positions[:, t * LANES : (t + 1) * LANES]
        near_ref[t * LANES : (t + 1) * LANES, :] = jnp.concatenate([tile] * (LANES // 8), axis=0).T


def own_cells(own_ref, table_ref):
    for t in range(own_ref.shape[1] // LANES):
        tile = own_ref[:, t * LANES : (t + 1) * LANES]
        other = pltpu.roll(tile, LANES // 2, 1)
        first = lanes_of(tile.shape) < LANES // 2
        table_ref[2 * t] = jnp.where(first, tile, other)
        table_ref[2 * t + 1] = jnp.where(first, other, tile)


def pair_field(list_ref, count_ref, table_ref, near_ref, pair_ref):
    cells, entries = list_ref.shape
    width = LANES // 2
    first_half = lanes_of((8, LANES)) < width
    is_moment = rows_of((8, LANES)) < 3
    itself = rows_of((width, LANES)) == lanes_of((width, LANES))

    def one_cell(cell, _):
        base = pl.multiple_of(cell * width, width)
        near = near_ref[pl.ds(base, width), :]
        near_x, near_y, near_z = (
            jnp.broadcast_to(near[:, 3 + a : 4 + a], (width, LANES)) for a in range(3)
        )
        count = count_ref[cell]

        def terms(pair, masked):
            one = table_ref[list_ref[cell, 2 * pair]]
            two = table_ref[list_ref[cell, 2 * pair + 1]]
            live_one = jnp.where(2 * pair < count, 1.0, 0.0)
            live_two = jnp.where(2 * pair + 1 < count, 1.0, 0.0)
            far = jnp.where(first_half, one, two)
            far = jnp.where(is_moment, far * jnp.where(first_half, live_one, live_two), far)
            mx, my, mz = far[0:1], far[1:2], far[2:3]
            dx = near_x - far[3:4]
            dy = near_y - far[4:5]
            dz = near_z - far[5:6]
            softened = dx * dx + dy * dy + dz * dz + damping
            inverse = lax.rsqrt(softened)
            square = inverse * inverse
            cube = square * inverse
            if masked:
                cube = jnp.where(itself, 0.0, cube)
            radial = (3.0 * (dx * mx + dy * my + dz * mz)) * (cube * square)
            return radial * dx - cube * mx, radial * dy - cube * my, radial * dz - cube * mz

        def step(pair, totals):
            return tuple(t + a for t, a in zip(totals, terms(pair, False)))

        totals = lax.fori_loop(1, entries // 2, step, terms(0, True))
        sums = [jnp.sum(t, axis=1, keepdims=True) for t in totals]
        lane = lanes_of((width, LANES))
        pair_ref[pl.ds(base, width), :] = jnp.where(
            lane == 0, sums[0], jnp.where(lane == 1, sums[1], jnp.where(lane == 2, sums[2], 0.0))
        )
        return 0

    lax.fori_loop(0, cells, one_cell, 0)


def around(slabs, subs):
    slab, sub = lax.axis_index("slab"), lax.axis_index("sub")
    up, down = lax.rem(sub + 1, subs), lax.rem(sub + subs - 1, subs)
    turns = [lax.rem(slab + k, slabs) for k in range(slabs)]
    return slab, sub, up, down, turns


def remote(source, target, send_sem, recv_sem, device):
    return pltpu.make_async_remote_copy(
        src_ref=source,
        dst_ref=target,
        send_sem=send_sem,
        recv_sem=recv_sem,
        device_id=device,
        device_id_type=MESH,
    )


def landed(ref, sem):
    pltpu.make_async_copy(ref, ref, sem).wait()


INPUTS = (
    ["cells", "counts", "sends", "pol", "perm", "pos", "frac", "base"]
    + ["phase_t", "phase_l", "tx_t", "tx_l", "bx_t", "bx_l", "ty_t", "ty_l", "by_t", "by_l"]
    + ["bm_t", "bm_l", "gather", "expand", "influence"]
)
SMEM_INPUTS = 3


class Refs:
    def __init__(self, names, refs):
        for name, ref in zip(names, refs, strict=True):
            setattr(self, name, ref)


def whole_kernel(slabs, subs, names, *refs):
    r = Refs(names, refs)
    slab, sub, up, down, turns = around(slabs, subs)
    depth, rows = r.moved.shape[0], r.moved.shape[1]
    half = slabs * subs
    middle = subs // 2
    group = 2 * subs

    def to_group(source, target, send_sem, recv_sem):
        goals = [(t, sub, slab) for t in turns[1:]] + [(t, up, slabs + slab) for t in turns]
        return [
            remote(source, target.at[slot], send_sem.at[n], recv_sem.at[slot], (to_slab, to_sub))
            for n, (to_slab, to_sub, slot) in enumerate(goals)
        ]

    def group_landed(target, recv_sem):
        for slot in [*turns[1:], *(slabs + k for k in range(slabs))]:
            landed(target.at[slot], recv_sem.at[slot])

    def ghost_copies(it):
        goals = [(slab, up), (slab, down), (turns[1], sub), (turns[-1], sub)]
        cells, ghosts = r.cells.shape[0], r.ghosts.shape[2]
        return [
            remote(
                r.ghosts.at[it, q],
                r.tables.at[it, pl.ds(cells + q * ghosts, ghosts)],
                r.ghost_send.at[q],
                r.ghost_recv.at[it, q],
                goal,
            )
            for q, goal in enumerate(goals)
        ]

    def send_cells(it):
        own_cells(r.own, r.own_tiles)
        r.tables[it, : r.cells.shape[0]] = r.own_tiles[...]
        ghosts = r.ghosts.shape[2]
        for q in range(4):
            for slot in range(ghosts):
                r.ghosts[it, q, slot] = r.own_tiles[r.sends[q * ghosts + slot]]
        for copy in ghost_copies(it):
            copy.start()

    def send_moments(it):
        for copy in to_group(r.own, r.mom.at[it], r.mom_send, r.mom_recv.at[it]):
            copy.start()
        r.mom[it, slab] = r.own[...]
        send_cells(it)

    moves = [pltpu.make_async_copy(r.influence.at[:, i, :], r.moved.at[i], r.move.at[i]) for i in range(depth)]
    for move in moves:
        move.start()
    atoms = r.own.shape[1]
    r.own[0:3] = r.pol[...] * r.perm[...]
    r.own[3:6] = r.pos[...]
    r.own[6:8] = jnp.zeros((2, atoms), jnp.float32)
    r.still[slab, 0:3] = r.frac[...]
    r.still[slab, 3:6] = r.base[...].astype(jnp.float32)
    r.still[slab, 6:8] = jnp.zeros((2, atoms), jnp.float32)
    still_copies = to_group(r.still.at[slab], r.still, r.still_send, r.still_recv)
    for copy in still_copies:
        copy.start()
    send_moments(0)

    def plane(i):
        kz = depth * sub + i
        upper = kz >= half
        folded = jnp.where(upper, lax.rem(2 * half - kz, half), kz)
        slot = jnp.where(upper, 1, 0)
        to_slab, to_sub = lax.rem(folded, slabs), lax.div(folded, slabs)
        target = r.planes.at[slot, pl.ds(slab * rows, rows)]
        far = remote(
            r.moved.at[i], target, r.plane_send.at[i], r.plane_recv.at[slot, slab], (to_slab, to_sub)
        )
        return far, slot, jnp.logical_and(to_slab == slab, to_sub == sub)

    def here(i, slot):
        return pltpu.make_async_copy(
            r.moved.at[i], r.planes.at[slot, pl.ds(slab * rows, rows)], r.plane_recv.at[slot, slab]
        )

    for i in range(depth):
        moves[i].wait()
        far, slot, mine = plane(i)

        @pl.when(mine)
        def _():
            here(i, slot).start()

        @pl.when(jnp.logical_not(mine))
        def _():
            far.start()

    first = r.moved[0]
    r.turned[...] = jnp.concatenate([first] * (LANES // rows), axis=0).T

    def hop(n):
        return remote(
            r.turned.at[pl.ds(turns[n] * group, group)],
            r.hop.at[slab],
            r.hop_send.at[n - 1],
            r.hop_recv.at[slab],
            (turns[n], sub),
        )

    def mid(n):
        to_sub = lax.rem(middle + n, subs)
        return remote(
            r.hop.at[:, pl.ds(lax.div(to_sub, 4) * 8, 8)],
            r.mids,
            r.mid_send.at[n - 1],
            r.mid_recv,
            (slab, to_sub),
        )

    @pl.when(sub == middle)
    def _():
        for n in range(1, slabs):
            hop(n).start()
        r.hop[slab] = r.turned[pl.ds(pl.multiple_of(slab * group, group), group)]

    near_columns(r.own[...], r.near)
    group_landed(r.still, r.still_recv)
    phase = (r.phase_t[...], r.phase_l[...])

    def tables(before):
        def one(block, _):
            tables_of(slabs, subs, r.still, block, before, phase, r.plane_t, r.plane_l, r.zhat)
            return 0

        lax.fori_loop(0, slabs, one, 0)

    tables(False)

    @pl.when(sub == middle)
    def _():
        for t in turns[1:]:
            landed(r.hop.at[t], r.hop_recv.at[t])
        for n in range(1, subs):
            mid(n).start()
        r.mids[...] = r.hop[:, (middle // 4) * 8 : (middle // 4) * 8 + 8]

    tables(True)

    def exchange(send, got, part, send_sem, recv_sem):
        first, count = part_rows(part, send.shape[1] // TILES)
        rows = pl.ds(first, count)
        pltpu.make_async_copy(send.at[sub, rows], got.at[sub, rows], recv_sem.at[part]).start()

        def one(n, _):
            to_sub = lax.rem(sub + n, subs)
            remote(
                send.at[to_sub, rows], got.at[sub, rows], send_sem.at[part], recv_sem.at[part], (slab, to_sub)
            ).start()
            return 0

        lax.fori_loop(1, subs, one, 0)

    def exchanged(got, part, recv_sem):
        first, count = part_rows(part, got.shape[1] // TILES)
        landed(got.at[:, pl.ds(first, count)], recv_sem.at[part])

    def iteration(it, _):
        group_landed(r.mom.at[it], r.mom_recv.at[it])
        density(slabs, subs, r.mom.at[it], r.plane_t, r.plane_l, r.zhat, r.grid)
        got_a, got_b = r.got_a.at[it], r.got_b.at[it]
        first_frequency(
            slabs,
            subs,
            slab,
            r.grid,
            r.tx_t,
            r.tx_l,
            r.gather,
            r.send_a,
            r.mid_rows,
            lambda part: exchange(r.send_a, got_a, part, r.a_send, r.a_recv.at[it]),
        )

        @pl.when(it == 0)
        def _():
            @pl.when(sub != middle)
            def _():
                landed(r.mids, r.mid_recv)

            for slot in range(2):
                for source in range(slabs):
                    landed(r.planes.at[slot, pl.ds(source * rows, rows)], r.plane_recv.at[slot, source])
            kernel_planes(slabs, subs, slab, sub, r.planes, r.mids, r.even, r.odd, r.mid_tile)

        cells, ghosts = r.cells.shape[0], r.ghosts.shape[2]
        for q in range(4):
            landed(r.tables.at[it, pl.ds(cells + q * ghosts, ghosts)], r.ghost_recv.at[it, q])
        pair_field(r.cells, r.counts, r.tables.at[it], r.near, r.pair)
        for t in range(atoms // LANES):
            tile = r.pair[t * LANES : (t + 1) * LANES, :].T[:8]
            r.rest[:, t * LANES : (t + 1) * LANES] = tile
        r.rest[0:3] += r.perm[...]

        second(
            got_a,
            r.even,
            r.odd,
            r.mid_tile,
            r.ty_t,
            r.ty_l,
            r.by_t,
            r.by_l,
            r.send_b,
            lambda part: exchanged(got_a, part, r.a_recv.at[it]),
            lambda part: exchange(r.send_b, got_b, part, r.b_send, r.b_recv.at[it]),
        )
        sample(
            slabs,
            subs,
            slab,
            got_b,
            r.plane_t,
            r.plane_l,
            r.zhat,
            r.bx_t,
            r.bx_l,
            r.bm_t,
            r.bm_l,
            r.expand,
            r.share,
            r.field,
            r.here,
            r.lhs_t,
            r.lhs_l,
            lambda part: exchanged(got_b, part, r.b_recv.at[it]),
        )
        goals = [(t, sub, t, slab) for t in turns[1:]] + [(t, down, slabs + t, slabs + slab) for t in turns]
        shares = [
            remote(
                r.share.at[source],
                r.land.at[it, slot],
                r.share_send.at[n],
                r.share_recv.at[it, slot],
                (to_slab, to_sub),
            )
            for n, (to_slab, to_sub, source, slot) in enumerate(goals)
        ]
        for copy in shares:
            copy.start()
        total = r.rest[...] + r.share[slab]
        for slot in [*turns[1:], *(slabs + k for k in range(slabs))]:
            landed(r.land.at[it, slot], r.share_recv.at[it, slot])
            total = total + r.land[it, slot]
        for copy in to_group(r.own, r.mom.at[it], r.mom_send, r.mom_recv.at[it]):
            copy.wait_send()
        for copy in ghost_copies(it):
            copy.wait_send()
        r.own[0:3] = r.pol[...] * total[0:3]

        @pl.when(it + 1 < ITERS)
        def _():
            send_moments(it + 1)

        for copy in shares:
            copy.wait_send()
        for part in range(2):
            rows_sent = pl.ds(*part_rows(part, r.send_a.shape[1] // TILES))
            landed(r.send_a.at[pl.ds(0, subs - 1), rows_sent], r.a_send.at[part])
            landed(r.send_b.at[pl.ds(0, subs - 1), rows_sent], r.b_send.at[part])
        return 0

    lax.fori_loop(0, ITERS, iteration, 0)
    r.out[...] = r.own[0:3]
    for copy in still_copies:
        copy.wait_send()

    @pl.when(sub == middle)
    def _():
        for n in range(1, slabs):
            hop(n).wait_send()
        for n in range(1, subs):
            mid(n).wait_send()

    for i in range(depth):
        far, slot, mine = plane(i)

        @pl.when(jnp.logical_not(mine))
        def _():
            far.wait_send()


def shards(
    positions,
    fraction,
    grid_base,
    polarizability,
    perm_field,
    influence,
    neighbour_cells,
    neighbour_count,
    send_cells,
):
    atoms = positions.shape[1]
    cells = neighbour_cells.shape[0]
    ghosts = send_cells.shape[2]
    slabs = lax.axis_size("slab")
    subs = lax.axis_size("sub")
    slab = lax.axis_index("slab")
    grid_x = G // slabs
    grid_y = G // subs
    depth = G // subs

    index = np.arange(G)
    angle = (index[:, None] * index[None, :] % G) * (2.0 * np.pi / G)
    kz_rows = np.arange(slabs)[:, None] + slabs * np.arange(subs)[None, :]
    turn = kz_rows[:, :, None] * index[None, None, :] % G * (2.0 * np.pi / G)
    ranks = 2 * subs + 8
    phase = np.zeros((slabs, ranks, G), np.float32)
    phase[:, :subs] = np.cos(turn)
    phase[:, subs : 2 * subs] = -np.sin(turn)
    phase[:, 2 * subs] = np.where(index % 2 == 0, 1.0, -1.0)
    cos_np, sin_np = np.cos(angle), np.sin(angle)
    turn_x = parts_of(np.block([[cos_np, -sin_np], [sin_np, cos_np]]))
    back_x = parts_of(np.block([[cos_np, sin_np], [-sin_np, cos_np]]))
    turn_y = parts_of(np.concatenate([cos_np, sin_np], axis=1))
    back_y = parts_of(np.concatenate([cos_np, -sin_np], axis=1))
    wide = np.stack(
        [
            np.concatenate([cos_np[w : w + LANES], -sin_np[w : w + LANES]], axis=0)
            for w in (np.arange(slabs) // 2 * LANES)
        ]
    )

    def mine(pair):
        return tuple(lax.dynamic_index_in_dim(p, slab, 0, keepdims=False) for p in pair)

    phase, back_mid = mine(parts_of(phase)), mine(parts_of(wide))
    select = np.zeros((4, LANES, LANES), np.float32)
    for q in range(4):
        for lane in range(LANES):
            select[q, lane, 2 + 2 * q + lane % 2] = 1.0
    gather = jnp.asarray(select.reshape(4 * LANES, LANES), jnp.bfloat16)
    expand = jnp.asarray(np.concatenate(list(select.transpose(0, 2, 1)), axis=1), jnp.bfloat16)

    operands = [
        neighbour_cells,
        neighbour_count,
        send_cells.reshape(4 * ghosts),
        polarizability[None, :],
        perm_field,
        positions,
        fraction,
        grid_base,
        *phase,
        *turn_x,
        *back_x,
        *turn_y,
        *back_y,
        *back_mid,
        gather,
        expand,
        influence,
    ]
    vmem = pl.BlockSpec(memory_space=pltpu.VMEM)
    smem = pl.BlockSpec(memory_space=pltpu.SMEM)
    specs = [smem] * SMEM_INPUTS + [vmem] * (len(operands) - SMEM_INPUTS - 1) + [pl.BlockSpec(memory_space=pl.ANY)]

    def held(*shape, dtype=jnp.float32):
        return pltpu.VMEM(shape, dtype)

    held16 = functools.partial(held, dtype=jnp.bfloat16)
    dma = pltpu.SemaphoreType.DMA
    chunk = (subs, TILES * grid_y, LANES)
    columns = 6 * subs + 16
    sends = 2 * slabs - 1
    planes = sum(plane_rows(slabs, subs))
    scratch = dict(
        mom=held(ITERS, 2 * slabs, 8, atoms),
        still=held(2 * slabs, 8, atoms),
        own=held(8, atoms),
        own_tiles=held(cells, 8, LANES),
        tables=held(ITERS, cells + 4 * ghosts, 8, LANES),
        ghosts=held(ITERS, 4, ghosts, 8, LANES),
        near=held(atoms, LANES),
        pair=held(atoms, LANES),
        rest=held(8, atoms),
        plane_t=held16(slabs, planes, atoms),
        plane_l=held16(slabs, planes, atoms),
        zhat=held(2 * slabs, ranks, atoms),
        moved=held(depth, grid_x, G),
        turned=held(G, LANES),
        hop=held(slabs, grid_x, LANES),
        planes=held(2, G, G),
        mids=held(slabs, 8, LANES),
        even=held(G, G),
        odd=held(G, G),
        mid_tile=held(G, LANES),
        grid=held(grid_y, G + 8, 256),
        mid_rows=held(4, grid_y, G),
        send_a=held(*chunk),
        got_a=held(ITERS, *chunk),
        send_b=held(*chunk),
        got_b=held(ITERS, *chunk),
        field=held(6 * G * G // LANES, LANES),
        here=held(grid_y, columns, G),
        lhs_t=held16(slabs, columns, plane_rows(slabs, subs)[0]),
        lhs_l=held16(slabs, columns, plane_rows(slabs, subs)[0]),
        share=held(2 * slabs, 8, atoms),
        land=held(ITERS, 2 * slabs, 8, atoms),
        mom_send=dma((sends,)),
        mom_recv=dma((ITERS, 2 * slabs)),
        still_send=dma((sends,)),
        still_recv=dma((2 * slabs,)),
        ghost_send=dma((4,)),
        ghost_recv=dma((ITERS, 4)),
        move=dma((depth,)),
        plane_send=dma((depth,)),
        plane_recv=dma((2, slabs)),
        hop_send=dma((slabs - 1,)),
        hop_recv=dma((slabs,)),
        mid_send=dma((subs - 1,)),
        mid_recv=dma,
        a_send=dma((2,)),
        a_recv=dma((ITERS, 2)),
        b_send=dma((2,)),
        b_recv=dma((ITERS, 2)),
        share_send=dma((sends,)),
        share_recv=dma((ITERS, 2 * slabs)),
    )
    names = [*INPUTS, "out", *scratch]
    return pl.pallas_call(
        functools.partial(whole_kernel, slabs, subs, names),
        out_shape=jax.ShapeDtypeStruct((3, atoms), jnp.float32),
        in_specs=specs,
        out_specs=vmem,
        scratch_shapes=list(scratch.values()),
        compiler_params=pltpu.CompilerParams(vmem_limit_bytes=60 << 20, has_side_effects=True),
        name="dipoles",
    )(*operands)


def solution(mesh):
    in_specs = (
        P(None, ("slab", "sub")),
        P(None, ("slab", "sub")),
        P(None, ("slab", "sub")),
        P(("slab", "sub")),
        P(None, ("slab", "sub")),
        P("slab", "sub", None),
        P(("slab", "sub"), None),
        P(("slab", "sub")),
        P(("slab", "sub"), None, None),
    )
    out_specs = P(None, ("slab", "sub"))
    return jax.shard_map(shards, mesh=mesh, in_specs=in_specs, out_specs=out_specs, check_vma=False)
```

time: 1020 us -> 165 us (0.16); the launches traced: 1000 us -> 164 us
  local copies, waits for them, and re-layouts: 449 us -> 5.71 us
  matrix products: 176 us -> 0 us
  other arithmetic: 172 us -> 0 us
  Pallas kernels: 0 us -> 158 us
  starting transfers between devices: 155 us -> 0 us
  waiting for transfers between devices: 47.3 us -> 0 us
    dot_general x44 -> x0, matrix products: 176 us -> none  [the longest x4 27.8 us: sample(): lax.dot_general(interpolate_widened, plane_rows, (((0,), (0,)), ((), ()))...]
    pallas_call x0 -> x1, Pallas kernels: none -> 158 us  [shards(): pl.pallas_call(functools.partial(whole_kernel, slabs, subs, names), out_s...]
    all_to_all x13 -> x0, starting transfers between devices: 109 us -> none  [the longest x12 105 us: one_exchange(): lax.all_to_all(pieces, axis, split_axis=0, concat_axis=0, tiled=True)]
    unnamed x179 -> x3, local copies, waits for them, and re-layouts: 91.6 us -> 2.01 us
    reshape x54 -> x1, local copies, waits for them, and re-layouts: 83.4 us -> 0.59 us  [shards(): send_cells.reshape(4 * ghosts)]
    another operation x28 -> x0, local copies, waits for them, and re-layouts: 80 us -> none
    all_to_all x12 -> x0, other arithmetic: 64 us -> none  [one_exchange(): lax.all_to_all(pieces, axis, split_axis=0, concat_axis=0, tiled=True)]
    ppermute x16 -> x0, waiting for transfers between devices: 47.2 us -> none  [shifted(): return lax.ppermute(value, axis, pairs)]
  transfers between devices with their start and end apart: 29 -> 0, of which waited for: 4 -> 0; matrix products, arithmetic and copies ran while one was open for 54% -> 0% of each run, Pallas kernels for 0% -> 0%
where the time goes in v3:
time: 165 us; the launch traced here: 164 us
  Pallas kernels  158 us (96%)
  local copies, waits for them, and re-layouts  5.71 us (3%)
    pallas_call x1, Pallas kernels, shards(): pl.pallas_call(functools.partial(whole_kernel, slabs, subs, names), out_s...  158 us

profile of v3, /device:TPU:1, one launch (start us, length us, event | category | flops | bytes accessed | tf_op | source)
XLA Modules:
  0.0 164.2 jit_solution(14802112565598404819)
XLA Ops:
  0.0 0.0 copy-start
  0.0 0.7 copy-done
  0.7 0.6 reshape.3.refs_2_
  1.3 1.4 dynamic-slice_bitcast_fusion.2
  2.7 1.7 %dynamic-slice_bitcast_fusion = (bf16[256,256]{1,0:T(8,128)(2,1)}, bf16[256,256]{1,0:T(8,128)(2,1)}) fusion(bf16[4,256,256]{2,1,0:T(8,128)(2,1)} %constant.59.clone, s32[]{:T(128)S(6)} %select_n.8, bf16[4,256,256]{2,1,0:T(8,128)(2,1)} %constant.58.clone), kind=kLoop, calls=%fused_computation | loop fusion | bytes 524292 | tf_op jit(solution)/shard_map/jit(dynamic_index_in_dim)/squeeze | solution.py:864
  4.4 158.5 %dipoles.1 = f32[3,1024]{1,0:T(4,128)} custom-call(s32[16,16]{1,0:T(8,128)} %refs_0_.1, s32[16]{0:T(128)} %refs_1_.1, s32[32]{0:T(128)} %reshape.3.refs_2_, f32[1,1024]{1,0:T(1,128)} %bitcast.9, f32[3,1024]{1,0:T(4,128)} %refs_4_.1, f32[3,1024]{1,0:T(4,128)} %refs_5_.1, f32[3,1024]{1,0:T(4,128)} %refs_6_.1, s32[3,1024]{1,0:T(4,128)} %refs_7_.1, ...), custom_call_target="tpu_custom_call" | custom-call | tf_op jit(solution)/shard_map/dipoles/pallas_call | solution.py:960
  162.8 1.3 copy.25
Async XLA Ops:
  0.0 0.7 copy-start

commit v4 on v3

--- a/solution.py
+++ b/solution.py
@@ -17,7 +17,6 @@
 highest = lax.Precision.HIGHEST
 LANES = 128
 TILES = 4 * G // LANES + 1
-EXTRA = 2 * G // LANES
 MESH = pl.DeviceIdType.MESH
 
 
@@ -76,17 +75,14 @@
     still = still_ref[at]
     atoms = still.shape[1]
 
-    def table(axis, length, wrapped):
-        start = still[3 + axis : 4 + axis].astype(jnp.int32)
-        offset = rows_of((length, atoms)) - start
-        if wrapped:
-            offset = jnp.where(offset < 0, offset + length, offset)
+    def table(axis, length):
+        offset = rows_of((length, atoms)) - still[3 + axis : 4 + axis].astype(jnp.int32)
         total = jnp.zeros(offset.shape, jnp.float32)
         for stencil, weight in enumerate(spline_weights(still[axis : 1 + axis])):
             total = jnp.where(offset == stencil, weight, total)
         return total
 
-    along_x, along_y = table(0, window_of(slabs), False), table(1, 16, False)
+    along_x, along_y = table(0, window_of(slabs)), table(1, 16)
     grid_y = G // subs
     first, count = (grid_y, 3) if before else (0, grid_y)
     own, spilt = plane_rows(slabs, subs)
@@ -96,7 +92,21 @@
     top, low = split(jnp.concatenate([*plane, blank], axis=0))
     top_ref[block, start : start + rows] = top
     low_ref[block, start : start + rows] = low
-    zh_ref[at] = dot3(phase, split(table(2, G, True)))
+    z0 = still[5:6].astype(jnp.int32)
+    chosen = (rows_of((G, atoms)) == z0).astype(jnp.float32).astype(jnp.bfloat16)
+    start = jnp.dot(phase[0], chosen, preferred_element_type=jnp.float32) + jnp.dot(
+        phase[1], chosen, preferred_element_type=jnp.float32
+    )
+    steps = phase[0][:, :LANES].astype(jnp.float32) + phase[1][:, :LANES].astype(jnp.float32)
+    wide = [jnp.zeros((subs, atoms), jnp.float32)] * 2
+    mid = jnp.zeros((1, atoms), jnp.float32)
+    for t, weight in enumerate(spline_weights(still[2:3])):
+        wide = [v + weight * steps[n * subs : (n + 1) * subs, t : t + 1] for n, v in enumerate(wide)]
+        mid = mid + (weight if t % 2 == 0 else -weight)
+    re, im = start[:subs], start[subs : 2 * subs]
+    zh_ref[at, :subs] = re * wide[0] - im * wide[1]
+    zh_ref[at, subs : 2 * subs] = re * wide[1] + im * wide[0]
+    zh_ref[at, 2 * subs :] = start[2 * subs :] * mid
 
 
 def frequency_rows(kind):
@@ -119,20 +129,32 @@
     return signed
 
 
-def density(slabs, subs, mom_ref, top_ref, low_ref, zh_ref, grid_ref):
+def density(slabs, subs, slab, mom_ref, top_ref, low_ref, zh_ref, grid_ref, wait_block):
     grid_y = G // subs
     grid_x = G // slabs
     window = window_of(slabs)
     own, _ = plane_rows(slabs, subs)
     grid_ref[...] = jnp.zeros_like(grid_ref)
 
-    def one(block, _):
-        for part in range(2):
-            mu = mom_ref[part * slabs + block]
-            zh = zh_ref[part * slabs + block]
+    for part in range(2):
+
+        def one(n, _):
+            block = lax.rem(slab + n, slabs)
+            at = block + part * slabs
+            if part == 0:
+
+                @pl.when(n > 0)
+                def _():
+                    wait_block(at)
+
+            else:
+                wait_block(at)
+            mu = mom_ref[at]
+            zh = zh_ref[at]
+            row = rows_of((8, mu.shape[1]))
+            last = jnp.where(row == 0, mu[0:1], jnp.where(row == 1, mu[1:2], mu[2:3]))
             values = jnp.concatenate(
-                [zh[: 2 * subs] * mu[c : c + 1] for c in range(3)] + [mu * zh[2 * subs : 2 * subs + 1]],
-                axis=0,
+                [zh[: 2 * subs] * mu[c : c + 1] for c in range(3)] + [last * zh[2 * subs : 2 * subs + 1]], axis=0
             )
             start, count = (0, grid_y) if part == 0 else (own, 3)
             rows = -(-count * window // 16) * 16
@@ -142,55 +164,62 @@
             for y in range(count):
                 where = pl.ds(pl.multiple_of(block * grid_x, grid_x), window)
                 grid_ref[y, where, :columns] += got[y * window : (y + 1) * window]
-        return 0
-
-    lax.fori_loop(0, slabs, one, 0)
+            return 0
+
+        lax.fori_loop(0, slabs, one, 0)
     for y in range(grid_y):
         grid_ref[y, :8] += grid_ref[y, G : G + 8]
+
+
+def half_of(row, part):
+    return row[:, part * LANES : (part + 1) * LANES]
 
 
 def first_frequency(slabs, subs, slab, grid_ref, wt_ref, wl_ref, sel_ref, out_ref, mid_ref, send_part):
     grid_y = G // subs
     half = G // 2
     flat_ref = out_ref.reshape(subs * TILES * grid_y, LANES)
-    turned = [grid_ref[y, :G].T for y in range(grid_y)]
-    weights = (wt_ref[...], wl_ref[...])
-
-    def pair_rows(value, c):
-        base = 2 * subs * c
-        return jnp.concatenate([value[base : base + subs], value[base + subs : base + 2 * subs]], axis=1)
-
-    def put(first, y, values):
-        tiles = [v[:, t * LANES : (t + 1) * LANES] for v in values for t in range(v.shape[1] // LANES)]
-        for t, value in enumerate(tiles):
-            flat_ref[pl.ds((first + t) * grid_y + y, subs, stride=TILES * grid_y), :] = value
-
-    spec = dot3(split(jnp.concatenate([pair_rows(v, 1) for v in turned], axis=0)), weights)
+    rows = []
     for y in range(grid_y):
-        put(EXTRA + 1, y, [spec[y * subs : (y + 1) * subs]])
-    send_part(1)
-    rows = []
-    for v in turned:
-        mids = v[6 * subs : 6 * subs + 8]
-        rows += [pair_rows(v, 0), pair_rows(v, 2), jnp.concatenate([mids, jnp.zeros_like(mids)], axis=1)]
-    spec = dot3(split(jnp.concatenate(rows, axis=0)), weights)
+        turned = grid_ref[y, :G].T
+        for c in range(3):
+            base = 2 * subs * c
+            rows.append(
+                jnp.concatenate([turned[base : base + subs], turned[base + subs : base + 2 * subs]], axis=1)
+            )
+        mids = turned[6 * subs : 6 * subs + 8]
+        rows.append(jnp.concatenate([mids, jnp.zeros_like(mids)], axis=1))
+    lhs = split(jnp.concatenate(rows, axis=0))
     odd, signed = frequency_rows("odd"), frequency_rows("signed")
     kz = (slabs * lax.broadcasted_iota(jnp.int32, (subs, 1), 0) + slab).astype(jnp.float32)
     lane = lanes_of((subs, LANES))
-    per_y = 2 * subs + 8
-    for y in range(grid_y):
-        at = spec[y * per_y : (y + 1) * per_y]
-        sx, sz, mid = at[:subs], at[subs : 2 * subs], at[2 * subs :]
-        edge = jnp.where(
-            lane == 0,
-            -float(half) * sx[:, half : half + 1],
-            jnp.where(lane == 1, -float(half) * sx[:, G + half : G + half + 1], 0.0),
-        )
-        put(0, y, [odd * sx[:, :G] + kz * sz[:, :G], odd * sx[:, G:] + kz * sz[:, G:], edge])
-        for part, shift in ((0, 0), (1, G)):
-            mx, my, mz = (mid[c : c + 1, shift : shift + G] for c in range(3))
-            mid_ref[part, y : y + 1] = signed * mx - float(half) * mz
-            mid_ref[2 + part, y : y + 1] = my
+    per_y = 3 * subs + 8
+
+    def transformed(part):
+        columns = slice(part * 2 * LANES, (part + 1) * 2 * LANES)
+        spec = dot3(lhs, (wt_ref[:, columns], wl_ref[:, columns]))
+        for y in range(grid_y):
+            at = spec[y * per_y : (y + 1) * per_y]
+            sx, sy, sz = (at[c * subs : (c + 1) * subs] for c in range(3))
+            tiles = [
+                half_of(odd, part) * half_of(sx, n) + kz * half_of(sz, n) for n in range(2)
+            ] + [half_of(sy, 0), half_of(sy, 1)]
+            if part == 1:
+                tiles.append(
+                    -float(half) * jnp.where(lane == 0, sx[:, :1], jnp.where(lane == 1, sx[:, LANES : LANES + 1], 0.0))
+                )
+            for t, value in enumerate(tiles):
+                flat_ref[pl.ds((part * 4 + t) * grid_y + y, subs, stride=TILES * grid_y), :] = value
+            mid = at[3 * subs :]
+            lanes = slice(part * LANES, (part + 1) * LANES)
+            for n in range(2):
+                mx, my, mz = (half_of(mid[c : c + 1], n) for c in range(3))
+                mid_ref[n, y : y + 1, lanes] = half_of(signed, part) * mx - float(half) * mz
+                mid_ref[2 + n, y : y + 1, lanes] = my
+
+    transformed(0)
+    send_part(0)
+    transformed(1)
     window = pl.ds(pl.multiple_of(slab // 2 * LANES, LANES), LANES)
     pair = (lanes_of((grid_y, LANES)) - lax.rem(slab, 2) * (2 * subs)) >> 1
     columns = []
@@ -202,12 +231,12 @@
     more = jnp.dot(top, sel, preferred_element_type=jnp.float32) + jnp.dot(
         low, sel, preferred_element_type=jnp.float32
     )
-    out_ref[:, EXTRA * grid_y : (EXTRA + 1) * grid_y, :] += more.reshape(subs, grid_y, LANES)
-    send_part(0)
+    out_ref[:, (TILES - 1) * grid_y :, :] += more.reshape(subs, grid_y, LANES)
+    send_part(1)
 
 
 def part_rows(part, high):
-    return (0, (EXTRA + 1) * high) if part == 0 else ((EXTRA + 1) * high, EXTRA * high)
+    return (0, 4 * high) if part == 0 else (4 * high, (TILES - 4) * high)
 
 
 def from_tiles(ref, part):
@@ -230,12 +259,15 @@
 
 
 def with_swapped(x):
-    top, low = split(x[:, : 2 * G])
+    def tile(v, t):
+        return v[:, t * LANES : (t + 1) * LANES]
+
     both = [
-        jnp.concatenate([v, jnp.concatenate([v[:, G:], -v[:, :G]], axis=1)], axis=0) for v in (top, low)
+        jnp.concatenate([v, jnp.concatenate([tile(v, 1), -tile(v, 0), tile(v, 3), -tile(v, 2)], axis=1)], axis=0)
+        for v in split(x[:, : 4 * LANES])
     ]
-    if x.shape[1] > 2 * G:
-        last = x[:, 2 * G :]
+    if x.shape[1] > 4 * LANES:
+        last = x[:, 4 * LANES :]
         lane = lanes_of(last.shape)
         back, on = pltpu.roll(last, LANES - 1, 1), pltpu.roll(last, 1, 1)
         back2, on2 = pltpu.roll(last, LANES - 2, 1), pltpu.roll(last, 2, 1)
@@ -247,35 +279,34 @@
 
 
 def second(got_ref, even_ref, odd_ref, mid_ref, ft_ref, fl_ref, bt_ref, bl_ref, out_ref, wait_part, send_part):
-    half = G // 2
     forward, backward = (ft_ref[...], fl_ref[...]), (bt_ref[...], bl_ref[...])
-    wait_part(1)
-    b_all = dot3(forward, with_swapped(from_tiles(got_ref, 1)))
-    wait_part(0)
-    a_all = dot3(forward, with_swapped(from_tiles(got_ref, 0)))
-    last = a_all[:, 2 * G :]
-    lane = lanes_of(last.shape)
-    at_half = (lanes_of((1, G)) == half).astype(jnp.float32)
     odd_y, even_y, full_y = (frequency_columns(k) for k in ("odd", "even", "signed"))
-    kernel_even, kernel_odd = even_ref[...], odd_ref[...]
-    phis, along_y, columns = [], [], []
     for part in range(2):
-        a = a_all[:, part * G : (part + 1) * G]
-        b = b_all[:, part * G : (part + 1) * G]
-        level = a + odd_y * b
-        edge = even_y * b + at_half * last[:, part : part + 1]
-        phi = kernel_even * level + kernel_odd * edge
-        phi_edge = kernel_odd * level + kernel_even * edge
-        phis.append(phi)
-        along_y.append(odd_y * phi + even_y * phi_edge)
-        columns.append(phi_edge[:, half : half + 1])
-    mid = mid_ref[...] * (last + full_y * pltpu.roll(last, LANES - 4, 1))
-    mid = mid + full_y * pltpu.roll(mid, 4, 1)
-    last = jnp.where(lane == 0, columns[0], jnp.where(lane == 1, columns[1], mid))
-    to_tiles(dot3(backward, with_swapped(jnp.concatenate([*phis, last], axis=1))), out_ref, 0)
-    send_part(0)
-    to_tiles(dot3(backward, with_swapped(jnp.concatenate(along_y, axis=1))), out_ref, 1)
-    send_part(1)
+        wait_part(part)
+        spec = dot3(forward, with_swapped(from_tiles(got_ref, part)))
+        lanes = slice(part * LANES, (part + 1) * LANES)
+        kernel_even, kernel_odd = even_ref[:, lanes], odd_ref[:, lanes]
+        lane = lanes_of(kernel_even.shape)
+        last = spec[:, 4 * LANES :]
+        tiles, columns = [None] * 4, []
+        for n in range(2):
+            a = spec[:, n * LANES : (n + 1) * LANES]
+            b = spec[:, (2 + n) * LANES : (3 + n) * LANES]
+            level = a + odd_y * b
+            edge = even_y * b
+            if part == 1:
+                edge = edge + jnp.where(lane == 0, last[:, n : n + 1], 0.0)
+            phi = kernel_even * level + kernel_odd * edge
+            phi_edge = kernel_odd * level + kernel_even * edge
+            tiles[n] = phi
+            tiles[2 + n] = odd_y * phi + even_y * phi_edge
+            columns.append(phi_edge[:, :1])
+        if part == 1:
+            mid = mid_ref[...] * (last + full_y * pltpu.roll(last, LANES - 4, 1))
+            mid = mid + full_y * pltpu.roll(mid, 4, 1)
+            tiles.append(jnp.where(lane == 0, columns[0], jnp.where(lane == 1, columns[1], mid)))
+        to_tiles(dot3(backward, with_swapped(jnp.concatenate(tiles, axis=1))), out_ref, part)
+        send_part(part)
 
 
 def sample(
@@ -303,25 +334,23 @@
     half = G // 2
     window = window_of(slabs)
     own, spilt = plane_rows(slabs, subs)
-    weights = (wt_ref[...], wl_ref[...])
-
-    def put(component, value):
-        for t in range(2 * G // LANES):
-            field_ref[pl.ds((3 * t + component) * G, G), :] = value[:, t * LANES : (t + 1) * LANES]
-
-    wait_part(0)
-    got = from_tiles(got_ref, 0)
-    last = got[:, 2 * G :]
     odd, even = frequency_rows("odd"), frequency_rows("even")
     kz = (slabs * (lax.broadcasted_iota(jnp.int32, (G, 1), 0) // grid_y) + slab).astype(jnp.float32)
-    phi = [got[:, :G], got[:, G : 2 * G]]
-    along_x = [odd * phi[part] + even * last[:, part : part + 1] for part in range(2)]
-    lhs = jnp.concatenate(
-        [jnp.concatenate(along_x, axis=1), jnp.concatenate([kz * phi[0], kz * phi[1]], axis=1)], axis=0
-    )
-    field = dot3(split(lhs), weights)
-    put(0, field[:G])
-    put(2, field[G:])
+    for part in range(2):
+        wait_part(part)
+        got = from_tiles(got_ref, part)
+        last = got[:, 4 * LANES :]
+        phi = got[:, : 2 * LANES]
+        along_x = [half_of(odd, part) * half_of(phi, n) for n in range(2)]
+        if part == 1:
+            along_x = [v + half_of(even, part) * last[:, n : n + 1] for n, v in enumerate(along_x)]
+        lhs = jnp.concatenate([jnp.concatenate(along_x, axis=1), got[:, 2 * LANES : 4 * LANES], kz * phi], axis=0)
+        rows = slice(part * 2 * LANES, (part + 1) * 2 * LANES)
+        field = dot3(split(lhs), (wt_ref[rows], wl_ref[rows]))
+        for t in range(2 * G // LANES):
+            where = pl.ds(3 * t * G, 3 * G)
+            value = field[:, t * LANES : (t + 1) * LANES]
+            field_ref[where, :] = value if part == 0 else field_ref[where, :] + value
     sel = sel_ref[...]
     top, low = split(last)
     expanded = jnp.dot(top, sel, preferred_element_type=jnp.float32) + jnp.dot(
@@ -336,8 +365,6 @@
     mid_phi = mids[:, : 2 * LANES]
     mid_lhs = jnp.concatenate([signed * mid_phi, mids[:, 2 * LANES :], -float(half) * mid_phi], axis=0)
     mid_field = dot3(split(mid_lhs), (mt_ref[...], ml_ref[...]))
-    wait_part(1)
-    put(1, dot3(split(from_tiles(got_ref, 1)), weights))
     row = rows_of((8, G))
     for y in range(grid_y):
         rows = []
@@ -381,10 +408,8 @@
                 value = jnp.sum(mixed[base : base + 2 * subs] * zh[: 2 * subs], axis=0, keepdims=True)
                 at = 6 * subs + c
                 fields.append(value + mixed[at : at + 1] * zh[2 * subs : 2 * subs + 1])
-            r = rows_of((8, zh.shape[1]))
-            out_ref[part * slabs + block] = jnp.where(
-                r == 0, fields[0], jnp.where(r == 1, fields[1], jnp.where(r == 2, fields[2], 0.0))
-            )
+            for c in range(3):
+                out_ref[part * slabs + block, c : c + 1] = fields[c]
         return 0
 
     lax.fori_loop(0, slabs, one, 0)
@@ -519,9 +544,10 @@
 
 INPUTS = (
     ["cells", "counts", "sends", "pol", "perm", "pos", "frac", "base"]
-    + ["phase_t", "phase_l", "tx_t", "tx_l", "bx_t", "bx_l", "ty_t", "ty_l", "by_t", "by_l"]
-    + ["bm_t", "bm_l", "gather", "expand", "influence"]
+    + ["phase_t", "phase_l", "bm_t", "bm_l", "gather", "expand", "influence"]
+    + ["tx_t", "tx_l", "bx_t", "bx_l", "ty_t", "ty_l", "by_t", "by_l"]
 )
+TWIDDLES = INPUTS[-8:]
 SMEM_INPUTS = 3
 
 
@@ -545,10 +571,6 @@
             remote(source, target.at[slot], send_sem.at[n], recv_sem.at[slot], (to_slab, to_sub))
             for n, (to_slab, to_sub, slot) in enumerate(goals)
         ]
-
-    def group_landed(target, recv_sem):
-        for slot in [*turns[1:], *(slabs + k for k in range(slabs))]:
-            landed(target.at[slot], recv_sem.at[slot])
 
     def ghost_copies(it):
         goals = [(slab, up), (slab, down), (turns[1], sub), (turns[-1], sub)]
@@ -565,12 +587,12 @@
         ]
 
     def send_cells(it):
-        own_cells(r.own, r.own_tiles)
+        own_cells(r.body, r.own_tiles)
         r.tables[it, : r.cells.shape[0]] = r.own_tiles[...]
         ghosts = r.ghosts.shape[2]
         for q in range(4):
             for slot in range(ghosts):
-                r.ghosts[it, q, slot] = r.own_tiles[r.sends[q * ghosts + slot]]
+                r.ghosts[it, q, slot] = r.own_tiles[r.sends[0, q, slot]]
         for copy in ghost_copies(it):
             copy.start()
 
@@ -578,15 +600,21 @@
         for copy in to_group(r.own, r.mom.at[it], r.mom_send, r.mom_recv.at[it]):
             copy.start()
         r.mom[it, slab] = r.own[...]
+        r.body[0:3] = r.own[0:3]
         send_cells(it)
 
     moves = [pltpu.make_async_copy(r.influence.at[:, i, :], r.moved.at[i], r.move.at[i]) for i in range(depth)]
-    for move in moves:
+    loads = [
+        pltpu.make_async_copy(getattr(r, name), getattr(r, "in_" + name), r.load.at[n])
+        for n, name in enumerate(TWIDDLES)
+    ]
+    for move in [*moves, *loads]:
         move.start()
     atoms = r.own.shape[1]
     r.own[0:3] = r.pol[...] * r.perm[...]
-    r.own[3:6] = r.pos[...]
-    r.own[6:8] = jnp.zeros((2, atoms), jnp.float32)
+    r.own[3:4] = jnp.zeros((1, atoms), jnp.float32)
+    r.body[3:6] = r.pos[...]
+    r.body[6:8] = jnp.zeros((2, atoms), jnp.float32)
     r.still[slab, 0:3] = r.frac[...]
     r.still[slab, 3:6] = r.base[...].astype(jnp.float32)
     r.still[slab, 6:8] = jnp.zeros((2, atoms), jnp.float32)
@@ -652,12 +680,18 @@
             hop(n).start()
         r.hop[slab] = r.turned[pl.ds(pl.multiple_of(slab * group, group), group)]
 
-    near_columns(r.own[...], r.near)
-    group_landed(r.still, r.still_recv)
-    phase = (r.phase_t[...], r.phase_l[...])
+    near_columns(r.body[...], r.near)
+    phase = (r.phase_t[slab], r.phase_l[slab])
 
     def tables(before):
-        def one(block, _):
+        def one(n, _):
+            block = lax.rem(slab + n, slabs)
+            at = block + slabs if before else block
+
+            @pl.when(jnp.logical_or(before, n > 0))
+            def _():
+                landed(r.still.at[at], r.still_recv.at[at])
+
             tables_of(slabs, subs, r.still, block, before, phase, r.plane_t, r.plane_l, r.zhat)
             return 0
 
@@ -674,6 +708,8 @@
         r.mids[...] = r.hop[:, (middle // 4) * 8 : (middle // 4) * 8 + 8]
 
     tables(True)
+    for load in loads:
+        load.wait()
 
     def exchange(send, got, part, send_sem, recv_sem):
         first, count = part_rows(part, send.shape[1] // TILES)
@@ -694,16 +730,25 @@
         landed(got.at[:, pl.ds(first, count)], recv_sem.at[part])
 
     def iteration(it, _):
-        group_landed(r.mom.at[it], r.mom_recv.at[it])
-        density(slabs, subs, r.mom.at[it], r.plane_t, r.plane_l, r.zhat, r.grid)
+        density(
+            slabs,
+            subs,
+            slab,
+            r.mom.at[it],
+            r.plane_t,
+            r.plane_l,
+            r.zhat,
+            r.grid,
+            lambda slot: landed(r.mom.at[it, slot], r.mom_recv.at[it, slot]),
+        )
         got_a, got_b = r.got_a.at[it], r.got_b.at[it]
         first_frequency(
             slabs,
             subs,
             slab,
             r.grid,
-            r.tx_t,
-            r.tx_l,
+            r.in_tx_t,
+            r.in_tx_l,
             r.gather,
             r.send_a,
             r.mid_rows,
@@ -735,10 +780,10 @@
             r.even,
             r.odd,
             r.mid_tile,
-            r.ty_t,
-            r.ty_l,
-            r.by_t,
-            r.by_l,
+            r.in_ty_t,
+            r.in_ty_l,
+            r.in_by_t,
+            r.in_by_l,
             r.send_b,
             lambda part: exchanged(got_a, part, r.a_recv.at[it]),
             lambda part: exchange(r.send_b, got_b, part, r.b_send, r.b_recv.at[it]),
@@ -751,10 +796,10 @@
             r.plane_t,
             r.plane_l,
             r.zhat,
-            r.bx_t,
-            r.bx_l,
-            r.bm_t,
-            r.bm_l,
+            r.in_bx_t,
+            r.in_bx_l,
+            r.bm_t.at[slab // 2],
+            r.bm_l.at[slab // 2],
             r.expand,
             r.share,
             r.field,
@@ -776,15 +821,15 @@
         ]
         for copy in shares:
             copy.start()
-        total = r.rest[...] + r.share[slab]
+        total = r.rest[0:3] + r.share[slab, 0:3]
         for slot in [*turns[1:], *(slabs + k for k in range(slabs))]:
             landed(r.land.at[it, slot], r.share_recv.at[it, slot])
-            total = total + r.land[it, slot]
+            total = total + r.land[it, slot, 0:3]
         for copy in to_group(r.own, r.mom.at[it], r.mom_send, r.mom_recv.at[it]):
             copy.wait_send()
         for copy in ghost_copies(it):
             copy.wait_send()
-        r.own[0:3] = r.pol[...] * total[0:3]
+        r.own[0:3] = r.pol[...] * total
 
         @pl.when(it + 1 < ITERS)
         def _():
@@ -834,7 +879,6 @@
     ghosts = send_cells.shape[2]
     slabs = lax.axis_size("slab")
     subs = lax.axis_size("sub")
-    slab = lax.axis_index("slab")
     grid_x = G // slabs
     grid_y = G // subs
     depth = G // subs
@@ -849,21 +893,15 @@
     phase[:, subs : 2 * subs] = -np.sin(turn)
     phase[:, 2 * subs] = np.where(index % 2 == 0, 1.0, -1.0)
     cos_np, sin_np = np.cos(angle), np.sin(angle)
-    turn_x = parts_of(np.block([[cos_np, -sin_np], [sin_np, cos_np]]))
-    back_x = parts_of(np.block([[cos_np, sin_np], [-sin_np, cos_np]]))
+    halves = np.concatenate([index[:LANES], G + index[:LANES], index[LANES:], G + index[LANES:]])
+    turn_x = parts_of(np.block([[cos_np, -sin_np], [sin_np, cos_np]])[:, halves])
+    back_x = parts_of(np.block([[cos_np, sin_np], [-sin_np, cos_np]])[halves])
     turn_y = parts_of(np.concatenate([cos_np, sin_np], axis=1))
     back_y = parts_of(np.concatenate([cos_np, -sin_np], axis=1))
     wide = np.stack(
-        [
-            np.concatenate([cos_np[w : w + LANES], -sin_np[w : w + LANES]], axis=0)
-            for w in (np.arange(slabs) // 2 * LANES)
-        ]
+        [np.concatenate([cos_np[w : w + LANES], -sin_np[w : w + LANES]], axis=0) for w in range(0, G, LANES)]
     )
-
-    def mine(pair):
-        return tuple(lax.dynamic_index_in_dim(p, slab, 0, keepdims=False) for p in pair)
-
-    phase, back_mid = mine(parts_of(phase)), mine(parts_of(wide))
+    phase, back_mid = parts_of(phase), parts_of(wide)
     select = np.zeros((4, LANES, LANES), np.float32)
     for q in range(4):
         for lane in range(LANES):
@@ -874,25 +912,27 @@
     operands = [
         neighbour_cells,
         neighbour_count,
-        send_cells.reshape(4 * ghosts),
+        send_cells,
         polarizability[None, :],
         perm_field,
         positions,
         fraction,
         grid_base,
         *phase,
+        *back_mid,
+        gather,
+        expand,
+        influence,
         *turn_x,
         *back_x,
         *turn_y,
         *back_y,
-        *back_mid,
-        gather,
-        expand,
-        influence,
     ]
     vmem = pl.BlockSpec(memory_space=pltpu.VMEM)
     smem = pl.BlockSpec(memory_space=pltpu.SMEM)
-    specs = [smem] * SMEM_INPUTS + [vmem] * (len(operands) - SMEM_INPUTS - 1) + [pl.BlockSpec(memory_space=pl.ANY)]
+    far = len(TWIDDLES) + 1
+    specs = [smem] * SMEM_INPUTS + [vmem] * (len(operands) - SMEM_INPUTS - far)
+    specs += [pl.BlockSpec(memory_space=pl.ANY)] * far
 
     def held(*shape, dtype=jnp.float32):
         return pltpu.VMEM(shape, dtype)
@@ -904,9 +944,10 @@
     sends = 2 * slabs - 1
     planes = sum(plane_rows(slabs, subs))
     scratch = dict(
-        mom=held(ITERS, 2 * slabs, 8, atoms),
+        mom=held(ITERS, 2 * slabs, 4, atoms),
         still=held(2 * slabs, 8, atoms),
-        own=held(8, atoms),
+        own=held(4, atoms),
+        body=held(8, atoms),
         own_tiles=held(cells, 8, LANES),
         tables=held(ITERS, cells + 4 * ghosts, 8, LANES),
         ghosts=held(ITERS, 4, ghosts, 8, LANES),
@@ -934,8 +975,13 @@
         here=held(grid_y, columns, G),
         lhs_t=held16(slabs, columns, plane_rows(slabs, subs)[0]),
         lhs_l=held16(slabs, columns, plane_rows(slabs, subs)[0]),
-        share=held(2 * slabs, 8, atoms),
-        land=held(ITERS, 2 * slabs, 8, atoms),
+        share=held(2 * slabs, 4, atoms),
+        land=held(ITERS, 2 * slabs, 4, atoms),
+        **{
+            "in_" + name: held16(*operand.shape)
+            for name, operand in zip(TWIDDLES, operands[-len(TWIDDLES) :], strict=True)
+        },
+        load=dma((len(TWIDDLES),)),
         mom_send=dma((sends,)),
         mom_recv=dma((ITERS, 2 * slabs)),
         still_send=dma((sends,)),

time: 165 us -> 142 us (0.86)
  Pallas kernels: 158 us -> 141 us
  local copies, waits for them, and re-layouts: 5.71 us -> 1.33 us
    pallas_call x1, Pallas kernels: 158 us -> 141 us  [shards(): pl.pallas_call(functools.partial(whole_kernel, slabs, subs, names), out_s...]
    squeeze x2 -> x0, local copies, waits for them, and re-layouts: 3.11 us -> none  [mine(): lax.dynamic_index_in_dim(p, slab, 0, keepdims=False)]
where the time goes in v4:
time: 142 us
  Pallas kernels  141 us (99%)
    pallas_call x1, Pallas kernels, shards(): pl.pallas_call(functools.partial(whole_kernel, slabs, subs, names), out_s...  141 us

profile of v4, /device:TPU:1, one launch (start us, length us, event | category | flops | bytes accessed | tf_op | source)
XLA Modules:
  0.0 142.3 jit_solution(14822798270827675703)
XLA Ops:
  0.0 141.0 %dipoles.1 = f32[3,1024]{1,0:T(4,128)} custom-call(s32[16,16]{1,0:T(8,128)} %refs_0_.1, s32[16]{0:T(128)} %refs_1_.1, s32[1,4,8]{2,1,0:T(4,128)} %refs_2_.1, f32[1,1024]{1,0:T(1,128)} %bitcast.1, f32[3,1024]{1,0:T(4,128)} %refs_4_.1, f32[3,1024]{1,0:T(4,128)} %refs_5_.1, f32[3,1024]{1,0:T(4,128)} %refs_6_.1, s32[3,1024]{1,0:T(4,128)} %refs_7_.1, ...), custom_call_target="tpu_custom_call" | custom-call | tf_op jit(solution)/shard_map/dipoles/pallas_call | solution.py:1006
  141.0 1.3 copy.25

commit v5 on v4

--- a/solution.py
+++ b/solution.py
@@ -325,9 +325,9 @@
     out_ref,
     field_ref,
     here_ref,
-    lhs_t_ref,
-    lhs_l_ref,
+    lhs_ref,
     wait_part,
+    send_share,
 ):
     grid_y = G // subs
     grid_x = G // slabs
@@ -393,26 +393,38 @@
                 inside = jnp.logical_and(lane >= low_lane, lane < low_lane + window)
                 value = jnp.where(inside, turned[y][:, side : side + LANES], value)
             tiles.append(value)
-        lhs_t_ref[block], lhs_l_ref[block] = split(jnp.concatenate(tiles, axis=1))
-
-    def one(block, _):
-        for part in range(2):
-            zh = zh_ref[part * slabs + block]
-            start, rows = (0, own) if part == 0 else (own, spilt)
-            a = tuple(ref[block, :, :rows] for ref in (lhs_t_ref, lhs_l_ref))
-            b = tuple(ref[block, start : start + rows] for ref in (top_ref, low_ref))
-            mixed = dot3(a, b)
-            fields = []
+        height = tiles[0].shape[0]
+        lhs_ref[block, :height], lhs_ref[block, height:] = split(jnp.concatenate(tiles, axis=1))
+
+    for part in (1, 0):
+        start, rows = (own, spilt) if part else (0, own)
+
+        def one(n, _):
+            block = lax.rem(slab + n, slabs)
+            at = part * slabs + block
+            zh = zh_ref[at]
+            lhs = lhs_ref[block, :, :rows]
+            top, low = (ref[block, start : start + rows] for ref in (top_ref, low_ref))
+            mixed = jnp.dot(lhs, top, preferred_element_type=jnp.float32)
+            mixed = (mixed[:height] + mixed[height:]) + jnp.dot(
+                lhs[:height], low, preferred_element_type=jnp.float32
+            )
             for c in range(3):
                 base = 2 * subs * c
                 value = jnp.sum(mixed[base : base + 2 * subs] * zh[: 2 * subs], axis=0, keepdims=True)
-                at = 6 * subs + c
-                fields.append(value + mixed[at : at + 1] * zh[2 * subs : 2 * subs + 1])
-            for c in range(3):
-                out_ref[part * slabs + block, c : c + 1] = fields[c]
-        return 0
-
-    lax.fori_loop(0, slabs, one, 0)
+                row = 6 * subs + c
+                out_ref[at, c : c + 1] = value + mixed[row : row + 1] * zh[2 * subs : 2 * subs + 1]
+            if part:
+                send_share(part, n)
+            else:
+
+                @pl.when(n < slabs)
+                def _():
+                    send_share(part, n)
+
+            return 0
+
+        lax.fori_loop(1 - part, slabs + 1 - part, one, 0)
 
 
 def kernel_planes(slabs, subs, slab, sub, planes_ref, mids_ref, even_ref, odd_ref, mid_ref):
@@ -471,8 +483,8 @@
         table_ref[2 * t + 1] = jnp.where(first, other, tile)
 
 
-def pair_field(list_ref, count_ref, table_ref, near_ref, pair_ref):
-    cells, entries = list_ref.shape
+def pair_field(first, last, list_ref, count_ref, table_ref, near_ref, pair_ref):
+    entries = list_ref.shape[1]
     width = LANES // 2
     first_half = lanes_of((8, LANES)) < width
     is_moment = rows_of((8, LANES)) < 3
@@ -517,7 +529,7 @@
         )
         return 0
 
-    lax.fori_loop(0, cells, one_cell, 0)
+    lax.fori_loop(first, last, one_cell, 0)
 
 
 def around(slabs, subs):
@@ -574,11 +586,11 @@
 
     def ghost_copies(it):
         goals = [(slab, up), (slab, down), (turns[1], sub), (turns[-1], sub)]
-        cells, ghosts = r.cells.shape[0], r.ghosts.shape[2]
+        ghosts = r.ghosts.shape[2]
         return [
             remote(
                 r.ghosts.at[it, q],
-                r.tables.at[it, pl.ds(cells + q * ghosts, ghosts)],
+                r.landing.at[it, pl.ds(q * ghosts, ghosts)],
                 r.ghost_send.at[q],
                 r.ghost_recv.at[it, q],
                 goal,
@@ -588,7 +600,7 @@
 
     def send_cells(it):
         own_cells(r.body, r.own_tiles)
-        r.tables[it, : r.cells.shape[0]] = r.own_tiles[...]
+        r.tables[: r.cells.shape[0]] = r.own_tiles[...]
         ghosts = r.ghosts.shape[2]
         for q in range(4):
             for slot in range(ghosts):
@@ -768,12 +780,18 @@
 
         cells, ghosts = r.cells.shape[0], r.ghosts.shape[2]
         for q in range(4):
-            landed(r.tables.at[it, pl.ds(cells + q * ghosts, ghosts)], r.ghost_recv.at[it, q])
-        pair_field(r.cells, r.counts, r.tables.at[it], r.near, r.pair)
-        for t in range(atoms // LANES):
-            tile = r.pair[t * LANES : (t + 1) * LANES, :].T[:8]
-            r.rest[:, t * LANES : (t + 1) * LANES] = tile
-        r.rest[0:3] += r.perm[...]
+            landed(r.landing.at[it, pl.ds(q * ghosts, ghosts)], r.ghost_recv.at[it, q])
+        r.tables[cells:] = r.landing[it]
+        cuts = [0, 3 * cells // 8, 5 * cells // 8, cells]
+
+        def pairs(step):
+            pair_field(cuts[step], cuts[step + 1], r.cells, r.counts, r.tables, r.near, r.pair)
+
+        def sent_back(part):
+            exchange(r.send_b, got_b, part, r.b_send, r.b_recv.at[it])
+            pairs(1 + part)
+
+        pairs(0)
 
         second(
             got_a,
@@ -786,8 +804,24 @@
             r.in_by_l,
             r.send_b,
             lambda part: exchanged(got_a, part, r.a_recv.at[it]),
-            lambda part: exchange(r.send_b, got_b, part, r.b_send, r.b_recv.at[it]),
+            sent_back,
         )
+        for t in range(atoms // LANES):
+            tile = r.pair[t * LANES : (t + 1) * LANES, :].T[:8]
+            r.rest[:, t * LANES : (t + 1) * LANES] = tile
+        r.rest[0:3] += r.perm[...]
+
+        def share_copy(part, n):
+            to_slab = lax.rem(slab + n, slabs)
+            slot = part * slabs + slab
+            return remote(
+                r.share.at[part * slabs + to_slab],
+                r.land.at[it, slot],
+                r.share_send.at[part * (slabs - 1) + n - 1 + part],
+                r.share_recv.at[it, slot],
+                (to_slab, down if part else sub),
+            )
+
         sample(
             slabs,
             subs,
@@ -804,23 +838,10 @@
             r.share,
             r.field,
             r.here,
-            r.lhs_t,
-            r.lhs_l,
+            r.lhs,
             lambda part: exchanged(got_b, part, r.b_recv.at[it]),
+            lambda part, n: share_copy(part, n).start(),
         )
-        goals = [(t, sub, t, slab) for t in turns[1:]] + [(t, down, slabs + t, slabs + slab) for t in turns]
-        shares = [
-            remote(
-                r.share.at[source],
-                r.land.at[it, slot],
-                r.share_send.at[n],
-                r.share_recv.at[it, slot],
-                (to_slab, to_sub),
-            )
-            for n, (to_slab, to_sub, source, slot) in enumerate(goals)
-        ]
-        for copy in shares:
-            copy.start()
         total = r.rest[0:3] + r.share[slab, 0:3]
         for slot in [*turns[1:], *(slabs + k for k in range(slabs))]:
             landed(r.land.at[it, slot], r.share_recv.at[it, slot])
@@ -835,8 +856,10 @@
         def _():
             send_moments(it + 1)
 
-        for copy in shares:
-            copy.wait_send()
+        for n in range(1, slabs):
+            share_copy(0, n).wait_send()
+        for n in range(slabs):
+            share_copy(1, n).wait_send()
         for part in range(2):
             rows_sent = pl.ds(*part_rows(part, r.send_a.shape[1] // TILES))
             landed(r.send_a.at[pl.ds(0, subs - 1), rows_sent], r.a_send.at[part])
@@ -949,7 +972,8 @@
         own=held(4, atoms),
         body=held(8, atoms),
         own_tiles=held(cells, 8, LANES),
-        tables=held(ITERS, cells + 4 * ghosts, 8, LANES),
+        tables=held(cells + 4 * ghosts, 8, LANES),
+        landing=held(ITERS, 4 * ghosts, 8, LANES),
         ghosts=held(ITERS, 4, ghosts, 8, LANES),
         near=held(atoms, LANES),
         pair=held(atoms, LANES),
@@ -973,8 +997,7 @@
         got_b=held(ITERS, *chunk),
         field=held(6 * G * G // LANES, LANES),
         here=held(grid_y, columns, G),
-        lhs_t=held16(slabs, columns, plane_rows(slabs, subs)[0]),
-        lhs_l=held16(slabs, columns, plane_rows(slabs, subs)[0]),
+        lhs=held16(slabs, 2 * columns, plane_rows(slabs, subs)[0]),
         share=held(2 * slabs, 4, atoms),
         land=held(ITERS, 2 * slabs, 4, atoms),
         **{

time: 142 us -> 138 us (0.972)
  Pallas kernels: 141 us -> 137 us
    pallas_call x1, Pallas kernels: 141 us -> 137 us  [shards(): pl.pallas_call(functools.partial(whole_kernel, slabs, subs, names), out_s...]
where the time goes in v5:
time: 138 us
  Pallas kernels  137 us (99%)
    pallas_call x1, Pallas kernels, shards(): pl.pallas_call(functools.partial(whole_kernel, slabs, subs, names), out_s...  137 us

profile of v5, /device:TPU:1, one launch (start us, length us, event | category | flops | bytes accessed | tf_op | source)
XLA Modules:
  0.0 138.2 jit_solution(2111727811304716293)
XLA Ops:
  0.0 136.9 %dipoles.1 = f32[3,1024]{1,0:T(4,128)} custom-call(s32[16,16]{1,0:T(8,128)} %refs_0_.1, s32[16]{0:T(128)} %refs_1_.1, s32[1,4,8]{2,1,0:T(4,128)} %refs_2_.1, f32[1,1024]{1,0:T(1,128)} %bitcast.1, f32[3,1024]{1,0:T(4,128)} %refs_4_.1, f32[3,1024]{1,0:T(4,128)} %refs_5_.1, f32[3,1024]{1,0:T(4,128)} %refs_6_.1, s32[3,1024]{1,0:T(4,128)} %refs_7_.1, ...), custom_call_target="tpu_custom_call" | custom-call | tf_op jit(solution)/shard_map/dipoles/pallas_call | solution.py:1029
  136.9 1.3 copy.25

commit v6 on v5

--- a/solution.py
+++ b/solution.py
@@ -16,7 +16,7 @@
 recip_scale = 16.0
 highest = lax.Precision.HIGHEST
 LANES = 128
-TILES = 4 * G // LANES + 1
+TILES = 4 * G // LANES
 MESH = pl.DeviceIdType.MESH
 
 
@@ -175,7 +175,7 @@
     return row[:, part * LANES : (part + 1) * LANES]
 
 
-def first_frequency(slabs, subs, slab, grid_ref, wt_ref, wl_ref, sel_ref, out_ref, mid_ref, send_part):
+def first_frequency(slabs, subs, slab, grid_ref, wt_ref, wl_ref, sel_ref, out_ref, few_ref, edge_ref, mid_ref, send_part):
     grid_y = G // subs
     half = G // 2
     flat_ref = out_ref.reshape(subs * TILES * grid_y, LANES)
@@ -205,8 +205,8 @@
                 half_of(odd, part) * half_of(sx, n) + kz * half_of(sz, n) for n in range(2)
             ] + [half_of(sy, 0), half_of(sy, 1)]
             if part == 1:
-                tiles.append(
-                    -float(half) * jnp.where(lane == 0, sx[:, :1], jnp.where(lane == 1, sx[:, LANES : LANES + 1], 0.0))
+                edge_ref[pl.ds(y, subs, stride=grid_y), :] = -float(half) * jnp.where(
+                    lane == 0, sx[:, :1], jnp.where(lane == 1, sx[:, LANES : LANES + 1], 0.0)
                 )
             for t, value in enumerate(tiles):
                 flat_ref[pl.ds((part * 4 + t) * grid_y + y, subs, stride=TILES * grid_y), :] = value
@@ -231,12 +231,28 @@
     more = jnp.dot(top, sel, preferred_element_type=jnp.float32) + jnp.dot(
         low, sel, preferred_element_type=jnp.float32
     )
-    out_ref[:, (TILES - 1) * grid_y :, :] += more.reshape(subs, grid_y, LANES)
+    pack_columns(edge_ref[...] + more, few_ref)
     send_part(1)
 
 
 def part_rows(part, high):
-    return (0, 4 * high) if part == 0 else (4 * high, (TILES - 4) * high)
+    return part * 4 * high, 4 * high
+
+
+def pack_columns(value, ref):
+    spread = pltpu.roll(value, 0, 1, stride=LANES // 8, stride_axis=0)
+    rows = jnp.sum(spread.reshape(ref.shape[0], 8, LANES), axis=1)
+    for block in range(ref.shape[0]):
+        ref[block] = rows[block : block + 1]
+
+
+def unpack_columns(ref):
+    rows = jnp.concatenate([jnp.broadcast_to(ref[block], (8, LANES)) for block in range(ref.shape[0])], axis=0)
+    y = rows_of(rows.shape) & 7
+    back = rows
+    for n in range(1, 8):
+        back = jnp.where(y == n, pltpu.roll(rows, LANES - n * (LANES // 8), 1), back)
+    return jnp.where(lanes_of(back.shape) < LANES // 8, back, 0.0)
 
 
 def from_tiles(ref, part):
@@ -278,12 +294,15 @@
     return tuple(both)
 
 
-def second(got_ref, even_ref, odd_ref, mid_ref, ft_ref, fl_ref, bt_ref, bl_ref, out_ref, wait_part, send_part):
+def second(got_ref, few_ref, even_ref, odd_ref, mid_ref, ft_ref, fl_ref, bt_ref, bl_ref, out_ref, few_out_ref, wait_part, send_part):
     forward, backward = (ft_ref[...], fl_ref[...]), (bt_ref[...], bl_ref[...])
     odd_y, even_y, full_y = (frequency_columns(k) for k in ("odd", "even", "signed"))
     for part in range(2):
         wait_part(part)
-        spec = dot3(forward, with_swapped(from_tiles(got_ref, part)))
+        got = from_tiles(got_ref, part)
+        if part == 1:
+            got = jnp.concatenate([got, unpack_columns(few_ref)], axis=1)
+        spec = dot3(forward, with_swapped(got))
         lanes = slice(part * LANES, (part + 1) * LANES)
         kernel_even, kernel_odd = even_ref[:, lanes], odd_ref[:, lanes]
         lane = lanes_of(kernel_even.shape)
@@ -305,7 +324,10 @@
             mid = mid_ref[...] * (last + full_y * pltpu.roll(last, LANES - 4, 1))
             mid = mid + full_y * pltpu.roll(mid, 4, 1)
             tiles.append(jnp.where(lane == 0, columns[0], jnp.where(lane == 1, columns[1], mid)))
-        to_tiles(dot3(backward, with_swapped(jnp.concatenate(tiles, axis=1))), out_ref, part)
+        back = dot3(backward, with_swapped(jnp.concatenate(tiles, axis=1)))
+        to_tiles(back, out_ref, part)
+        if part == 1:
+            pack_columns(back[:, 4 * LANES :], few_out_ref)
         send_part(part)
 
 
@@ -314,6 +336,7 @@
     subs,
     slab,
     got_ref,
+    few_ref,
     top_ref,
     low_ref,
     zh_ref,
@@ -339,10 +362,10 @@
     for part in range(2):
         wait_part(part)
         got = from_tiles(got_ref, part)
-        last = got[:, 4 * LANES :]
         phi = got[:, : 2 * LANES]
         along_x = [half_of(odd, part) * half_of(phi, n) for n in range(2)]
         if part == 1:
+            last = unpack_columns(few_ref)
             along_x = [v + half_of(even, part) * last[:, n : n + 1] for n, v in enumerate(along_x)]
         lhs = jnp.concatenate([jnp.concatenate(along_x, axis=1), got[:, 2 * LANES : 4 * LANES], kz * phi], axis=0)
         rows = slice(part * 2 * LANES, (part + 1) * 2 * LANES)
@@ -615,7 +638,10 @@
         r.body[0:3] = r.own[0:3]
         send_cells(it)
 
-    moves = [pltpu.make_async_copy(r.influence.at[:, i, :], r.moved.at[i], r.move.at[i]) for i in range(depth)]
+    moves = [
+        pltpu.make_async_copy(r.influence.at[:, :, pl.ds(h * LANES, LANES)], r.raw.at[h], r.move.at[h])
+        for h in range(G // LANES)
+    ]
     loads = [
         pltpu.make_async_copy(getattr(r, name), getattr(r, "in_" + name), r.load.at[n])
         for n, name in enumerate(TWIDDLES)
@@ -652,8 +678,12 @@
             r.moved.at[i], r.planes.at[slot, pl.ds(slab * rows, rows)], r.plane_recv.at[slot, slab]
         )
 
+    for move in moves:
+        move.wait()
+    raw = r.raw.reshape(G // LANES * rows * depth, LANES)
     for i in range(depth):
-        moves[i].wait()
+        for h in range(G // LANES):
+            r.moved[i, :, h * LANES : (h + 1) * LANES] = raw[pl.ds(h * rows * depth + i, rows, stride=depth), :]
         far, slot, mine = plane(i)
 
         @pl.when(mine)
@@ -723,23 +753,29 @@
     for load in loads:
         load.wait()
 
-    def exchange(send, got, part, send_sem, recv_sem):
+    def exchange(send, few, got, got_few, part, send_sem, recv_sem):
         first, count = part_rows(part, send.shape[1] // TILES)
         rows = pl.ds(first, count)
-        pltpu.make_async_copy(send.at[sub, rows], got.at[sub, rows], recv_sem.at[part]).start()
-
-        def one(n, _):
-            to_sub = lax.rem(sub + n, subs)
-            remote(
-                send.at[to_sub, rows], got.at[sub, rows], send_sem.at[part], recv_sem.at[part], (slab, to_sub)
-            ).start()
-            return 0
-
-        lax.fori_loop(1, subs, one, 0)
-
-    def exchanged(got, part, recv_sem):
+
+        def all_to_all(sources, targets, n):
+            pltpu.make_async_copy(sources(sub), targets, recv_sem.at[n]).start()
+
+            def one(k, _):
+                to_sub = lax.rem(sub + k, subs)
+                remote(sources(to_sub), targets, send_sem.at[n], recv_sem.at[n], (slab, to_sub)).start()
+                return 0
+
+            lax.fori_loop(1, subs, one, 0)
+
+        if part == 1:
+            all_to_all(lambda to: few.at[to], got_few.at[sub], 2)
+        all_to_all(lambda to: send.at[to, rows], got.at[sub, rows], part)
+
+    def exchanged(got, got_few, part, recv_sem):
         first, count = part_rows(part, got.shape[1] // TILES)
         landed(got.at[:, pl.ds(first, count)], recv_sem.at[part])
+        if part == 1:
+            landed(got_few, recv_sem.at[2])
 
     def iteration(it, _):
         density(
@@ -754,6 +790,7 @@
             lambda slot: landed(r.mom.at[it, slot], r.mom_recv.at[it, slot]),
         )
         got_a, got_b = r.got_a.at[it], r.got_b.at[it]
+        few_a, few_b = r.got_few_a.at[it], r.got_few_b.at[it]
         first_frequency(
             slabs,
             subs,
@@ -763,8 +800,10 @@
             r.in_tx_l,
             r.gather,
             r.send_a,
+            r.few_a,
+            r.edge,
             r.mid_rows,
-            lambda part: exchange(r.send_a, got_a, part, r.a_send, r.a_recv.at[it]),
+            lambda part: exchange(r.send_a, r.few_a, got_a, few_a, part, r.a_send, r.a_recv.at[it]),
         )
 
         @pl.when(it == 0)
@@ -788,13 +827,14 @@
             pair_field(cuts[step], cuts[step + 1], r.cells, r.counts, r.tables, r.near, r.pair)
 
         def sent_back(part):
-            exchange(r.send_b, got_b, part, r.b_send, r.b_recv.at[it])
+            exchange(r.send_b, r.few_b, got_b, few_b, part, r.b_send, r.b_recv.at[it])
             pairs(1 + part)
 
         pairs(0)
 
         second(
             got_a,
+            few_a,
             r.even,
             r.odd,
             r.mid_tile,
@@ -803,7 +843,8 @@
             r.in_by_t,
             r.in_by_l,
             r.send_b,
-            lambda part: exchanged(got_a, part, r.a_recv.at[it]),
+            r.few_b,
+            lambda part: exchanged(got_a, few_a, part, r.a_recv.at[it]),
             sent_back,
         )
         for t in range(atoms // LANES):
@@ -827,6 +868,7 @@
             subs,
             slab,
             got_b,
+            few_b,
             r.plane_t,
             r.plane_l,
             r.zhat,
@@ -839,7 +881,7 @@
             r.field,
             r.here,
             r.lhs,
-            lambda part: exchanged(got_b, part, r.b_recv.at[it]),
+            lambda part: exchanged(got_b, few_b, part, r.b_recv.at[it]),
             lambda part, n: share_copy(part, n).start(),
         )
         total = r.rest[0:3] + r.share[slab, 0:3]
@@ -864,6 +906,8 @@
             rows_sent = pl.ds(*part_rows(part, r.send_a.shape[1] // TILES))
             landed(r.send_a.at[pl.ds(0, subs - 1), rows_sent], r.a_send.at[part])
             landed(r.send_b.at[pl.ds(0, subs - 1), rows_sent], r.b_send.at[part])
+        landed(r.few_a.at[pl.ds(0, subs - 1)], r.a_send.at[2])
+        landed(r.few_b.at[pl.ds(0, subs - 1)], r.b_send.at[2])
         return 0
 
     lax.fori_loop(0, ITERS, iteration, 0)
@@ -981,6 +1025,7 @@
         plane_t=held16(slabs, planes, atoms),
         plane_l=held16(slabs, planes, atoms),
         zhat=held(2 * slabs, ranks, atoms),
+        raw=held(G // LANES, grid_x, depth, LANES),
         moved=held(depth, grid_x, G),
         turned=held(G, LANES),
         hop=held(slabs, grid_x, LANES),
@@ -993,6 +1038,11 @@
         mid_rows=held(4, grid_y, G),
         send_a=held(*chunk),
         got_a=held(ITERS, *chunk),
+        few_a=held(subs, 1, LANES),
+        got_few_a=held(ITERS, subs, 1, LANES),
+        few_b=held(subs, 1, LANES),
+        got_few_b=held(ITERS, subs, 1, LANES),
+        edge=held(G, LANES),
         send_b=held(*chunk),
         got_b=held(ITERS, *chunk),
         field=held(6 * G * G // LANES, LANES),
@@ -1011,17 +1061,17 @@
         still_recv=dma((2 * slabs,)),
         ghost_send=dma((4,)),
         ghost_recv=dma((ITERS, 4)),
-        move=dma((depth,)),
+        move=dma((G // LANES,)),
         plane_send=dma((depth,)),
         plane_recv=dma((2, slabs)),
         hop_send=dma((slabs - 1,)),
         hop_recv=dma((slabs,)),
         mid_send=dma((subs - 1,)),
         mid_recv=dma,
-        a_send=dma((2,)),
-        a_recv=dma((ITERS, 2)),
-        b_send=dma((2,)),
-        b_recv=dma((ITERS, 2)),
+        a_send=dma((3,)),
+        a_recv=dma((ITERS, 3)),
+        b_send=dma((3,)),
+        b_recv=dma((ITERS, 3)),
         share_send=dma((sends,)),
         share_recv=dma((ITERS, 2 * slabs)),
     )

time: 138 us -> 135 us (0.978)
  Pallas kernels: 137 us -> 134 us
    pallas_call x1, Pallas kernels: 137 us -> 134 us  [shards(): pl.pallas_call(functools.partial(whole_kernel, slabs, subs, names), out_s...]
where the time goes in v6:
time: 135 us
  Pallas kernels  134 us (99%)
    pallas_call x1, Pallas kernels, shards(): pl.pallas_call(functools.partial(whole_kernel, slabs, subs, names), out_s...  134 us

profile of v6, /device:TPU:1, one launch (start us, length us, event | category | flops | bytes accessed | tf_op | source)
XLA Modules:
  0.0 134.9 jit_solution(1737375192572819798)
XLA Ops:
  0.0 133.6 %dipoles.1 = f32[3,1024]{1,0:T(4,128)} custom-call(s32[16,16]{1,0:T(8,128)} %refs_0_.1, s32[16]{0:T(128)} %refs_1_.1, s32[1,4,8]{2,1,0:T(4,128)} %refs_2_.1, f32[1,1024]{1,0:T(1,128)} %bitcast.1, f32[3,1024]{1,0:T(4,128)} %refs_4_.1, f32[3,1024]{1,0:T(4,128)} %refs_5_.1, f32[3,1024]{1,0:T(4,128)} %refs_6_.1, s32[3,1024]{1,0:T(4,128)} %refs_7_.1, ...), custom_call_target="tpu_custom_call" | custom-call | tf_op jit(solution)/shard_map/dipoles/pallas_call | solution.py:1079
  133.6 1.3 copy.25

commit v7 on v6

--- a/solution.py
+++ b/solution.py
@@ -600,6 +600,54 @@
     middle = subs // 2
     group = 2 * subs
 
+    barrier = pltpu.get_barrier_semaphore()
+
+    def greet(to_slab, to_sub):
+        pl.semaphore_signal(barrier, inc=1, device_id=(to_slab, to_sub), device_id_type=MESH)
+
+    def folded_of(kz):
+        upper = kz >= half
+        folded = jnp.where(upper, lax.rem(2 * half - kz, half), kz)
+        return folded, jnp.where(upper, 1, 0)
+
+    for t in turns[1:]:
+        greet(t, sub)
+    for t in turns:
+        greet(t, up)
+        greet(t, down)
+
+    def greet_sub(k, _):
+        greet(slab, lax.rem(sub + k, subs))
+        return 0
+
+    lax.fori_loop(2, subs - 1, greet_sub, 0)
+    here_kz = slabs * sub + slab
+    expected = 3 * slabs - 1 + subs - 3
+    for kz in (here_kz, jnp.where(here_kz == 0, half, 2 * half - here_kz)):
+        from_sub = lax.div(kz, depth)
+        for t in range(slabs):
+            other = jnp.logical_or(from_sub != sub, slab != t)
+
+            @pl.when(other)
+            def _():
+                greet(t, from_sub)
+
+    for i in range(depth):
+        folded, _ = folded_of(depth * sub + i)
+        mine = jnp.logical_and(lax.rem(folded, slabs) == slab, lax.div(folded, slabs) == sub)
+        expected = expected + jnp.where(mine, 0, 1)
+    moves = [
+        pltpu.make_async_copy(r.influence.at[:, :, pl.ds(h * LANES, LANES)], r.raw.at[h], r.move.at[h])
+        for h in range(G // LANES)
+    ]
+    loads = [
+        pltpu.make_async_copy(getattr(r, name), getattr(r, "in_" + name), r.load.at[n])
+        for n, name in enumerate(TWIDDLES)
+    ]
+    for move in [*moves, *loads]:
+        move.start()
+    pl.semaphore_wait(barrier, expected)
+
     def to_group(source, target, send_sem, recv_sem):
         goals = [(t, sub, slab) for t in turns[1:]] + [(t, up, slabs + slab) for t in turns]
         return [
@@ -638,16 +686,6 @@
         r.body[0:3] = r.own[0:3]
         send_cells(it)
 
-    moves = [
-        pltpu.make_async_copy(r.influence.at[:, :, pl.ds(h * LANES, LANES)], r.raw.at[h], r.move.at[h])
-        for h in range(G // LANES)
-    ]
-    loads = [
-        pltpu.make_async_copy(getattr(r, name), getattr(r, "in_" + name), r.load.at[n])
-        for n, name in enumerate(TWIDDLES)
-    ]
-    for move in [*moves, *loads]:
-        move.start()
     atoms = r.own.shape[1]
     r.own[0:3] = r.pol[...] * r.perm[...]
     r.own[3:4] = jnp.zeros((1, atoms), jnp.float32)
@@ -662,10 +700,7 @@
     send_moments(0)
 
     def plane(i):
-        kz = depth * sub + i
-        upper = kz >= half
-        folded = jnp.where(upper, lax.rem(2 * half - kz, half), kz)
-        slot = jnp.where(upper, 1, 0)
+        folded, slot = folded_of(depth * sub + i)
         to_slab, to_sub = lax.rem(folded, slabs), lax.div(folded, slabs)
         target = r.planes.at[slot, pl.ds(slab * rows, rows)]
         far = remote(
@@ -1082,7 +1117,7 @@
         in_specs=specs,
         out_specs=vmem,
         scratch_shapes=list(scratch.values()),
-        compiler_params=pltpu.CompilerParams(vmem_limit_bytes=60 << 20, has_side_effects=True),
+        compiler_params=pltpu.CompilerParams(vmem_limit_bytes=60 << 20, collective_id=0, has_side_effects=True),
         name="dipoles",
     )(*operands)
 

time: 135 us -> 132 us (0.978)
  Pallas kernels: 134 us -> 130 us
    pallas_call x1, Pallas kernels: 134 us -> 130 us  [shards(): pl.pallas_call(functools.partial(whole_kernel, slabs, subs, names), out_s...]
where the time goes in v7:
time: 132 us; the launch traced here: 131 us
  Pallas kernels  130 us (98%)
  local copies, waits for them, and re-layouts  1.33 us (1%)
    pallas_call x1, Pallas kernels, shards(): pl.pallas_call(functools.partial(whole_kernel, slabs, subs, names), out_s...  130 us

profile of v7, /device:TPU:1, one launch (start us, length us, event | category | flops | bytes accessed | tf_op | source)
XLA Modules:
  0.0 131.3 jit_solution(615233361281698758)
XLA Ops:
  0.0 130.0 %dipoles.1 = f32[3,1024]{1,0:T(4,128)} custom-call(s32[16,16]{1,0:T(8,128)} %refs_0_.1, s32[16]{0:T(128)} %refs_1_.1, s32[1,4,8]{2,1,0:T(4,128)} %refs_2_.1, f32[1,1024]{1,0:T(1,128)} %bitcast.1, f32[3,1024]{1,0:T(4,128)} %refs_4_.1, f32[3,1024]{1,0:T(4,128)} %refs_5_.1, f32[3,1024]{1,0:T(4,128)} %refs_6_.1, s32[3,1024]{1,0:T(4,128)} %refs_7_.1, ...), custom_call_target="tpu_custom_call" | custom-call | tf_op jit(solution)/shard_map/dipoles/pallas_call | solution.py:1114
  130.0 1.3 %copy.25 = f32[3,1024]{1,0:T(4,128)} copy(f32[3,1024]{1,0:T(4,128)} %dipoles.1) | data formatting | bytes 24576

commit v8 on v7

--- a/solution.py
+++ b/solution.py
@@ -646,7 +646,6 @@
     ]
     for move in [*moves, *loads]:
         move.start()
-    pl.semaphore_wait(barrier, expected)
 
     def to_group(source, target, send_sem, recv_sem):
         goals = [(t, sub, slab) for t in turns[1:]] + [(t, up, slabs + slab) for t in turns]
@@ -669,13 +668,16 @@
             for q, goal in enumerate(goals)
         ]
 
-    def send_cells(it):
+    def build_cells(it):
+        r.body[0:3] = r.own[0:3]
         own_cells(r.body, r.own_tiles)
         r.tables[: r.cells.shape[0]] = r.own_tiles[...]
         ghosts = r.ghosts.shape[2]
         for q in range(4):
             for slot in range(ghosts):
                 r.ghosts[it, q, slot] = r.own_tiles[r.sends[0, q, slot]]
+
+    def send_ghosts(it):
         for copy in ghost_copies(it):
             copy.start()
 
@@ -683,8 +685,6 @@
         for copy in to_group(r.own, r.mom.at[it], r.mom_send, r.mom_recv.at[it]):
             copy.start()
         r.mom[it, slab] = r.own[...]
-        r.body[0:3] = r.own[0:3]
-        send_cells(it)
 
     atoms = r.own.shape[1]
     r.own[0:3] = r.pol[...] * r.perm[...]
@@ -694,10 +694,6 @@
     r.still[slab, 0:3] = r.frac[...]
     r.still[slab, 3:6] = r.base[...].astype(jnp.float32)
     r.still[slab, 6:8] = jnp.zeros((2, atoms), jnp.float32)
-    still_copies = to_group(r.still.at[slab], r.still, r.still_send, r.still_recv)
-    for copy in still_copies:
-        copy.start()
-    send_moments(0)
 
     def plane(i):
         folded, slot = folded_of(depth * sub + i)
@@ -713,12 +709,30 @@
             r.moved.at[i], r.planes.at[slot, pl.ds(slab * rows, rows)], r.plane_recv.at[slot, slab]
         )
 
+    build_cells(0)
+    near_columns(r.body[...], r.near)
+    phase = (r.phase_t[slab], r.phase_l[slab])
+
+    def own_table(at):
+        tables_of(slabs, subs, r.still, at, False, phase, r.plane_t, r.plane_l, r.zhat)
+
+    own_table(slab)
     for move in moves:
         move.wait()
     raw = r.raw.reshape(G // LANES * rows * depth, LANES)
     for i in range(depth):
         for h in range(G // LANES):
             r.moved[i, :, h * LANES : (h + 1) * LANES] = raw[pl.ds(h * rows * depth + i, rows, stride=depth), :]
+    first = r.moved[0]
+    r.turned[...] = jnp.concatenate([first] * (LANES // rows), axis=0).T
+
+    pl.semaphore_wait(barrier, expected)
+    still_copies = to_group(r.still.at[slab], r.still, r.still_send, r.still_recv)
+    for copy in still_copies:
+        copy.start()
+    send_moments(0)
+    send_ghosts(0)
+    for i in range(depth):
         far, slot, mine = plane(i)
 
         @pl.when(mine)
@@ -728,9 +742,6 @@
         @pl.when(jnp.logical_not(mine))
         def _():
             far.start()
-
-    first = r.moved[0]
-    r.turned[...] = jnp.concatenate([first] * (LANES // rows), axis=0).T
 
     def hop(n):
         return remote(
@@ -757,22 +768,16 @@
             hop(n).start()
         r.hop[slab] = r.turned[pl.ds(pl.multiple_of(slab * group, group), group)]
 
-    near_columns(r.body[...], r.near)
-    phase = (r.phase_t[slab], r.phase_l[slab])
-
     def tables(before):
         def one(n, _):
             block = lax.rem(slab + n, slabs)
             at = block + slabs if before else block
 
-            @pl.when(jnp.logical_or(before, n > 0))
-            def _():
-                landed(r.still.at[at], r.still_recv.at[at])
-
+            landed(r.still.at[at], r.still_recv.at[at])
             tables_of(slabs, subs, r.still, block, before, phase, r.plane_t, r.plane_l, r.zhat)
             return 0
 
-        lax.fori_loop(0, slabs, one, 0)
+        lax.fori_loop(0 if before else 1, slabs, one, 0)
 
     tables(False)
 
@@ -932,6 +937,8 @@
         @pl.when(it + 1 < ITERS)
         def _():
             send_moments(it + 1)
+            build_cells(it + 1)
+            send_ghosts(it + 1)
 
         for n in range(1, slabs):
             share_copy(0, n).wait_send()

time: 132 us -> 131 us (level)
  no operation moved by 1% of the time
where the time goes in v8:
time: 131 us
  Pallas kernels  130 us (99%)
  local copies, waits for them, and re-layouts  1.33 us (1%)
    pallas_call x1, Pallas kernels, shards(): pl.pallas_call(functools.partial(whole_kernel, slabs, subs, names), out_s...  130 us

profile of v8, /device:TPU:1, one launch (start us, length us, event | category | flops | bytes accessed | tf_op | source)
XLA Modules:
  0.0 131.1 jit_solution(16138457022811936191)
XLA Ops:
  0.0 129.8 %dipoles.1 = f32[3,1024]{1,0:T(4,128)} custom-call(s32[16,16]{1,0:T(8,128)} %refs_0_.1, s32[16]{0:T(128)} %refs_1_.1, s32[1,4,8]{2,1,0:T(4,128)} %refs_2_.1, f32[1,1024]{1,0:T(1,128)} %bitcast.1, f32[3,1024]{1,0:T(4,128)} %refs_4_.1, f32[3,1024]{1,0:T(4,128)} %refs_5_.1, f32[3,1024]{1,0:T(4,128)} %refs_6_.1, s32[3,1024]{1,0:T(4,128)} %refs_7_.1, ...), custom_call_target="tpu_custom_call" | custom-call | tf_op jit(solution)/shard_map/dipoles/pallas_call | solution.py:1121
  129.8 1.3 %copy.25 = f32[3,1024]{1,0:T(4,128)} copy(f32[3,1024]{1,0:T(4,128)} %dipoles.1) | data formatting | bytes 24576

commit v9 on v7

--- a/solution.py
+++ b/solution.py
@@ -40,10 +40,9 @@
 def dot3(a, b, turned=False):
     dims = (((1,), (1 if turned else 0,)), ((), ()))
 
-    def one(x, y):
-        return lax.dot_general(x, y, dims, preferred_element_type=jnp.float32)
-
-    return one(a[0], b[0]) + (one(a[1], b[0]) + one(a[0], b[1]))
+    left = jnp.concatenate([a[1], a[0], a[0]], axis=1)
+    right = jnp.concatenate([b[0], b[1], b[0]], axis=1 if turned else 0)
+    return lax.dot_general(left, right, dims, preferred_element_type=jnp.float32)
 
 
 def parts_of(table):

time: 132 us -> 131 us (level)
  no operation moved by 1% of the time
where the time goes in v9:
time: 131 us
  Pallas kernels  130 us (99%)
  local copies, waits for them, and re-layouts  1.33 us (1%)
    pallas_call x1, Pallas kernels, shards(): pl.pallas_call(functools.partial(whole_kernel, slabs, subs, names), out_s...  130 us

profile of v9, /device:TPU:1, one launch (start us, length us, event | category | flops | bytes accessed | tf_op | source)
XLA Modules:
  0.0 131.0 jit_solution(1079793062635205679)
XLA Ops:
  0.0 129.7 %dipoles.1 = f32[3,1024]{1,0:T(4,128)} custom-call(s32[16,16]{1,0:T(8,128)} %refs_0_.1, s32[16]{0:T(128)} %refs_1_.1, s32[1,4,8]{2,1,0:T(4,128)} %refs_2_.1, f32[1,1024]{1,0:T(1,128)} %bitcast.1, f32[3,1024]{1,0:T(4,128)} %refs_4_.1, f32[3,1024]{1,0:T(4,128)} %refs_5_.1, f32[3,1024]{1,0:T(4,128)} %refs_6_.1, s32[3,1024]{1,0:T(4,128)} %refs_7_.1, ...), custom_call_target="tpu_custom_call" | custom-call | tf_op jit(solution)/shard_map/dipoles/pallas_call | solution.py:1113
  129.7 1.3 %copy.25 = f32[3,1024]{1,0:T(4,128)} copy(f32[3,1024]{1,0:T(4,128)} %dipoles.1) | data formatting | bytes 24576
